TPU v7x, 128 devices: a whole 4x4x4 slice. The times are simulated.
128 devices in a mesh: grp: 4 (over z), tm: 32 (over y, x, core).
Axes of the slice: x: 4, y: 4, z: 4, core: 2. Of those that a mesh axis runs over, the one named last changes fastest.
Arguments:
- frames: bfloat16 [4, 128, 24, 24, 2048], P('grp', 'tm'), may hold values from -6 to 6
- sample_counts: int32 [4, 128], P('grp', 'tm'), may hold values from 0 to 3, as said below
- dest_groups: int32 [4, 128], P('grp', 'tm'), may hold values from 0 to 3, as said below
- episode_ends: int32 [4, 128], P('grp', 'tm'), may hold values 0 or 1
- valid_steps: int32 [4, 128], P('grp', 'tm'), may hold values 0 or 1
- rewards: float32 [4, 128], P('grp', 'tm'), may hold values from -1.25 to 1.25
- ratios: float32 [4, 128], P('grp', 'tm'), may hold values from 0.5 to 1.04
- stored_values: float32 [4, 128, 128], P('grp', 'tm'), may hold values from -6 to 6
- stem_weight: bfloat16 [2048, 256], replicated, may hold values from -0.125 to 0.125
- conv_first: bfloat16 [2, 9, 256, 256], replicated, may hold values from -0.125 to 0.125
- conv_second: bfloat16 [2, 9, 256, 256], replicated, may hold values from -0.125 to 0.125
- value_weight: bfloat16 [256, 128], replicated, may hold values from -0.375 to 0.375
- discounts: float32 [128], replicated, may hold values from 0.97 to 1
- lambdas: float32 [128], replicated, may hold values from 0.95 to 1
Outputs:
- latents: bfloat16 [4, 128, 24, 24, 256], P('grp', 'tm')
- values: float32 [4, 128, 128], P('grp', 'tm')
- targets: float32 [4, 128, 128], P('grp', 'tm')
- group_load: int32 [4, 32], P('grp', 'tm')
Inputs may be any that keep to these rules, and one draw needn't show every extreme that they name: `sample_counts`: in every time shard, one of the 4 devices holding it has all 4 of its blocks sampled. `dest_groups`: read only for sampled blocks. At most 1 sampled blocks of one device name the same group, and at most 2 sampled blocks of one time shard (over all groups) name the same group; both bounds are reached in every draw.
All inputs are finite; a program needn't handle non-finite values. No bound on the sum of `episode_ends` or of `valid_steps` on one device may be relied on, other than what follows from the above.
Results may differ from a plain program's by a relative error of at most 0.014.
Values may be sent and summed in bfloat16 or wider, within the bound.
No kernel may reach another device: no remote copies, remote signals or barrier semaphores. Data moves between devices by JAX's collectives and lax.ppermute only.
A program may use at most 128 MiB of HBM per device.

v0:
```python
import jax
import jax.numpy as jnp
from jax import lax
from jax.sharding import PartitionSpec as P


def from_behind(block, axis, distance):
    devices = range(lax.axis_size(axis))
    route = [(i - distance, i) for i in devices if i - distance in devices]
    return lax.ppermute(block, axis, route)


def conv_tap(source, weight):
    count_rows, grid_side, _, channels = source.shape
    padded = jnp.pad(source, ((0, 0), (1, 1), (1, 1), (0, 0)))
    accumulated = jnp.zeros((count_rows * grid_side * grid_side, weight.shape[2]), jnp.float32)
    for tap_index in range(9):
        tap_row = tap_index // 3
        tap_col = tap_index % 3
        window = padded[:, tap_row : tap_row + grid_side, tap_col : tap_col + grid_side, :]
        window = window.reshape(count_rows * grid_side * grid_side, channels)
        accumulated = accumulated + jnp.dot(
            window, weight[tap_index], preferred_element_type=jnp.float32
        )
    return accumulated.reshape(count_rows, grid_side, grid_side, weight.shape[2])


def stem_layer(blocks, stem_weight):
    count_rows, grid_side, _, patch_values = blocks.shape
    hidden = jnp.dot(
        blocks.reshape(-1, patch_values), stem_weight, preferred_element_type=jnp.float32
    )
    hidden = jax.nn.relu(hidden).astype(jnp.bfloat16)
    return hidden.reshape(count_rows, grid_side, grid_side, stem_weight.shape[1])


def residual_tower(hidden, conv_first, conv_second):
    for layer_index in range(conv_first.shape[0]):
        widened = hidden.astype(jnp.float32)
        normed = widened * lax.rsqrt(jnp.mean(widened * widened, axis=-1, keepdims=True) + 1e-05)
        activated = jax.nn.relu(normed).astype(jnp.bfloat16)
        middle = jax.nn.relu(conv_tap(activated, conv_first[layer_index])).astype(jnp.bfloat16)
        hidden = (widened + conv_tap(middle, conv_second[layer_index])).astype(jnp.bfloat16)
    return hidden


def per_device(
    frames,
    sample_counts,
    dest_groups,
    episode_ends,
    valid_steps,
    rewards,
    ratios,
    stored_values,
    stem_weight,
    conv_first,
    conv_second,
    value_weight,
    discounts,
    lambdas,
):
    groups_here = lax.axis_size("grp")
    shards = lax.axis_size("tm")
    blocks = frames[0]
    steps_here = blocks.shape[0]
    grid_side = blocks.shape[1]
    channels = stem_weight.shape[1]
    per_pair = steps_here // groups_here
    received = steps_here // 2
    slot_count = groups_here * per_pair
    counts = sample_counts[0]
    sampled = counts > 0
    group_ids = jnp.arange(groups_here, dtype=jnp.int32)
    matches = (dest_groups[0][:, None] == group_ids[None, :]) & sampled[:, None]
    as_int = matches.astype(jnp.int32)
    earlier_hits = jnp.cumsum(as_int, axis=0) - as_int
    slot_of_block = dest_groups[0] * per_pair + jnp.sum(earlier_hits * as_int, axis=1)
    slot_ids = jnp.arange(slot_count, dtype=jnp.int32)
    assign = sampled[:, None] & (slot_of_block[:, None] == slot_ids[None, :])
    assign_int = assign.astype(jnp.int32)
    block_of_slot = jnp.sum(assign_int * jnp.arange(steps_here, dtype=jnp.int32)[:, None], axis=0)
    slot_live = jnp.any(assign, axis=0)
    chosen = jnp.take(blocks, block_of_slot, axis=0)
    outgoing = stem_layer(chosen, stem_weight)
    outgoing = jnp.where(slot_live[:, None, None, None], outgoing, jnp.zeros_like(outgoing))
    slot_weight = jnp.sum(assign_int * counts[:, None], axis=0).astype(jnp.bfloat16)
    arrived, arrived_counts = (
        lax.all_to_all(
            outgoing.reshape(groups_here, per_pair, grid_side, grid_side, channels),
            "grp",
            split_axis=0,
            concat_axis=0,
            tiled=True,
        ),
        lax.all_to_all(
            slot_weight.reshape(groups_here, per_pair),
            "grp",
            split_axis=0,
            concat_axis=0,
            tiled=True,
        ),
    )
    arrived = arrived.reshape(slot_count, grid_side, grid_side, channels)
    arrived_counts = arrived_counts.reshape(slot_count).astype(jnp.float32)
    arrived_live = arrived_counts > 0
    load_here = jnp.sum(arrived_counts).astype(jnp.int32)
    live_int = arrived_live.astype(jnp.int32)
    position = jnp.cumsum(live_int) - 1
    compact_ids = jnp.arange(received, dtype=jnp.int32)
    gather_index = jnp.sum(
        jnp.where(
            arrived_live[None, :] & (position[None, :] == compact_ids[:, None]),
            slot_ids[None, :],
            0,
        ),
        axis=1,
    )
    compact = jnp.take(arrived, gather_index, axis=0)
    encoded = residual_tower(compact, conv_first, conv_second)
    returning = jnp.take(encoded, jnp.clip(position, 0, received - 1), axis=0)
    returning = jnp.where(arrived_live[:, None, None, None], returning, jnp.zeros_like(returning))
    home_slots = lax.all_to_all(
        returning.reshape(groups_here, per_pair, grid_side, grid_side, channels),
        "grp",
        split_axis=0,
        concat_axis=0,
        tiled=True,
    )
    home_slots = home_slots.reshape(slot_count, grid_side, grid_side, channels)
    latents = jnp.take(home_slots, jnp.clip(slot_of_block, 0, slot_count - 1), axis=0)
    latents = jnp.where(sampled[:, None, None, None], latents, jnp.zeros_like(latents))
    pooled = jnp.mean(latents.astype(jnp.float32), axis=(1, 2))
    fresh_values = jnp.dot(
        pooled, value_weight.astype(jnp.float32), precision=lax.Precision.HIGHEST
    )
    values = jnp.where(sampled[:, None], fresh_values, stored_values[0])
    following = from_behind(values[0:1], "tm", -1)
    next_values = jnp.concatenate([values[1:], following], axis=0)
    continuing = (1.0 - episode_ends[0].astype(jnp.float32))[:, None]
    trace_cut = jnp.minimum(1.0, ratios[0])[:, None]
    add_terms = (
        rewards[0][:, None]
        + discounts[None, :] * continuing * (1.0 - lambdas[None, :] * trace_cut) * next_values
    )
    mul_terms = discounts[None, :] * lambdas[None, :] * trace_cut * continuing

    def suffix(carry, inputs):
        add_term, mul_term = inputs
        new_add = add_term + mul_term * carry[0]
        new_mul = mul_term * carry[1]
        return ((new_add, new_mul), (new_add, new_mul))

    zero_row = jnp.zeros((add_terms.shape[1],), jnp.float32)
    one_row = jnp.ones((add_terms.shape[1],), jnp.float32)
    (shard_add, shard_mul), (prefix_add, prefix_mul) = lax.scan(
        suffix, (zero_row, one_row), (add_terms, mul_terms), reverse=True
    )

    def relay_carry(step_index, incoming_row):
        return from_behind((shard_add + shard_mul * incoming_row)[None], "tm", -1)[0]

    incoming = lax.fori_loop(0, shards - 1, relay_carry, zero_row)
    returns = prefix_add + prefix_mul * incoming[None, :]
    targets = valid_steps[0].astype(jnp.float32)[:, None] * returns
    return (latents[None], values[None], targets[None], load_here.reshape(1, 1))


def solution(mesh):
    in_specs = (
        P("grp", "tm", None, None, None),
        P("grp", "tm"),
        P("grp", "tm"),
        P("grp", "tm"),
        P("grp", "tm"),
        P("grp", "tm"),
        P("grp", "tm"),
        P("grp", "tm", None),
        P(),
        P(),
        P(),
        P(),
        P(),
        P(),
    )
    out_specs = (
        P("grp", "tm", None, None, None),
        P("grp", "tm", None),
        P("grp", "tm", None),
        P("grp", "tm"),
    )
    return jax.shard_map(
        per_device, mesh=mesh, in_specs=in_specs, out_specs=out_specs, check_vma=False
    )
```

profile of v0, /device:TPU:7, one launch (start us, length us, event | category | flops | bytes accessed | tf_op | source)
XLA Modules:
  0.0 341.8 jit_solution(16778305689908661221)
XLA Ops:
  10.3 8.7 %fusion.116 = (bf16[4,24,24,1024]{3,2,1,0:T(8,128)(2,1)}, bf16[4,24,24,1024]{3,2,1,0:T(8,128)(2,1)}) fusion(bf16[4,24,24,2048]{3,2,1,0:T(8,128)(2,1)} %bitcast.273), kind=kLoop, calls=%fused_computation.243 | loop fusion | bytes 18874368 | tf_op jit(solution)/shard_map/jit(_take)/gather | solution.py:84
  19.0 5.4 %gather_fusion.3 = bf16[4,24,24,1024]{3,2,1,0:T(8,128)(2,1)} fusion(bf16[4,24,24,1024]{3,2,1,0:T(8,128)(2,1)} %get-tuple-element.231, s32[1024]{0:T(1024)S(1)} %pad_clamp_fusion.3), kind=kCustom, calls=%fused_computation.3 | custom fusion | bytes 9437200 | tf_op jit(solution)/shard_map/jit(_take)/gather | solution.py:84
  24.4 5.3 %gather_fusion.4 = bf16[4,24,24,1024]{3,2,1,0:T(8,128)(2,1)} fusion(bf16[4,24,24,1024]{3,2,1,0:T(8,128)(2,1)} %get-tuple-element.232, s32[1024]{0:T(1024)S(1)} %pad_clamp_fusion.3), kind=kCustom, calls=%fused_computation.4 | custom fusion | bytes 9437200 | tf_op jit(solution)/shard_map/jit(_take)/gather | solution.py:84
  29.9 9.3 %pad_maximum_fusion = bf16[4,24,24,2048]{3,2,1,0:T(8,128)(2,1)} fusion(bf16[4,24,24,1024]{3,2,1,0:T(8,128)(2,1)} %gather_fusion.4, bf16[4,24,24,1024]{3,2,1,0:T(8,128)(2,1)} %gather_fusion.3), kind=kLoop, calls=%fused_computation.12 | loop fusion | flops 18874368 | bytes 18874368
  39.2 8.3 %bitcast_select_fusion = bf16[2304,2048]{1,0:T(8,128)(2,1)} fusion(bf16[4,24,24,2048]{3,2,1,0:T(8,128)(2,1)} %pad_maximum_fusion, pred[2304]{0:T(1024)(128)(4,1)S(1)} %broadcast_in_dim.164), kind=kLoop, calls=%fused_computation.13 | loop fusion | flops 4718592 | bytes 18876672 | tf_op jit(solution)/shard_map/jit(_take)/select_n | solution.py:84
  47.4 6.3 %fusion.3 = bf16[2304,256]{1,0:T(8,128)(2,1)S(1)} fusion(bf16[2304,2048]{1,0:T(8,128)(2,1)} %bitcast_select_fusion, bf16[2048,256]{1,0:T(8,128)(2,1)S(1)} %copy-done), kind=kOutput, calls=%fused_computation.15 | convolution fusion | flops 2417098752 | bytes 11665408 | tf_op jit(solution)/shard_map/dot_general | solution.py:30
  60.1 14.1 %all-to-all-done.1 = bf16[4,1,24,24,256]{4,3,2,1,0:T(8,128)(2,1)S(1)} async-done(((bf16[4,1,24,24,256]{4,3,2,1,0:T(8,128)(2,1)}), bf16[4,1,24,24,256]{4,3,2,1,0:T(8,128)(2,1)S(1)}, u32[]{:S(2)}, u32[]{:S(2)}) %all-to-all-start.1) | async-done | bytes 1179680 | tf_op jit(solution)/shard_map/all_to_all | solution.py:89
  101.6 12.7 %all-to-all-done.2 = bf16[4,1,24,24,256]{4,3,2,1,0:T(8,128)(2,1)S(1)} async-done(((bf16[4,1,24,24,256]{4,3,2,1,0:T(8,128)(2,1)}), bf16[4,1,24,24,256]{4,3,2,1,0:T(8,128)(2,1)S(1)}, u32[]{:S(2)}, u32[]{:S(2)}) %all-to-all-start.2) | async-done | bytes 1179680 | tf_op jit(solution)/shard_map/all_to_all | solution.py:123
  116.0 5.4 %collective-permute-start.1 = (f32[1,128]{1,0:T(1,128)S(1)}, f32[1,128]{1,0:T(1,128)S(1)}, u32[]{:S(2)}, u32[]{:S(2)}) collective-permute-start(f32[1,128]{1,0:T(1,128)S(1)} %slice.359), channel_id=1, source_target_pairs={{1,0},{2,1},{3,2},{4,3},{5,4},{6,5},{7,6},{8,7},{9,8},{10,9},{11,1... | collective-permute-start | bytes 1544 | tf_op jit(solution)/shard_map/ppermute | solution.py:10
  124.2 215.9 %while.31 = (s32[]{:T(128)}, f32[128]{0:T(128)S(1)}, f32[128]{0:T(128)S(1)}, f32[128]{0:T(128)S(1)}, s32[]{:T(128)}) while((s32[]{:T(128)}, f32[128]{0:T(128)S(1)}, f32[128]{0:T(128)S(1)}, f32[128]{0:T(128)S(1)}, s32[]{:T(128)}) %tuple.98), condition=%wide.region_13.14_spmd, body=%wide.region_12.13_spmd.sunk | while | flops 258 | bytes 4197 | solution.py:163
  126.1 5.0 %collective-permute-done = f32[1,128]{1,0:T(1,128)S(1)} collective-permute-done((f32[1,128]{1,0:T(1,128)S(1)}, f32[1,128]{1,0:T(1,128)S(1)}, u32[]{:S(2)}, u32[]{:S(2)}) %collective-permute-start) | collective-permute-done | bytes 544 | tf_op jit(solution)/shard_map/while/body/eval_jaxpr/ppermute | solution.py:10
  133.1 5.0 %collective-permute-done = f32[1,128]{1,0:T(1,128)S(1)} collective-permute-done((f32[1,128]{1,0:T(1,128)S(1)}, f32[1,128]{1,0:T(1,128)S(1)}, u32[]{:S(2)}, u32[]{:S(2)}) %collective-permute-start) | collective-permute-done | bytes 544 | tf_op jit(solution)/shard_map/while/body/eval_jaxpr/ppermute | solution.py:10
  140.1 5.0 %collective-permute-done = f32[1,128]{1,0:T(1,128)S(1)} collective-permute-done((f32[1,128]{1,0:T(1,128)S(1)}, f32[1,128]{1,0:T(1,128)S(1)}, u32[]{:S(2)}, u32[]{:S(2)}) %collective-permute-start) | collective-permute-done | bytes 544 | tf_op jit(solution)/shard_map/while/body/eval_jaxpr/ppermute | solution.py:10
  147.0 5.0 %collective-permute-done = f32[1,128]{1,0:T(1,128)S(1)} collective-permute-done((f32[1,128]{1,0:T(1,128)S(1)}, f32[1,128]{1,0:T(1,128)S(1)}, u32[]{:S(2)}, u32[]{:S(2)}) %collective-permute-start) | collective-permute-done | bytes 544 | tf_op jit(solution)/shard_map/while/body/eval_jaxpr/ppermute | solution.py:10
  154.0 5.0 %collective-permute-done = f32[1,128]{1,0:T(1,128)S(1)} collective-permute-done((f32[1,128]{1,0:T(1,128)S(1)}, f32[1,128]{1,0:T(1,128)S(1)}, u32[]{:S(2)}, u32[]{:S(2)}) %collective-permute-start) | collective-permute-done | bytes 544 | tf_op jit(solution)/shard_map/while/body/eval_jaxpr/ppermute | solution.py:10
  160.9 5.0 %collective-permute-done = f32[1,128]{1,0:T(1,128)S(1)} collective-permute-done((f32[1,128]{1,0:T(1,128)S(1)}, f32[1,128]{1,0:T(1,128)S(1)}, u32[]{:S(2)}, u32[]{:S(2)}) %collective-permute-start) | collective-permute-done | bytes 544 | tf_op jit(solution)/shard_map/while/body/eval_jaxpr/ppermute | solution.py:10
  167.9 5.0 %collective-permute-done = f32[1,128]{1,0:T(1,128)S(1)} collective-permute-done((f32[1,128]{1,0:T(1,128)S(1)}, f32[1,128]{1,0:T(1,128)S(1)}, u32[]{:S(2)}, u32[]{:S(2)}) %collective-permute-start) | collective-permute-done | bytes 544 | tf_op jit(solution)/shard_map/while/body/eval_jaxpr/ppermute | solution.py:10
  174.9 5.0 %collective-permute-done = f32[1,128]{1,0:T(1,128)S(1)} collective-permute-done((f32[1,128]{1,0:T(1,128)S(1)}, f32[1,128]{1,0:T(1,128)S(1)}, u32[]{:S(2)}, u32[]{:S(2)}) %collective-permute-start) | collective-permute-done | bytes 544 | tf_op jit(solution)/shard_map/while/body/eval_jaxpr/ppermute | solution.py:10
  181.8 5.0 %collective-permute-done = f32[1,128]{1,0:T(1,128)S(1)} collective-permute-done((f32[1,128]{1,0:T(1,128)S(1)}, f32[1,128]{1,0:T(1,128)S(1)}, u32[]{:S(2)}, u32[]{:S(2)}) %collective-permute-start) | collective-permute-done | bytes 544 | tf_op jit(solution)/shard_map/while/body/eval_jaxpr/ppermute | solution.py:10
  188.8 5.0 %collective-permute-done = f32[1,128]{1,0:T(1,128)S(1)} collective-permute-done((f32[1,128]{1,0:T(1,128)S(1)}, f32[1,128]{1,0:T(1,128)S(1)}, u32[]{:S(2)}, u32[]{:S(2)}) %collective-permute-start) | collective-permute-done | bytes 544 | tf_op jit(solution)/shard_map/while/body/eval_jaxpr/ppermute | solution.py:10
  195.8 5.0 %collective-permute-done = f32[1,128]{1,0:T(1,128)S(1)} collective-permute-done((f32[1,128]{1,0:T(1,128)S(1)}, f32[1,128]{1,0:T(1,128)S(1)}, u32[]{:S(2)}, u32[]{:S(2)}) %collective-permute-start) | collective-permute-done | bytes 544 | tf_op jit(solution)/shard_map/while/body/eval_jaxpr/ppermute | solution.py:10
  202.7 5.0 %collective-permute-done = f32[1,128]{1,0:T(1,128)S(1)} collective-permute-done((f32[1,128]{1,0:T(1,128)S(1)}, f32[1,128]{1,0:T(1,128)S(1)}, u32[]{:S(2)}, u32[]{:S(2)}) %collective-permute-start) | collective-permute-done | bytes 544 | tf_op jit(solution)/shard_map/while/body/eval_jaxpr/ppermute | solution.py:10
  209.7 5.0 %collective-permute-done = f32[1,128]{1,0:T(1,128)S(1)} collective-permute-done((f32[1,128]{1,0:T(1,128)S(1)}, f32[1,128]{1,0:T(1,128)S(1)}, u32[]{:S(2)}, u32[]{:S(2)}) %collective-permute-start) | collective-permute-done | bytes 544 | tf_op jit(solution)/shard_map/while/body/eval_jaxpr/ppermute | solution.py:10
  216.6 5.0 %collective-permute-done = f32[1,128]{1,0:T(1,128)S(1)} collective-permute-done((f32[1,128]{1,0:T(1,128)S(1)}, f32[1,128]{1,0:T(1,128)S(1)}, u32[]{:S(2)}, u32[]{:S(2)}) %collective-permute-start) | collective-permute-done | bytes 544 | tf_op jit(solution)/shard_map/while/body/eval_jaxpr/ppermute | solution.py:10
  223.6 5.0 %collective-permute-done = f32[1,128]{1,0:T(1,128)S(1)} collective-permute-done((f32[1,128]{1,0:T(1,128)S(1)}, f32[1,128]{1,0:T(1,128)S(1)}, u32[]{:S(2)}, u32[]{:S(2)}) %collective-permute-start) | collective-permute-done | bytes 544 | tf_op jit(solution)/shard_map/while/body/eval_jaxpr/ppermute | solution.py:10
  230.6 5.0 %collective-permute-done = f32[1,128]{1,0:T(1,128)S(1)} collective-permute-done((f32[1,128]{1,0:T(1,128)S(1)}, f32[1,128]{1,0:T(1,128)S(1)}, u32[]{:S(2)}, u32[]{:S(2)}) %collective-permute-start) | collective-permute-done | bytes 544 | tf_op jit(solution)/shard_map/while/body/eval_jaxpr/ppermute | solution.py:10
  237.5 5.0 %collective-permute-done = f32[1,128]{1,0:T(1,128)S(1)} collective-permute-done((f32[1,128]{1,0:T(1,128)S(1)}, f32[1,128]{1,0:T(1,128)S(1)}, u32[]{:S(2)}, u32[]{:S(2)}) %collective-permute-start) | collective-permute-done | bytes 544 | tf_op jit(solution)/shard_map/while/body/eval_jaxpr/ppermute | solution.py:10
  244.5 5.0 %collective-permute-done = f32[1,128]{1,0:T(1,128)S(1)} collective-permute-done((f32[1,128]{1,0:T(1,128)S(1)}, f32[1,128]{1,0:T(1,128)S(1)}, u32[]{:S(2)}, u32[]{:S(2)}) %collective-permute-start) | collective-permute-done | bytes 544 | tf_op jit(solution)/shard_map/while/body/eval_jaxpr/ppermute | solution.py:10
  251.5 5.0 %collective-permute-done = f32[1,128]{1,0:T(1,128)S(1)} collective-permute-done((f32[1,128]{1,0:T(1,128)S(1)}, f32[1,128]{1,0:T(1,128)S(1)}, u32[]{:S(2)}, u32[]{:S(2)}) %collective-permute-start) | collective-permute-done | bytes 544 | tf_op jit(solution)/shard_map/while/body/eval_jaxpr/ppermute | solution.py:10
  258.4 5.0 %collective-permute-done = f32[1,128]{1,0:T(1,128)S(1)} collective-permute-done((f32[1,128]{1,0:T(1,128)S(1)}, f32[1,128]{1,0:T(1,128)S(1)}, u32[]{:S(2)}, u32[]{:S(2)}) %collective-permute-start) | collective-permute-done | bytes 544 | tf_op jit(solution)/shard_map/while/body/eval_jaxpr/ppermute | solution.py:10
  265.4 5.0 %collective-permute-done = f32[1,128]{1,0:T(1,128)S(1)} collective-permute-done((f32[1,128]{1,0:T(1,128)S(1)}, f32[1,128]{1,0:T(1,128)S(1)}, u32[]{:S(2)}, u32[]{:S(2)}) %collective-permute-start) | collective-permute-done | bytes 544 | tf_op jit(solution)/shard_map/while/body/eval_jaxpr/ppermute | solution.py:10
  321.1 5.0 %collective-permute-done = f32[1,128]{1,0:T(1,128)S(1)} collective-permute-done((f32[1,128]{1,0:T(1,128)S(1)}, f32[1,128]{1,0:T(1,128)S(1)}, u32[]{:S(2)}, u32[]{:S(2)}) %collective-permute-start) | collective-permute-done | bytes 544 | tf_op jit(solution)/shard_map/while/body/eval_jaxpr/ppermute | solution.py:10
  (217 shorter events, 152.5 us)
Async XLA Ops:
  5.2 49.7 %all-to-all-start = ((bf16[4,1,1]{2,1,0:T(2,128)(2,1)}), bf16[4,1,1]{2,1,0:T(2,128)(2,1)S(1)}, u32[]{:S(2)}, u32[]{:S(2)}) async-start(bf16[4,1,1]{2,1,0:T(2,128)(2,1)} %copy.22), calls=%async_computation | async-start | bytes 4096 | tf_op jit(solution)/shard_map/all_to_all | solution.py:96
  54.9 19.3 %all-to-all-start.1 = ((bf16[4,1,24,24,256]{4,3,2,1,0:T(8,128)(2,1)}), bf16[4,1,24,24,256]{4,3,2,1,0:T(8,128)(2,1)S(1)}, u32[]{:S(2)}, u32[]{:S(2)}) async-start(bf16[4,1,24,24,256]{4,3,2,1,0:T(8,128)(2,1)} %broadcast_select_fusion.2), calls=%async_computation.1 | async-start | bytes 2359296 | tf_op jit(solution)/shard_map/all_to_all | solution.py:89
  96.6 17.8 %all-to-all-start.2 = ((bf16[4,1,24,24,256]{4,3,2,1,0:T(8,128)(2,1)}), bf16[4,1,24,24,256]{4,3,2,1,0:T(8,128)(2,1)S(1)}, u32[]{:S(2)}, u32[]{:S(2)}) async-start(bf16[4,1,24,24,256]{4,3,2,1,0:T(8,128)(2,1)} %fusion.19), calls=%async_computation.2 | async-start | bytes 2359296 | tf_op jit(solution)/shard_map/all_to_all | solution.py:123
  116.0 7.7 %collective-permute-start.1 = (f32[1,128]{1,0:T(1,128)S(1)}, f32[1,128]{1,0:T(1,128)S(1)}, u32[]{:S(2)}, u32[]{:S(2)}) collective-permute-start(f32[1,128]{1,0:T(1,128)S(1)} %slice.359), channel_id=1, source_target_pairs={{1,0},{2,1},{3,2},{4,3},{5,4},{6,5},{7,6},{8,7},{9,8},{10,9},{11,1... | collective-permute-start | bytes 1544 | tf_op jit(solution)/shard_map/ppermute | solution.py:10
  124.2 7.0 %collective-permute-start = (f32[1,128]{1,0:T(1,128)S(1)}, f32[1,128]{1,0:T(1,128)S(1)}, u32[]{:S(2)}, u32[]{:S(2)}) collective-permute-start(f32[1,128]{1,0:T(1,128)S(1)} %add_bitcast_fusion.3), channel_id=1, source_target_pairs={{1,0},{2,1},{3,2},{4,3},{5,4},{6,5},{7,6},{8,7},{9,8},{10,9},{11,1... | collective-permute-start | bytes 1544 | tf_op jit(solution)/shard_map/while/body/eval_jaxpr/ppermute | solution.py:10
  131.2 7.0 %collective-permute-start = (f32[1,128]{1,0:T(1,128)S(1)}, f32[1,128]{1,0:T(1,128)S(1)}, u32[]{:S(2)}, u32[]{:S(2)}) collective-permute-start(f32[1,128]{1,0:T(1,128)S(1)} %add_bitcast_fusion.3), channel_id=1, source_target_pairs={{1,0},{2,1},{3,2},{4,3},{5,4},{6,5},{7,6},{8,7},{9,8},{10,9},{11,1... | collective-permute-start | bytes 1544 | tf_op jit(solution)/shard_map/while/body/eval_jaxpr/ppermute | solution.py:10
  138.1 7.0 %collective-permute-start = (f32[1,128]{1,0:T(1,128)S(1)}, f32[1,128]{1,0:T(1,128)S(1)}, u32[]{:S(2)}, u32[]{:S(2)}) collective-permute-start(f32[1,128]{1,0:T(1,128)S(1)} %add_bitcast_fusion.3), channel_id=1, source_target_pairs={{1,0},{2,1},{3,2},{4,3},{5,4},{6,5},{7,6},{8,7},{9,8},{10,9},{11,1... | collective-permute-start | bytes 1544 | tf_op jit(solution)/shard_map/while/body/eval_jaxpr/ppermute | solution.py:10
  145.1 7.0 %collective-permute-start = (f32[1,128]{1,0:T(1,128)S(1)}, f32[1,128]{1,0:T(1,128)S(1)}, u32[]{:S(2)}, u32[]{:S(2)}) collective-permute-start(f32[1,128]{1,0:T(1,128)S(1)} %add_bitcast_fusion.3), channel_id=1, source_target_pairs={{1,0},{2,1},{3,2},{4,3},{5,4},{6,5},{7,6},{8,7},{9,8},{10,9},{11,1... | collective-permute-start | bytes 1544 | tf_op jit(solution)/shard_map/while/body/eval_jaxpr/ppermute | solution.py:10
  152.1 7.0 %collective-permute-start = (f32[1,128]{1,0:T(1,128)S(1)}, f32[1,128]{1,0:T(1,128)S(1)}, u32[]{:S(2)}, u32[]{:S(2)}) collective-permute-start(f32[1,128]{1,0:T(1,128)S(1)} %add_bitcast_fusion.3), channel_id=1, source_target_pairs={{1,0},{2,1},{3,2},{4,3},{5,4},{6,5},{7,6},{8,7},{9,8},{10,9},{11,1... | collective-permute-start | bytes 1544 | tf_op jit(solution)/shard_map/while/body/eval_jaxpr/ppermute | solution.py:10
  159.0 7.0 %collective-permute-start = (f32[1,128]{1,0:T(1,128)S(1)}, f32[1,128]{1,0:T(1,128)S(1)}, u32[]{:S(2)}, u32[]{:S(2)}) collective-permute-start(f32[1,128]{1,0:T(1,128)S(1)} %add_bitcast_fusion.3), channel_id=1, source_target_pairs={{1,0},{2,1},{3,2},{4,3},{5,4},{6,5},{7,6},{8,7},{9,8},{10,9},{11,1... | collective-permute-start | bytes 1544 | tf_op jit(solution)/shard_map/while/body/eval_jaxpr/ppermute | solution.py:10
  166.0 7.0 %collective-permute-start = (f32[1,128]{1,0:T(1,128)S(1)}, f32[1,128]{1,0:T(1,128)S(1)}, u32[]{:S(2)}, u32[]{:S(2)}) collective-permute-start(f32[1,128]{1,0:T(1,128)S(1)} %add_bitcast_fusion.3), channel_id=1, source_target_pairs={{1,0},{2,1},{3,2},{4,3},{5,4},{6,5},{7,6},{8,7},{9,8},{10,9},{11,1... | collective-permute-start | bytes 1544 | tf_op jit(solution)/shard_map/while/body/eval_jaxpr/ppermute | solution.py:10
  172.9 7.0 %collective-permute-start = (f32[1,128]{1,0:T(1,128)S(1)}, f32[1,128]{1,0:T(1,128)S(1)}, u32[]{:S(2)}, u32[]{:S(2)}) collective-permute-start(f32[1,128]{1,0:T(1,128)S(1)} %add_bitcast_fusion.3), channel_id=1, source_target_pairs={{1,0},{2,1},{3,2},{4,3},{5,4},{6,5},{7,6},{8,7},{9,8},{10,9},{11,1... | collective-permute-start | bytes 1544 | tf_op jit(solution)/shard_map/while/body/eval_jaxpr/ppermute | solution.py:10
  179.9 7.0 %collective-permute-start = (f32[1,128]{1,0:T(1,128)S(1)}, f32[1,128]{1,0:T(1,128)S(1)}, u32[]{:S(2)}, u32[]{:S(2)}) collective-permute-start(f32[1,128]{1,0:T(1,128)S(1)} %add_bitcast_fusion.3), channel_id=1, source_target_pairs={{1,0},{2,1},{3,2},{4,3},{5,4},{6,5},{7,6},{8,7},{9,8},{10,9},{11,1... | collective-permute-start | bytes 1544 | tf_op jit(solution)/shard_map/while/body/eval_jaxpr/ppermute | solution.py:10
  186.9 7.0 %collective-permute-start = (f32[1,128]{1,0:T(1,128)S(1)}, f32[1,128]{1,0:T(1,128)S(1)}, u32[]{:S(2)}, u32[]{:S(2)}) collective-permute-start(f32[1,128]{1,0:T(1,128)S(1)} %add_bitcast_fusion.3), channel_id=1, source_target_pairs={{1,0},{2,1},{3,2},{4,3},{5,4},{6,5},{7,6},{8,7},{9,8},{10,9},{11,1... | collective-permute-start | bytes 1544 | tf_op jit(solution)/shard_map/while/body/eval_jaxpr/ppermute | solution.py:10
  193.8 7.0 %collective-permute-start = (f32[1,128]{1,0:T(1,128)S(1)}, f32[1,128]{1,0:T(1,128)S(1)}, u32[]{:S(2)}, u32[]{:S(2)}) collective-permute-start(f32[1,128]{1,0:T(1,128)S(1)} %add_bitcast_fusion.3), channel_id=1, source_target_pairs={{1,0},{2,1},{3,2},{4,3},{5,4},{6,5},{7,6},{8,7},{9,8},{10,9},{11,1... | collective-permute-start | bytes 1544 | tf_op jit(solution)/shard_map/while/body/eval_jaxpr/ppermute | solution.py:10
  200.8 7.0 %collective-permute-start = (f32[1,128]{1,0:T(1,128)S(1)}, f32[1,128]{1,0:T(1,128)S(1)}, u32[]{:S(2)}, u32[]{:S(2)}) collective-permute-start(f32[1,128]{1,0:T(1,128)S(1)} %add_bitcast_fusion.3), channel_id=1, source_target_pairs={{1,0},{2,1},{3,2},{4,3},{5,4},{6,5},{7,6},{8,7},{9,8},{10,9},{11,1... | collective-permute-start | bytes 1544 | tf_op jit(solution)/shard_map/while/body/eval_jaxpr/ppermute | solution.py:10
  207.8 7.0 %collective-permute-start = (f32[1,128]{1,0:T(1,128)S(1)}, f32[1,128]{1,0:T(1,128)S(1)}, u32[]{:S(2)}, u32[]{:S(2)}) collective-permute-start(f32[1,128]{1,0:T(1,128)S(1)} %add_bitcast_fusion.3), channel_id=1, source_target_pairs={{1,0},{2,1},{3,2},{4,3},{5,4},{6,5},{7,6},{8,7},{9,8},{10,9},{11,1... | collective-permute-start | bytes 1544 | tf_op jit(solution)/shard_map/while/body/eval_jaxpr/ppermute | solution.py:10
  214.7 7.0 %collective-permute-start = (f32[1,128]{1,0:T(1,128)S(1)}, f32[1,128]{1,0:T(1,128)S(1)}, u32[]{:S(2)}, u32[]{:S(2)}) collective-permute-start(f32[1,128]{1,0:T(1,128)S(1)} %add_bitcast_fusion.3), channel_id=1, source_target_pairs={{1,0},{2,1},{3,2},{4,3},{5,4},{6,5},{7,6},{8,7},{9,8},{10,9},{11,1... | collective-permute-start | bytes 1544 | tf_op jit(solution)/shard_map/while/body/eval_jaxpr/ppermute | solution.py:10
  221.7 7.0 %collective-permute-start = (f32[1,128]{1,0:T(1,128)S(1)}, f32[1,128]{1,0:T(1,128)S(1)}, u32[]{:S(2)}, u32[]{:S(2)}) collective-permute-start(f32[1,128]{1,0:T(1,128)S(1)} %add_bitcast_fusion.3), channel_id=1, source_target_pairs={{1,0},{2,1},{3,2},{4,3},{5,4},{6,5},{7,6},{8,7},{9,8},{10,9},{11,1... | collective-permute-start | bytes 1544 | tf_op jit(solution)/shard_map/while/body/eval_jaxpr/ppermute | solution.py:10
  228.7 7.0 %collective-permute-start = (f32[1,128]{1,0:T(1,128)S(1)}, f32[1,128]{1,0:T(1,128)S(1)}, u32[]{:S(2)}, u32[]{:S(2)}) collective-permute-start(f32[1,128]{1,0:T(1,128)S(1)} %add_bitcast_fusion.3), channel_id=1, source_target_pairs={{1,0},{2,1},{3,2},{4,3},{5,4},{6,5},{7,6},{8,7},{9,8},{10,9},{11,1... | collective-permute-start | bytes 1544 | tf_op jit(solution)/shard_map/while/body/eval_jaxpr/ppermute | solution.py:10
  235.6 7.0 %collective-permute-start = (f32[1,128]{1,0:T(1,128)S(1)}, f32[1,128]{1,0:T(1,128)S(1)}, u32[]{:S(2)}, u32[]{:S(2)}) collective-permute-start(f32[1,128]{1,0:T(1,128)S(1)} %add_bitcast_fusion.3), channel_id=1, source_target_pairs={{1,0},{2,1},{3,2},{4,3},{5,4},{6,5},{7,6},{8,7},{9,8},{10,9},{11,1... | collective-permute-start | bytes 1544 | tf_op jit(solution)/shard_map/while/body/eval_jaxpr/ppermute | solution.py:10
  242.6 7.0 %collective-permute-start = (f32[1,128]{1,0:T(1,128)S(1)}, f32[1,128]{1,0:T(1,128)S(1)}, u32[]{:S(2)}, u32[]{:S(2)}) collective-permute-start(f32[1,128]{1,0:T(1,128)S(1)} %add_bitcast_fusion.3), channel_id=1, source_target_pairs={{1,0},{2,1},{3,2},{4,3},{5,4},{6,5},{7,6},{8,7},{9,8},{10,9},{11,1... | collective-permute-start | bytes 1544 | tf_op jit(solution)/shard_map/while/body/eval_jaxpr/ppermute | solution.py:10
  249.5 7.0 %collective-permute-start = (f32[1,128]{1,0:T(1,128)S(1)}, f32[1,128]{1,0:T(1,128)S(1)}, u32[]{:S(2)}, u32[]{:S(2)}) collective-permute-start(f32[1,128]{1,0:T(1,128)S(1)} %add_bitcast_fusion.3), channel_id=1, source_target_pairs={{1,0},{2,1},{3,2},{4,3},{5,4},{6,5},{7,6},{8,7},{9,8},{10,9},{11,1... | collective-permute-start | bytes 1544 | tf_op jit(solution)/shard_map/while/body/eval_jaxpr/ppermute | solution.py:10
  256.5 7.0 %collective-permute-start = (f32[1,128]{1,0:T(1,128)S(1)}, f32[1,128]{1,0:T(1,128)S(1)}, u32[]{:S(2)}, u32[]{:S(2)}) collective-permute-start(f32[1,128]{1,0:T(1,128)S(1)} %add_bitcast_fusion.3), channel_id=1, source_target_pairs={{1,0},{2,1},{3,2},{4,3},{5,4},{6,5},{7,6},{8,7},{9,8},{10,9},{11,1... | collective-permute-start | bytes 1544 | tf_op jit(solution)/shard_map/while/body/eval_jaxpr/ppermute | solution.py:10
  263.5 7.0 %collective-permute-start = (f32[1,128]{1,0:T(1,128)S(1)}, f32[1,128]{1,0:T(1,128)S(1)}, u32[]{:S(2)}, u32[]{:S(2)}) collective-permute-start(f32[1,128]{1,0:T(1,128)S(1)} %add_bitcast_fusion.3), channel_id=1, source_target_pairs={{1,0},{2,1},{3,2},{4,3},{5,4},{6,5},{7,6},{8,7},{9,8},{10,9},{11,1... | collective-permute-start | bytes 1544 | tf_op jit(solution)/shard_map/while/body/eval_jaxpr/ppermute | solution.py:10
  270.4 7.0 %collective-permute-start = (f32[1,128]{1,0:T(1,128)S(1)}, f32[1,128]{1,0:T(1,128)S(1)}, u32[]{:S(2)}, u32[]{:S(2)}) collective-permute-start(f32[1,128]{1,0:T(1,128)S(1)} %add_bitcast_fusion.3), channel_id=1, source_target_pairs={{1,0},{2,1},{3,2},{4,3},{5,4},{6,5},{7,6},{8,7},{9,8},{10,9},{11,1... | collective-permute-start | bytes 1544 | tf_op jit(solution)/shard_map/while/body/eval_jaxpr/ppermute | solution.py:10
  277.4 7.0 %collective-permute-start = (f32[1,128]{1,0:T(1,128)S(1)}, f32[1,128]{1,0:T(1,128)S(1)}, u32[]{:S(2)}, u32[]{:S(2)}) collective-permute-start(f32[1,128]{1,0:T(1,128)S(1)} %add_bitcast_fusion.3), channel_id=1, source_target_pairs={{1,0},{2,1},{3,2},{4,3},{5,4},{6,5},{7,6},{8,7},{9,8},{10,9},{11,1... | collective-permute-start | bytes 1544 | tf_op jit(solution)/shard_map/while/body/eval_jaxpr/ppermute | solution.py:10
  284.4 7.0 %collective-permute-start = (f32[1,128]{1,0:T(1,128)S(1)}, f32[1,128]{1,0:T(1,128)S(1)}, u32[]{:S(2)}, u32[]{:S(2)}) collective-permute-start(f32[1,128]{1,0:T(1,128)S(1)} %add_bitcast_fusion.3), channel_id=1, source_target_pairs={{1,0},{2,1},{3,2},{4,3},{5,4},{6,5},{7,6},{8,7},{9,8},{10,9},{11,1... | collective-permute-start | bytes 1544 | tf_op jit(solution)/shard_map/while/body/eval_jaxpr/ppermute | solution.py:10
  291.3 7.0 %collective-permute-start = (f32[1,128]{1,0:T(1,128)S(1)}, f32[1,128]{1,0:T(1,128)S(1)}, u32[]{:S(2)}, u32[]{:S(2)}) collective-permute-start(f32[1,128]{1,0:T(1,128)S(1)} %add_bitcast_fusion.3), channel_id=1, source_target_pairs={{1,0},{2,1},{3,2},{4,3},{5,4},{6,5},{7,6},{8,7},{9,8},{10,9},{11,1... | collective-permute-start | bytes 1544 | tf_op jit(solution)/shard_map/while/body/eval_jaxpr/ppermute | solution.py:10
  298.3 7.0 %collective-permute-start = (f32[1,128]{1,0:T(1,128)S(1)}, f32[1,128]{1,0:T(1,128)S(1)}, u32[]{:S(2)}, u32[]{:S(2)}) collective-permute-start(f32[1,128]{1,0:T(1,128)S(1)} %add_bitcast_fusion.3), channel_id=1, source_target_pairs={{1,0},{2,1},{3,2},{4,3},{5,4},{6,5},{7,6},{8,7},{9,8},{10,9},{11,1... | collective-permute-start | bytes 1544 | tf_op jit(solution)/shard_map/while/body/eval_jaxpr/ppermute | solution.py:10
  319.2 7.0 %collective-permute-start = (f32[1,128]{1,0:T(1,128)S(1)}, f32[1,128]{1,0:T(1,128)S(1)}, u32[]{:S(2)}, u32[]{:S(2)}) collective-permute-start(f32[1,128]{1,0:T(1,128)S(1)} %add_bitcast_fusion.3), channel_id=1, source_target_pairs={{1,0},{2,1},{3,2},{4,3},{5,4},{6,5},{7,6},{8,7},{9,8},{10,9},{11,1... | collective-permute-start | bytes 1544 | tf_op jit(solution)/shard_map/while/body/eval_jaxpr/ppermute | solution.py:10
  333.1 7.0 %collective-permute-start = (f32[1,128]{1,0:T(1,128)S(1)}, f32[1,128]{1,0:T(1,128)S(1)}, u32[]{:S(2)}, u32[]{:S(2)}) collective-permute-start(f32[1,128]{1,0:T(1,128)S(1)} %add_bitcast_fusion.3), channel_id=1, source_target_pairs={{1,0},{2,1},{3,2},{4,3},{5,4},{6,5},{7,6},{8,7},{9,8},{10,9},{11,1... | collective-permute-start | bytes 1544 | tf_op jit(solution)/shard_map/while/body/eval_jaxpr/ppermute | solution.py:10
  (19 other events, 332.4 us)
where the time goes:
time: 344 us; the launch traced here: 342 us
  waiting for transfers between devices  184 us (53%)
  starting transfers between devices  77.5 us (23%)
  local copies, waits for them, and re-layouts  29.8 us (9%)
  other arithmetic  28.8 us (8%)
  matrix products  18.2 us (5%)
    ppermute x32, waiting for transfers between devices, from_behind(): return lax.ppermute(block, axis, route)  157 us
    ppermute x32, starting transfers between devices, from_behind(): return lax.ppermute(block, axis, route)  64.6 us
    gather x3, local copies, waits for them, and re-layouts, per_device(): chosen = jnp.take(blocks, block_of_slot, axis=0)  19.5 us
    all_to_all x1, waiting for transfers between devices, per_device(): lax.all_to_all(outgoing.reshape(groups_here, per_pair, grid_side, grid_si...  14.1 us
    all_to_all x1, waiting for transfers between devices, per_device(): lax.all_to_all(returning.reshape(groups_here, per_pair, grid_side, grid_s...  12.7 us
    dot_general x36, matrix products, conv_tap(): jnp.dot(window, weight[tap_index], preferred_element_type=jnp.float32)  11.8 us
    unnamed x3, other arithmetic  9.25 us
    select_n x2, other arithmetic, per_device(): chosen = jnp.take(blocks, block_of_slot, axis=0)  8.26 us
  transfers between devices with their start and end apart: 35, of which 34 were waited for; matrix products, arithmetic and copies ran while one was open for 14% of the time, Pallas kernels for 0%

commit v1 on v0

v1 whole, which is shorter than its diff:
```python
import jax
import jax.numpy as jnp
from jax import lax
from jax.experimental import pallas as pl
from jax.experimental.pallas import tpu as pltpu
from jax.sharding import PartitionSpec as P

BF = jnp.bfloat16
F32 = jnp.float32


def conv(x, w):
    return lax.conv_general_dilated(
        x,
        w.reshape(3, 3, w.shape[1], w.shape[2]),
        (1, 1),
        "SAME",
        dimension_numbers=("NHWC", "HWIO", "NHWC"),
        preferred_element_type=F32,
    )


def encode(blocks, counts, stem_weight, conv_first, conv_second):
    steps, side, _, pdim = blocks.shape
    channels = stem_weight.shape[1]
    hidden = jnp.dot(blocks.reshape(-1, pdim), stem_weight, preferred_element_type=F32)
    hidden = jax.nn.relu(hidden).astype(BF).reshape(steps, side, side, channels)
    for layer in range(conv_first.shape[0]):
        wide = hidden.astype(F32)
        normed = wide * lax.rsqrt(jnp.mean(wide * wide, axis=-1, keepdims=True) + 1e-05)
        activated = jax.nn.relu(normed).astype(BF)
        middle = jax.nn.relu(conv(activated, conv_first[layer])).astype(BF)
        hidden = (wide + conv(middle, conv_second[layer])).astype(BF)
    latents = jnp.where((counts > 0)[:, None, None, None], hidden, jnp.zeros_like(hidden))
    pooled = jnp.mean(latents.astype(F32), axis=(1, 2))
    return latents, pooled


def head_kernel(
    steps,
    counts_ref,
    ends_ref,
    rewards_ref,
    ratios_ref,
    pooled_ref,
    stored_ref,
    head_ref,
    discounts_ref,
    lambdas_ref,
    values_ref,
    send_ref,
    chain_ref,
):
    fresh = jnp.dot(
        pooled_ref[...],
        head_ref[...].astype(F32),
        precision=lax.Precision.HIGHEST,
        preferred_element_type=F32,
    )
    discount = discounts_ref[...]
    trace = lambdas_ref[...]
    rows = []
    for t in range(steps):
        live = jnp.full((1, fresh.shape[1]), counts_ref[0, t], jnp.int32) > 0
        rows.append(jnp.where(live, fresh[t : t + 1], stored_ref[t : t + 1]))
        values_ref[t : t + 1] = rows[t]
    add = jnp.zeros_like(discount)
    mul = jnp.ones_like(discount)
    last = jnp.zeros_like(discount)
    for t in range(steps - 1, -1, -1):
        going = 1.0 - ends_ref[0, t].astype(F32)
        cut = jnp.minimum(1.0, ratios_ref[0, t])
        weight = discount * going * (1.0 - trace * cut)
        step_mul = discount * trace * cut * going
        reward = rewards_ref[0, t]
        if t == steps - 1:
            add = reward + step_mul * add
            last = weight
        else:
            add = reward + weight * rows[t + 1] + step_mul * add
            last = step_mul * last
        mul = step_mul * mul
        chain_ref[t : t + 1] = add
        chain_ref[steps + t : steps + t + 1] = mul
        chain_ref[2 * steps + t : 2 * steps + t + 1] = last
    shards = send_ref.shape[0]
    width = discount.shape[1]
    for place, row in enumerate((add, mul, last, rows[0])):
        send_ref[:, place : place + 1, :] = jnp.broadcast_to(row[None], (shards, 1, width))


def target_kernel(
    steps,
    here_ref,
    valid_ref,
    counts_ref,
    dests_ref,
    chain_ref,
    got_ref,
    targets_ref,
    load_ref,
):
    group, shard = here_ref[0], here_ref[1]
    shards = got_ref.shape[0]
    width = chain_ref.shape[1]
    zero = jnp.zeros((1, width), F32)

    carry, first = zero, zero
    kept_carry, kept_first = zero, zero
    for s in range(shards - 1, -1, -1):
        carry = got_ref[s, 0:1] + got_ref[s, 1:2] * carry + got_ref[s, 2:3] * first
        first = got_ref[s, 3:4]
        follows = jnp.full((1, width), shard + 1, jnp.int32) == s
        kept_carry = jnp.where(follows, carry, kept_carry)
        kept_first = jnp.where(follows, first, kept_first)
    for t in range(steps):
        total = (
            chain_ref[t : t + 1]
            + chain_ref[steps + t : steps + t + 1] * kept_carry
            + chain_ref[2 * steps + t : 2 * steps + t + 1] * kept_first
        )
        targets_ref[t : t + 1] = valid_ref[0, t].astype(F32) * total
    load = jnp.int32(0)
    for g in range(counts_ref.shape[0]):
        for t in range(steps):
            count = counts_ref[g, t]
            hit = jnp.logical_and(count > 0, dests_ref[g, t] == group)
            load = load + jnp.where(hit, count, 0)
    load_ref[0, 0] = load


def per_device(
    frames,
    sample_counts,
    dest_groups,
    episode_ends,
    valid_steps,
    rewards,
    ratios,
    stored_values,
    stem_weight,
    conv_first,
    conv_second,
    value_weight,
    discounts,
    lambdas,
):
    steps = frames.shape[1]
    shards = lax.axis_size("tm")
    heads = value_weight.shape[1]
    here = jnp.stack([lax.axis_index("grp"), lax.axis_index("tm")]).astype(jnp.int32)
    all_counts = lax.all_gather(sample_counts, "grp", axis=0, tiled=True)
    all_dests = lax.all_gather(dest_groups, "grp", axis=0, tiled=True)
    latents, pooled = encode(frames[0], sample_counts[0], stem_weight, conv_first, conv_second)
    smem = pl.BlockSpec(memory_space=pltpu.SMEM)
    vmem = pl.BlockSpec(memory_space=pltpu.VMEM)
    values, send, chain = pl.pallas_call(
        lambda *refs: head_kernel(steps, *refs),
        out_shape=(
            jax.ShapeDtypeStruct((steps, heads), F32),
            jax.ShapeDtypeStruct((shards, 4, heads), F32),
            jax.ShapeDtypeStruct((3 * steps, heads), F32),
        ),
        in_specs=[smem] * 4 + [vmem] * 5,
        out_specs=(vmem, vmem, vmem),
    )(
        sample_counts,
        episode_ends,
        rewards,
        ratios,
        pooled,
        stored_values[0],
        value_weight,
        discounts[None],
        lambdas[None],
    )
    got = lax.all_to_all(send, "tm", split_axis=0, concat_axis=0, tiled=True)
    targets, load = pl.pallas_call(
        lambda *refs: target_kernel(steps, *refs),
        out_shape=(
            jax.ShapeDtypeStruct((steps, heads), F32),
            jax.ShapeDtypeStruct((1, 1), jnp.int32),
        ),
        in_specs=[smem] * 4 + [vmem] * 2,
        out_specs=(vmem, smem),
    )(here, valid_steps, all_counts, all_dests, chain, got)
    return latents[None], values[None], targets[None], load


def solution(mesh):
    rows = P("grp", "tm")
    deep = P("grp", "tm", None)
    whole = P("grp", "tm", None, None, None)
    in_specs = (whole,) + (rows,) * 6 + (deep,) + (P(),) * 6
    out_specs = (whole, deep, deep, rows)
    return jax.shard_map(
        per_device, mesh=mesh, in_specs=in_specs, out_specs=out_specs, check_vma=False
    )
```

time: 344 us -> 79.5 us (0.23)
  the two profiles are of different devices: /device:TPU:7 before, /device:TPU:34 now
where the time goes in v1:
time: 79.5 us; the launch traced here: 79.2 us
  matrix products  38.6 us (49%)
  blocking collectives  18.6 us (23%)
  local copies, waits for them, and re-layouts  8.94 us (11%)
  starting transfers between devices  7.62 us (10%)
  Pallas kernels  3.29 us (4%)
  other arithmetic  1.24 us (2%)
  between operations  0.88 us (1%)
    conv_general_dilated x2, matrix products, conv(): lax.conv_general_dilated(x, w.reshape(3, 3, w.shape[1], w.shape[2]), (1,...  30.8 us
    all_gather x1, blocking collectives, per_device(): all_dests = lax.all_gather(dest_groups, 'grp', axis=0, tiled=True)  10.5 us
    all_gather x1, blocking collectives, per_device(): all_counts = lax.all_gather(sample_counts, 'grp', axis=0, tiled=True)  8.17 us
    dot_general x1, matrix products, encode(): jnp.dot(blocks.reshape(-1, pdim), stem_weight, preferred_element_type=F32)  7.81 us
    all_to_all x1, starting transfers between devices, per_device(): got = lax.all_to_all(send, 'tm', split_axis=0, concat_axis=0, tiled=True)  7.62 us
    unnamed x13, local copies, waits for them, and re-layouts  2.35 us
    rsqrt x3, local copies, waits for them, and re-layouts, encode(): lax.rsqrt(jnp.mean(wide * wide, axis=-1, keepdims=True) + 1e-05)  1.96 us
    slice x1, local copies, waits for them, and re-layouts, encode(): hidden = (wide + conv(middle, conv_second[layer])).astype(BF)  1.93 us
  transfers between devices with their start and end apart: 1, of which 0 were waited for; matrix products, arithmetic and copies ran while one was open for 2% of the time, Pallas kernels for 0%

profile of v1, /device:TPU:34, one launch (start us, length us, event | category | flops | bytes accessed | tf_op | source)
XLA Modules:
  0.0 79.2 jit_solution(975685897782337468)
XLA Ops:
  0.6 0.0 copy-start
  0.6 0.0 copy-start.1
  0.7 1.9 %fusion.18 = (bf16[1,9,256,256]{3,2,1,0:T(8,128)(2,1)S(1)}, bf16[1,9,256,256]{3,2,1,0:T(8,128)(2,1)S(1)}) fusion(bf16[2,9,256,256]{3,2,1,0:T(8,128)(2,1)} %param.24), kind=kLoop, calls=%fused_computation.29 | loop fusion | bytes 4718592 | tf_op jit(solution)/shard_map/slice | solution.py:33
  2.6 0.5 copy-done.1
  3.1 1.6 %fusion.17 = (bf16[1,9,256,256]{3,2,1,0:T(8,128)(2,1)}, bf16[1,9,256,256]{3,2,1,0:T(8,128)(2,1)}) fusion(bf16[2,9,256,256]{3,2,1,0:T(8,128)(2,1)S(1)} %copy-done.1), kind=kLoop, calls=%fused_computation.28 | loop fusion | bytes 4718592 | tf_op jit(solution)/shard_map/slice | solution.py:32
  4.7 0.0 copy-done
  4.7 7.8 %multiply_reduce_fusion = (f32[2304]{0:T(1024)S(1)}, f32[2304,256]{1,0:T(8,128)}) fusion(bf16[2304,2048]{1,0:T(8,128)(2,1)} %bitcast.38, bf16[2048,256]{1,0:T(8,128)(2,1)S(1)} %copy-done), kind=kOutput, calls=%fused_computation.15 | convolution fusion | flops 2418865920 | bytes 12854272 | tf_op jit(solution)/shard_map/dot_general | solution.py:26
  12.5 0.1 rsqrt.20
  12.6 0.9 %copy.34 = f32[4,24,24]{0,2,1:T(8,128)} copy(f32[4,24,24]{2,1,0:T(8,128)S(1)} %rsqrt.20) | data formatting | bytes 18432 | tf_op jit(solution)/shard_map/rsqrt | solution.py:30
  13.5 0.0 copy-start.3
  13.5 18.3 %fusion.2 = (f32[4,24,24]{0,2,1:T(8,128)}, bf16[4,24,24,256]{3,0,2,1:T(4,128)(2,1)}) fusion(bf16[3,3,256,256]{3,2,1,0:T(8,128)(2,1)S(1)} %bitcast.29, bf16[3,3,256,256]{3,2,1,0:T(8,128)(2,1)} %bitcast.30, f32[4,24,24,256]{3,2,1,0:T(8,128)} %bitcast.41, f32[4,24,24]{0,2,1:T(8,128)} %copy.34), kind=kOutput, calls=%fused_computation.6 | convolution fusion | flops 5143918592 | bytes 5916672 | tf_op jit(solution)/shard_map/conv_general_dilated | solution.py:13
  31.9 1.1 %copy.37 = f32[4,24,24]{2,1,0:T(8,128)S(1)} copy(f32[4,24,24]{0,2,1:T(8,128)} %get-tuple-element.40) | data formatting | bytes 18432 | tf_op jit(solution)/shard_map/reduce_sum | solution.py:30
  33.1 0.9 %copy.38 = f32[4,24,24]{0,2,1:T(8,128)} copy(f32[4,24,24]{2,1,0:T(8,128)S(1)} %add_rsqrt_fusion) | data formatting | bytes 18432 | tf_op jit(solution)/shard_map/rsqrt | solution.py:30
  34.0 0.0 copy-done.3
  34.0 12.4 %convert_reduce_fusion = (f32[4,256]{1,0:T(4,128)S(1)}, bf16[4,24,24,256]{3,0,2,1:T(4,128)(2,1)S(1)}) fusion(bf16[3,3,256,256]{3,2,1,0:T(8,128)(2,1)S(1)} %bitcast.27, bf16[3,3,256,256]{3,2,1,0:T(8,128)(2,1)} %bitcast.28, bf16[4,24,24,256]{3,0,2,1:T(4,128)(2,1)} %get-tuple-element.41, f32[4,24,24]{0,2,1:T(8,128)} %copy.38, ...), kind=kOutput, calls=%fused_computation.10 | convolution fusion | flops 5145099264 | bytes 4731908 | tf_op jit(solution)/shard_map/conv_general_dilated | solution.py:13
  46.4 0.0 copy-start.4
  46.4 0.0 copy-start.5
  46.5 0.6 broadcast_multiply_fusion.refs_4_
  47.0 1.7 %shard_map.165 = (f32[4,128]{1,0:T(4,128)}, f32[32,4,128]{2,1,0:T(4,128)}, f32[12,128]{1,0:T(8,128)}) custom-call(s32[1,4]{1,0:T(1,128)} %refs_0_.1, s32[1,4]{1,0:T(1,128)} %refs_1_.2, f32[1,4]{1,0:T(1,128)} %refs_2_.1, f32[1,4]{1,0:T(1,128)} %refs_3_.1, f32[4,256]{1,0:T(4,128)} %broadcast_multiply_fusion.refs_4_, f32[4,128]{1,0:T(4,128)} %bitcast.34, ...), custom_call_target="tpu_custom_call" | custom-call | tf_op jit(solution)/shard_map/pallas_call | solution.py:157
  48.8 7.6 %all-to-all-start = ((f32[32,4,128]{2,1,0:T(4,128)}), f32[32,4,128]{2,1,0:T(4,128)S(1)}, u32[]{:S(2)}, u32[]{:S(2)}) async-start(f32[32,4,128]{2,1,0:T(4,128)} %get-tuple-element.11), calls=%async_computation | async-start | bytes 131072 | tf_op jit(solution)/shard_map/all_to_all | solution.py:177
  56.4 1.2 %copy.39 = bf16[1,4,24,24,256]{4,3,2,1,0:T(8,128)(2,1)} copy(bf16[1,4,24,24,256]{4,1,3,2,0:T(4,128)(2,1)S(1)} %bitcast.26) | data formatting | bytes 2359296
  57.6 0.0 copy-done.4
  57.6 8.2 %all-gather = s32[4,1,4]{2,1,0:T(1,128)} all-gather(s32[1,1,4]{2,1,0:T(1,128)S(1)} %bitcast.33), channel_id=1, replica_groups=mesh['grp'=4,'tm'=32] {'grp'}, dimensions={0}, use_global_device_ids=true | all-gather | bytes 80 | tf_op jit(solution)/shard_map/all_gather | solution.py:152
  65.8 0.0 copy-done.5
  65.8 10.5 %all-gather.1 = s32[4,1,4]{2,1,0:T(1,128)} all-gather(s32[1,1,4]{2,1,0:T(1,128)S(1)} %bitcast.37), channel_id=1, replica_groups=mesh['grp'=4,'tm'=32] {'grp'}, dimensions={0}, use_global_device_ids=true | all-gather | bytes 80 | tf_op jit(solution)/shard_map/all_gather | solution.py:153
  76.2 0.6 pad_add_fusion.refs_0_
  76.8 0.0 all-to-all-done.refs_5_
  76.8 0.0 copy-start.2
  76.8 0.6 copy-done.2
  77.4 1.6 %shard_map.166 = (f32[4,128]{1,0:T(4,128)}, s32[1,1]{1,0:T(1,128)}) custom-call(s32[2]{0:T(128)} %pad_add_fusion.refs_0_, s32[1,4]{1,0:T(1,128)} %refs_1_.3, s32[4,4]{1,0:T(4,128)} %bitcast.31, s32[4,4]{1,0:T(4,128)} %bitcast.32, f32[12,128]{1,0:T(8,128)} %get-tuple-element.10.refs_4_, f32[32,4,128]{2,1,0:T(4,128)} %copy-done.2), custom_call_target="tpu_custom_call" | custom-call | tf_op jit(solution)/shard_map/pallas_call | solution.py:178
  (3 shorter events, 0.1 us)
Async XLA Ops:
  0.6 4.0 %copy-start = (bf16[2048,256]{1,0:T(8,128)(2,1)S(1)}, bf16[2048,256]{1,0:T(8,128)(2,1)}, u32[]{:S(2)}) copy-start(bf16[2048,256]{1,0:T(8,128)(2,1)} %param.22) | copy-start | bytes 3145732
  0.6 2.5 %copy-start.1 = (bf16[2,9,256,256]{3,2,1,0:T(8,128)(2,1)S(1)}, bf16[2,9,256,256]{3,2,1,0:T(8,128)(2,1)}, u32[]{:S(2)}) copy-start(bf16[2,9,256,256]{3,2,1,0:T(8,128)(2,1)} %param.23) | copy-start | bytes 7077892
  13.5 20.5 %copy-start.3 = (s32[1,4]{1,0:T(1,128)S(1)}, s32[1,4]{1,0:T(1,128)}, u32[]{:S(2)}) copy-start(s32[1,4]{1,0:T(1,128)} %refs_0_.1) | copy-start | bytes 52
  46.4 11.2 %copy-start.4 = (s32[1,4]{1,0:T(1,128)S(1)}, s32[1,4]{1,0:T(1,128)}, u32[]{:S(2)}) copy-start(s32[1,4]{1,0:T(1,128)} %refs_0_.1) | copy-start | bytes 52
  46.4 19.3 %copy-start.5 = (s32[1,4]{1,0:T(1,128)S(1)}, s32[1,4]{1,0:T(1,128)}, u32[]{:S(2)}) copy-start(s32[1,4]{1,0:T(1,128)} %param.16) | copy-start | bytes 52
  48.8 28.0 %all-to-all-start = ((f32[32,4,128]{2,1,0:T(4,128)}), f32[32,4,128]{2,1,0:T(4,128)S(1)}, u32[]{:S(2)}, u32[]{:S(2)}) async-start(f32[32,4,128]{2,1,0:T(4,128)} %get-tuple-element.11), calls=%async_computation | async-start | bytes 131072 | tf_op jit(solution)/shard_map/all_to_all | solution.py:177
  76.8 0.6 copy-start.2

commit v2 on v1

--- a/solution.py
+++ b/solution.py
@@ -1,3 +1,5 @@
+import functools
+
 import jax
 import jax.numpy as jnp
 from jax import lax
@@ -7,52 +9,192 @@
 
 BF = jnp.bfloat16
 F32 = jnp.float32
-
-
-def conv(x, w):
-    return lax.conv_general_dilated(
-        x,
-        w.reshape(3, 3, w.shape[1], w.shape[2]),
-        (1, 1),
-        "SAME",
-        dimension_numbers=("NHWC", "HWIO", "NHWC"),
-        preferred_element_type=F32,
-    )
-
-
-def encode(blocks, counts, stem_weight, conv_first, conv_second):
-    steps, side, _, pdim = blocks.shape
-    channels = stem_weight.shape[1]
-    hidden = jnp.dot(blocks.reshape(-1, pdim), stem_weight, preferred_element_type=F32)
-    hidden = jax.nn.relu(hidden).astype(BF).reshape(steps, side, side, channels)
-    for layer in range(conv_first.shape[0]):
-        wide = hidden.astype(F32)
-        normed = wide * lax.rsqrt(jnp.mean(wide * wide, axis=-1, keepdims=True) + 1e-05)
-        activated = jax.nn.relu(normed).astype(BF)
-        middle = jax.nn.relu(conv(activated, conv_first[layer])).astype(BF)
-        hidden = (wide + conv(middle, conv_second[layer])).astype(BF)
-    latents = jnp.where((counts > 0)[:, None, None, None], hidden, jnp.zeros_like(hidden))
-    pooled = jnp.mean(latents.astype(F32), axis=(1, 2))
-    return latents, pooled
-
-
-def head_kernel(
-    steps,
+LANE = 8
+TAPS = 9
+GRANT = 60 * 2**20
+
+
+def tile_order(flat_ref, side):
+    half, third = side // 2, side // LANE
+    tiles = []
+    for y in range(half):
+        for j in range(third):
+            for h in range(2):
+                start = side * (half * h + y) + j
+                rows = pl.ds(start, LANE, stride=third)
+                parts = [flat_ref[c, rows, :] for c in range(flat_ref.shape[0])]
+                tiles.append(jnp.concatenate(parts, axis=1))
+    return jnp.stack(tiles).reshape(half, third, 2, LANE, -1)
+
+
+def put_padded(out_ref, b, tiles):
+    half, third, _, _, width = tiles.shape
+    place = lax.broadcasted_iota(jnp.int32, (half * 2, LANE, width), 1)
+    before = pltpu.roll(tiles[:, third - 1].reshape(half * 2, LANE, width), 1, 1)
+    before = jnp.where(place == 0, 0.0, before).reshape(half, 1, 2, LANE, width)
+    after = pltpu.roll(tiles[:, 0].reshape(half * 2, LANE, width), LANE - 1, 1)
+    after = jnp.where(place == LANE - 1, 0.0, after).reshape(half, 1, 2, LANE, width)
+    wide = jnp.concatenate([before, tiles, after], axis=1)
+    rows = wide.reshape(half, third + 2, 2 * LANE, width).astype(BF)
+    out_ref[b, 1 : half + 1] = rows
+    none = jnp.zeros((third + 2, 1, LANE, width), F32)
+    top = jnp.concatenate([none, wide[half - 1, :, 0:1]], axis=1)
+    out_ref[b, 0] = top.reshape(third + 2, 2 * LANE, width).astype(BF)
+    bottom = jnp.concatenate([wide[0, :, 1:2], none], axis=1)
+    out_ref[b, half + 1] = bottom.reshape(third + 2, 2 * LANE, width).astype(BF)
+
+
+def normed(hidden):
+    wide = hidden.astype(F32)
+    scale = lax.rsqrt(jnp.mean(wide * wide, axis=-1, keepdims=True) + 1e-05)
+    return jnp.maximum(wide * scale, 0.0)
+
+
+def conv(src_ref, b, weight_ref):
+    _, tall, broad, rows, width = src_ref.shape
+    half, third = tall - 2, broad - 2
+    total = None
+    for tap in range(TAPS):
+        dy, dx = tap // 3, tap % 3
+        window = src_ref[b, dy : dy + half, dx : dx + third].reshape(half * third * rows, width)
+        part = jnp.dot(window, weight_ref[tap], preferred_element_type=F32)
+        total = part if total is None else total + part
+    return total.reshape(half, third, 2, LANE, weight_ref.shape[2])
+
+
+def window_rows(side):
+    half, third = side // 2, side // LANE
+    shape = (2 * LANE, side * side)
+    tap = lax.broadcasted_iota(jnp.int32, shape, 0)
+    at = lax.broadcasted_iota(jnp.int32, shape, 1)
+    s = at % LANE
+    h = (at // LANE) % 2
+    j = (at // (2 * LANE)) % third
+    y = at // (2 * LANE * third) + half * h
+    x = s * third + j
+    dy, dx = tap // 3 - 1, tap % 3 - 1
+    out = ((dy == -1) & (y == side - 1)) | ((dy == 1) & (y == 0))
+    out = out | ((dx == -1) & (x == side - 1)) | ((dx == 1) & (x == 0))
+    inside = (tap == TAPS) | ((tap < TAPS) & jnp.logical_not(out))
+    return jnp.where(inside, 1.0, 0.0).astype(BF)
+
+
+def front_kernel(
+    side,
+    counts_hbm,
+    ends_hbm,
+    rewards_hbm,
+    ratios_hbm,
+    frames_hbm,
+    stored_hbm,
+    stem_hbm,
+    first_hbm,
+    second_hbm,
+    head_hbm,
+    discounts_hbm,
+    lambdas_hbm,
+    middle_hbm,
+    hidden_hbm,
+    values_ref,
+    send_ref,
+    chain_ref,
+    frames,
+    stem,
+    weights,
+    flat,
+    hidden,
+    act,
+    mid,
     counts_ref,
     ends_ref,
     rewards_ref,
     ratios_ref,
-    pooled_ref,
     stored_ref,
     head_ref,
     discounts_ref,
     lambdas_ref,
-    values_ref,
-    send_ref,
-    chain_ref,
+    sems,
 ):
+    steps = frames.shape[0]
+    half = side // 2
+    sem = iter(range(64))
+
+    def load(src, dst):
+        copy = pltpu.make_async_copy(src, dst, sems.at[next(sem)])
+        copy.start()
+        return copy
+
+    stem_copy = load(stem_hbm, stem)
+    frame_copies = [load(frames_hbm.at[b], frames.at[b]) for b in range(steps)]
+    weight_copies = [
+        load(src, weights.at[i])
+        for i, src in enumerate((first_hbm.at[0], second_hbm.at[0], first_hbm.at[1], second_hbm.at[1]))
+    ]
+    small = [
+        load(src, dst)
+        for src, dst in (
+            (counts_hbm, counts_ref),
+            (ends_hbm, ends_ref),
+            (rewards_hbm, rewards_ref),
+            (ratios_hbm, ratios_ref),
+            (stored_hbm, stored_ref),
+            (head_hbm, head_ref),
+            (discounts_hbm, discounts_ref),
+            (lambdas_hbm, lambdas_ref),
+        )
+    ]
+    stem_copy.wait()
+    for b in range(steps):
+        frame_copies[b].wait()
+        rows = jnp.maximum(jnp.dot(frames[b], stem[...], preferred_element_type=F32), 0.0)
+        for c in range(flat.shape[1]):
+            flat[b, c] = rows[:, 128 * c : 128 * c + 128]
+        start = tile_order(flat.at[b], side).astype(BF)
+        hidden[b] = start.reshape(hidden.shape[1:])
+        put_padded(act, b, normed(start))
+    weight_copies[0].wait()
+    for b in range(steps):
+        put_padded(mid, b, jnp.maximum(conv(act, b, weights.at[0]), 0.0))
+    weight_copies[1].wait()
+    for b in range(steps):
+        out = conv(mid, b, weights.at[1])
+        now = (hidden[b].astype(F32).reshape(out.shape) + out).astype(BF)
+        hidden[b] = now.reshape(hidden.shape[1:])
+        put_padded(act, b, normed(now))
+    out_copies = []
+    for b in range(steps):
+        out_copies.append(load(hidden.at[b], hidden_hbm.at[b]))
+    weight_copies[2].wait()
+    for b in range(steps):
+        put_padded(mid, b, jnp.maximum(conv(act, b, weights.at[2]), 0.0))
+        out_copies.append(load(mid.at[b], middle_hbm.at[b]))
+
+    select = window_rows(side)
+    width = hidden.shape[-1]
+    sums, kept = [], []
+    for b in range(steps):
+        block = mid[b, 1 : half + 1, 1 : mid.shape[2] - 1].reshape(side * side, width)
+        sums.append(jnp.dot(select, block, preferred_element_type=F32))
+        rows = hidden[b].reshape(side * side, width)
+        kept.append(jnp.dot(select, rows, preferred_element_type=F32)[TAPS : TAPS + 1])
+    weight_copies[3].wait()
+    pooled = None
+    for tap in range(TAPS):
+        exact = jnp.concatenate([block[tap : tap + 1] for block in sums], axis=0)
+        parts, rest = [], exact
+        for _ in range(3):
+            part = rest.astype(BF)
+            parts.append(part.astype(F32))
+            rest = rest - part.astype(F32)
+        stacked = jnp.concatenate(parts + [jnp.zeros_like(exact)], axis=0).astype(BF)
+        term = jnp.dot(stacked, weights[3, tap], preferred_element_type=F32)
+        pooled = term if pooled is None else pooled + term
+    pooled = pooled[0:steps] + pooled[steps : 2 * steps] + pooled[2 * steps : 3 * steps]
+    pooled = (pooled + jnp.concatenate(kept, axis=0)) * (1.0 / (side * side))
+    for copy in small:
+        copy.wait()
     fresh = jnp.dot(
-        pooled_ref[...],
+        pooled,
         head_ref[...].astype(F32),
         precision=lax.Precision.HIGHEST,
         preferred_element_type=F32,
@@ -84,9 +226,119 @@
         chain_ref[steps + t : steps + t + 1] = mul
         chain_ref[2 * steps + t : 2 * steps + t + 1] = last
     shards = send_ref.shape[0]
-    width = discount.shape[1]
     for place, row in enumerate((add, mul, last, rows[0])):
-        send_ref[:, place : place + 1, :] = jnp.broadcast_to(row[None], (shards, 1, width))
+        send_ref[:, place : place + 1, :] = jnp.broadcast_to(row[None], (shards, 1, row.shape[1]))
+    for copy in out_copies:
+        copy.wait()
+
+
+def back_kernel(side, counts_ref, middle_hbm, hidden_hbm, second_hbm, out_hbm, mid, hidden, weight, flat, done, sems):
+    steps = mid.shape[0]
+    half, third = side // 2, side // LANE
+    copies = []
+
+    def load(i, src, dst):
+        copy = pltpu.make_async_copy(src, dst, sems.at[i])
+        copy.start()
+        return copy
+
+    weight_copy = load(0, second_hbm.at[1], weight)
+    for b in range(steps):
+        copies.append(
+            (
+                load(1 + 3 * b, middle_hbm.at[b], mid.at[b]),
+                load(2 + 3 * b, hidden_hbm.at[b], hidden.at[b]),
+            )
+        )
+    weight_copy.wait()
+    outs = []
+    for b in range(steps):
+        for copy in copies[b]:
+            copy.wait()
+        out = conv(mid, b, weight)
+        out = hidden[b].astype(F32).reshape(out.shape) + out
+        out = jnp.where(counts_ref[0, b] > 0, out, jnp.zeros_like(out))
+        for y in range(half):
+            for j in range(third):
+                for h in range(2):
+                    start = side * (half * h + y) + j
+                    for c in range(flat.shape[1]):
+                        flat[b, c, pl.ds(start, LANE, stride=third), :] = out[y, j, h, :, 128 * c : 128 * c + 128]
+        for c in range(flat.shape[1]):
+            done[b, :, 128 * c : 128 * c + 128] = flat[b, c].astype(BF)
+        outs.append(load(3 + 3 * b, done.at[b], out_hbm.at[b]))
+    for copy in outs:
+        copy.wait()
+
+
+SMEM = pl.BlockSpec(memory_space=pltpu.SMEM)
+VMEM = pl.BlockSpec(memory_space=pltpu.VMEM)
+HBM = pl.BlockSpec(memory_space=pl.ANY)
+
+
+def front(counts, ends, rewards, ratios, frames, stored, stem, first, second, head, discounts, lambdas, shards):
+    steps, side, _, pdim = frames.shape
+    width, heads = stem.shape[1], head.shape[1]
+    half, third = side // 2, side // LANE
+    padded = (steps, half + 2, third + 2, 2 * LANE, width)
+    plain = (steps, half, third, 2 * LANE, width)
+    area = side * side
+    work = steps * area * 2 * width * (pdim + 3 * TAPS * width)
+    return pl.pallas_call(
+        functools.partial(front_kernel, side),
+        out_shape=(
+            jax.ShapeDtypeStruct(padded, BF),
+            jax.ShapeDtypeStruct(plain, BF),
+            jax.ShapeDtypeStruct((steps, heads), F32),
+            jax.ShapeDtypeStruct((shards, 4, heads), F32),
+            jax.ShapeDtypeStruct((3 * steps, heads), F32),
+        ),
+        in_specs=[HBM] * 12,
+        out_specs=(HBM, HBM, VMEM, VMEM, VMEM),
+        scratch_shapes=[
+            pltpu.VMEM((steps, area, pdim), BF),
+            pltpu.VMEM(stem.shape, BF),
+            pltpu.VMEM((4, TAPS, width, width), BF),
+            pltpu.VMEM((steps, width // 128, area, 128), F32),
+            pltpu.VMEM(plain, BF),
+            pltpu.VMEM(padded, BF),
+            pltpu.VMEM(padded, BF),
+            pltpu.SMEM(counts.shape, jnp.int32),
+            pltpu.SMEM(ends.shape, jnp.int32),
+            pltpu.SMEM(rewards.shape, F32),
+            pltpu.SMEM(ratios.shape, F32),
+            pltpu.VMEM(stored.shape, F32),
+            pltpu.VMEM(head.shape, BF),
+            pltpu.VMEM(discounts.shape, F32),
+            pltpu.VMEM(lambdas.shape, F32),
+            pltpu.SemaphoreType.DMA((32,)),
+        ],
+        compiler_params=pltpu.CompilerParams(vmem_limit_bytes=GRANT),
+        cost_estimate=pl.CostEstimate(flops=work, bytes_accessed=16 * 10**6, transcendentals=0),
+    )(counts, ends, rewards, ratios, frames.reshape(steps, area, pdim), stored, stem, first, second, head, discounts, lambdas)
+
+
+def back(counts, middle, hidden, second, side):
+    steps, width = middle.shape[0], middle.shape[-1]
+    area = side * side
+    return pl.pallas_call(
+        functools.partial(back_kernel, side),
+        out_shape=jax.ShapeDtypeStruct((steps, area, width), BF),
+        in_specs=[SMEM, HBM, HBM, HBM],
+        out_specs=HBM,
+        scratch_shapes=[
+            pltpu.VMEM(middle.shape, BF),
+            pltpu.VMEM(hidden.shape, BF),
+            pltpu.VMEM((TAPS, width, width), BF),
+            pltpu.VMEM((steps, width // 128, area, 128), F32),
+            pltpu.VMEM((steps, area, width), BF),
+            pltpu.SemaphoreType.DMA((32,)),
+        ],
+        compiler_params=pltpu.CompilerParams(vmem_limit_bytes=GRANT),
+        cost_estimate=pl.CostEstimate(
+            flops=steps * area * 2 * width * TAPS * width, bytes_accessed=8 * 10**6, transcendentals=0
+        ),
+    )(counts, middle, hidden, second)
 
 
 def target_kernel(
@@ -145,46 +397,41 @@
     discounts,
     lambdas,
 ):
-    steps = frames.shape[1]
+    steps, side = frames.shape[1], frames.shape[2]
+    width = stem_weight.shape[1]
+    heads = value_weight.shape[1]
     shards = lax.axis_size("tm")
-    heads = value_weight.shape[1]
     here = jnp.stack([lax.axis_index("grp"), lax.axis_index("tm")]).astype(jnp.int32)
     all_counts = lax.all_gather(sample_counts, "grp", axis=0, tiled=True)
     all_dests = lax.all_gather(dest_groups, "grp", axis=0, tiled=True)
-    latents, pooled = encode(frames[0], sample_counts[0], stem_weight, conv_first, conv_second)
-    smem = pl.BlockSpec(memory_space=pltpu.SMEM)
-    vmem = pl.BlockSpec(memory_space=pltpu.VMEM)
-    values, send, chain = pl.pallas_call(
-        lambda *refs: head_kernel(steps, *refs),
-        out_shape=(
-            jax.ShapeDtypeStruct((steps, heads), F32),
-            jax.ShapeDtypeStruct((shards, 4, heads), F32),
-            jax.ShapeDtypeStruct((3 * steps, heads), F32),
-        ),
-        in_specs=[smem] * 4 + [vmem] * 5,
-        out_specs=(vmem, vmem, vmem),
-    )(
+    middle, hidden, values, send, chain = front(
         sample_counts,
         episode_ends,
         rewards,
         ratios,
-        pooled,
+        frames[0],
         stored_values[0],
+        stem_weight,
+        conv_first,
+        conv_second,
         value_weight,
         discounts[None],
         lambdas[None],
+        shards,
     )
     got = lax.all_to_all(send, "tm", split_axis=0, concat_axis=0, tiled=True)
+    latents = back(sample_counts, middle, hidden, conv_second, side)
     targets, load = pl.pallas_call(
-        lambda *refs: target_kernel(steps, *refs),
+        functools.partial(target_kernel, steps),
         out_shape=(
             jax.ShapeDtypeStruct((steps, heads), F32),
             jax.ShapeDtypeStruct((1, 1), jnp.int32),
         ),
-        in_specs=[smem] * 4 + [vmem] * 2,
-        out_specs=(vmem, smem),
+        in_specs=[SMEM] * 4 + [VMEM] * 2,
+        out_specs=(VMEM, SMEM),
     )(here, valid_steps, all_counts, all_dests, chain, got)
-    return latents[None], values[None], targets[None], load
+    latents = latents.reshape(1, steps, side, side, width)
+    return latents, values[None], targets[None], load
 
 
 def solution(mesh):

time: 79.5 us -> 58.7 us (0.74)
  matrix products: 38.6 us -> 0 us
  Pallas kernels: 3.29 us -> 29.9 us
  local copies, waits for them, and re-layouts: 8.94 us -> 0.64 us
    conv_general_dilated x2 -> x0, matrix products: 30.8 us -> none  [conv(): lax.conv_general_dilated(x, w.reshape(3, 3, w.shape[1], w.shape[2]), (1,...]
    pallas_call x2 -> x3, Pallas kernels: 3.29 us -> 29.9 us  [the longest x1 19 us: front(): pl.pallas_call(functools.partial(front_kernel, side), out_shape=(jax.Shap...]
    dot_general x1 -> x0, matrix products: 7.81 us -> none  [encode(): jnp.dot(blocks.reshape(-1, pdim), stem_weight, preferred_element_type=F32)]
    slice x2 -> x0, local copies, waits for them, and re-layouts: 3.49 us -> none  [the longest x1 1.93 us: encode(): hidden = (wide + conv(middle, conv_second[layer])).astype(BF)]
    all_gather x1, blocking collectives: 8.17 us -> 10.2 us  [per_device(): all_counts = lax.all_gather(sample_counts, 'grp', axis=0, tiled=True)]
    rsqrt x3 -> x0, local copies, waits for them, and re-layouts: 1.96 us -> none  [encode(): lax.rsqrt(jnp.mean(wide * wide, axis=-1, keepdims=True) + 1e-05)]
    all_gather x1, blocking collectives: 10.5 us -> 8.65 us  [per_device(): all_dests = lax.all_gather(dest_groups, 'grp', axis=0, tiled=True)]
    unnamed x13 -> x6, local copies, waits for them, and re-layouts: 2.35 us -> 0.64 us
  transfers between devices with their start and end apart: 1 -> 1, of which waited for: 0 -> 0; matrix products, arithmetic and copies ran while one was open for 2% -> 1% of each run, Pallas kernels for 0% -> 16%
where the time goes in v2:
time: 58.7 us; the launch traced here: 58.5 us
  Pallas kernels  29.9 us (51%)
  blocking collectives  18.8 us (32%)
  starting transfers between devices  7.63 us (13%)
  between operations  0.85 us (1%)
  local copies, waits for them, and re-layouts  0.64 us (1%)
  other arithmetic  0.61 us (1%)
    pallas_call x1, Pallas kernels, front(): pl.pallas_call(functools.partial(front_kernel, side), out_shape=(jax.Shap...  19 us
    all_gather x1, blocking collectives, per_device(): all_counts = lax.all_gather(sample_counts, 'grp', axis=0, tiled=True)  10.2 us
    pallas_call x1, Pallas kernels, back(): pl.pallas_call(functools.partial(back_kernel, side), out_shape=jax.ShapeD...  9.32 us
    all_gather x1, blocking collectives, per_device(): all_dests = lax.all_gather(dest_groups, 'grp', axis=0, tiled=True)  8.65 us
    all_to_all x1, starting transfers between devices, per_device(): got = lax.all_to_all(send, 'tm', split_axis=0, concat_axis=0, tiled=True)  7.63 us
    pallas_call x1, Pallas kernels, per_device(): pl.pallas_call(functools.partial(target_kernel, steps), out_shape=(jax.Sh...  1.56 us
  transfers between devices with their start and end apart: 1, of which 0 were waited for; matrix products, arithmetic and copies ran while one was open for 1% of the time, Pallas kernels for 16%

profile of v2, /device:TPU:34, one launch (start us, length us, event | category | flops | bytes accessed | tf_op | source)
XLA Modules:
  0.0 58.5 jit_solution(8781443547809053993)
XLA Ops:
  0.6 0.0 copy-start.1
  0.6 0.0 copy-start.2
  0.7 19.0 %shard_map.165 = (bf16[4,14,5,16,256]{4,3,2,1,0:T(8,128)(2,1)}, bf16[4,12,3,16,256]{4,3,2,1,0:T(8,128)(2,1)}, f32[4,128]{1,0:T(4,128)}, f32[32,4,128]{2,1,0:T(4,128)}, f32[12,128]{1,0:T(8,128)}) custom-call(s32[1,4]{1,0:T(1,128)} %counts_ref.1, s32[1,4]{1,0:T(1,128)} %ends_hbm.1, f32[1,4]{1,0:T(1,128)} %rewards_hbm.1, f32[1,4]{1,0:T(1,128)} %ratios_hbm.1, ...), custom_call_target="tpu_custom_call" | custom-call | flops 10569646080 | bytes 16000000 | tf_op jit(solution)/shard_map/pallas_call | solution.py:287
  19.7 7.6 %all-to-all-start = ((f32[32,4,128]{2,1,0:T(4,128)}), f32[32,4,128]{2,1,0:T(4,128)S(1)}, u32[]{:S(2)}, u32[]{:S(2)}) async-start(f32[32,4,128]{2,1,0:T(4,128)} %get-tuple-element.15), calls=%async_computation | async-start | bytes 131072 | tf_op jit(solution)/shard_map/all_to_all | solution.py:422
  27.3 0.0 copy-done.1
  27.3 8.6 %all-gather.1 = s32[4,1,4]{2,1,0:T(1,128)} all-gather(s32[1,1,4]{2,1,0:T(1,128)S(1)} %bitcast.15), channel_id=1, replica_groups=mesh['grp'=4,'tm'=32] {'grp'}, dimensions={0}, use_global_device_ids=true | all-gather | bytes 80 | tf_op jit(solution)/shard_map/all_gather | solution.py:406
  36.0 0.0 copy-done.2
  36.0 10.2 %all-gather = s32[4,1,4]{2,1,0:T(1,128)} all-gather(s32[1,1,4]{2,1,0:T(1,128)S(1)} %bitcast.16), channel_id=1, replica_groups=mesh['grp'=4,'tm'=32] {'grp'}, dimensions={0}, use_global_device_ids=true | all-gather | bytes 80 | tf_op jit(solution)/shard_map/all_gather | solution.py:405
  46.2 9.3 %shard_map.166 = bf16[4,576,256]{2,1,0:T(8,128)(2,1)} custom-call(s32[1,4]{1,0:T(1,128)} %counts_ref.1, bf16[4,14,5,16,256]{4,3,2,1,0:T(8,128)(2,1)} %get-tuple-element.11.middle_hbm, bf16[4,12,3,16,256]{4,3,2,1,0:T(8,128)(2,1)} %get-tuple-element.12.hidden_hbm, bf16[2,9,256,256]{3,2,1,0:T(8,128)(2,1)} %second_hbm.3), custom_call_target="tpu_custom_call" | custom-call | flops 2717908992 | bytes 8000000 | tf_op jit(solution)/shard_map/pallas_call | solution.py:324
  55.5 0.6 %pad_add_fusion.here_ref = s32[2]{0:T(128)} fusion(s32[1]{0:T(128)} %bitcast.7, s32[1]{0:T(128)} %bitcast.6), kind=kLoop, calls=%fused_computation | loop fusion | flops 2 | bytes 16 | tf_op jit(solution)/shard_map/stack | solution.py:404
  56.1 0.0 all-to-all-done.got_ref
  56.1 0.0 copy-start
  56.1 0.6 %copy-done = f32[32,4,128]{2,1,0:T(4,128)} copy-done((f32[32,4,128]{2,1,0:T(4,128)}, f32[32,4,128]{2,1,0:T(4,128)S(1)}, u32[]{:S(2)}) %copy-start) | copy-done | bytes 65560
  56.8 1.6 %shard_map.167 = (f32[4,128]{1,0:T(4,128)}, s32[1,1]{1,0:T(1,128)}) custom-call(s32[2]{0:T(128)} %pad_add_fusion.here_ref, s32[1,4]{1,0:T(1,128)} %valid_ref.1, s32[4,4]{1,0:T(4,128)} %bitcast.14, s32[4,4]{1,0:T(4,128)} %bitcast.13, f32[12,128]{1,0:T(8,128)} %get-tuple-element.14.chain_ref, f32[32,4,128]{2,1,0:T(4,128)} %copy-done), custom_call_target="tpu_custom_call" | custom-call | tf_op jit(solution)/shard_map/pallas_call | solution.py:424
Async XLA Ops:
  0.6 26.7 %copy-start.1 = (s32[1,4]{1,0:T(1,128)S(1)}, s32[1,4]{1,0:T(1,128)}, u32[]{:S(2)}) copy-start(s32[1,4]{1,0:T(1,128)} %param.16) | copy-start | bytes 52
  0.6 35.4 %copy-start.2 = (s32[1,4]{1,0:T(1,128)S(1)}, s32[1,4]{1,0:T(1,128)}, u32[]{:S(2)}) copy-start(s32[1,4]{1,0:T(1,128)} %counts_ref.1) | copy-start | bytes 52
  19.7 36.4 %all-to-all-start = ((f32[32,4,128]{2,1,0:T(4,128)}), f32[32,4,128]{2,1,0:T(4,128)S(1)}, u32[]{:S(2)}, u32[]{:S(2)}) async-start(f32[32,4,128]{2,1,0:T(4,128)} %get-tuple-element.15), calls=%async_computation | async-start | bytes 131072 | tf_op jit(solution)/shard_map/all_to_all | solution.py:422
  56.1 0.6 %copy-start = (f32[32,4,128]{2,1,0:T(4,128)}, f32[32,4,128]{2,1,0:T(4,128)S(1)}, u32[]{:S(2)}) copy-start(f32[32,4,128]{2,1,0:T(4,128)S(1)} %all-to-all-done.got_ref) | copy-start | bytes 196612

commit v3 on v2

--- a/solution.py
+++ b/solution.py
@@ -125,11 +125,14 @@
         return copy
 
     stem_copy = load(stem_hbm, stem)
-    frame_copies = [load(frames_hbm.at[b], frames.at[b]) for b in range(steps)]
+    frame_copies = [pltpu.make_async_copy(frames_hbm.at[b], frames.at[b], sems.at[next(sem)]) for b in range(steps)]
     weight_copies = [
-        load(src, weights.at[i])
+        pltpu.make_async_copy(src, weights.at[i], sems.at[next(sem)])
         for i, src in enumerate((first_hbm.at[0], second_hbm.at[0], first_hbm.at[1], second_hbm.at[1]))
     ]
+    frame_copies[0].start()
+    weight_copies[0].start()
+    frame_copies[1].start()
     small = [
         load(src, dst)
         for src, dst in (
@@ -144,30 +147,61 @@
         )
     ]
     stem_copy.wait()
-    for b in range(steps):
-        frame_copies[b].wait()
+
+    def begin(b):
+        for c in range(steps):
+
+            @pl.when(b == c)
+            def _():
+                frame_copies[c].wait()
+                if c + 2 < steps:
+                    frame_copies[c + 2].start()
+                else:
+                    for i in range(c - 1, 2 * c - 2):
+                        weight_copies[i].start()
+
         rows = jnp.maximum(jnp.dot(frames[b], stem[...], preferred_element_type=F32), 0.0)
-        for c in range(flat.shape[1]):
-            flat[b, c] = rows[:, 128 * c : 128 * c + 128]
-        start = tile_order(flat.at[b], side).astype(BF)
+        for c in range(flat.shape[0]):
+            flat[c] = rows[:, 128 * c : 128 * c + 128]
+        start = tile_order(flat, side).astype(BF)
         hidden[b] = start.reshape(hidden.shape[1:])
         put_padded(act, b, normed(start))
-    weight_copies[0].wait()
-    for b in range(steps):
-        put_padded(mid, b, jnp.maximum(conv(act, b, weights.at[0]), 0.0))
-    weight_copies[1].wait()
-    for b in range(steps):
-        out = conv(mid, b, weights.at[1])
-        now = (hidden[b].astype(F32).reshape(out.shape) + out).astype(BF)
-        hidden[b] = now.reshape(hidden.shape[1:])
-        put_padded(act, b, normed(now))
-    out_copies = []
-    for b in range(steps):
-        out_copies.append(load(hidden.at[b], hidden_hbm.at[b]))
-    weight_copies[2].wait()
-    for b in range(steps):
-        put_padded(mid, b, jnp.maximum(conv(act, b, weights.at[2]), 0.0))
-        out_copies.append(load(mid.at[b], middle_hbm.at[b]))
+
+    def layer(l, _):
+        def first(b, _):
+            @pl.when(l == 0)
+            def _():
+                begin(b)
+
+            @pl.when((l == 0) & (b == 0))
+            def _():
+                weight_copies[0].wait()
+
+            @pl.when((l == 1) & (b == 0))
+            def _():
+                weight_copies[2].wait()
+
+            put_padded(mid, b, jnp.maximum(conv(act, b, weights.at[2 * l]), 0.0))
+            return 0
+
+        def second(b, _):
+            out = conv(mid, b, weights.at[1])
+            now = (hidden[b].astype(F32).reshape(out.shape) + out).astype(BF)
+            hidden[b] = now.reshape(hidden.shape[1:])
+            put_padded(act, b, normed(now))
+            return 0
+
+        lax.fori_loop(0, steps, first, 0)
+
+        @pl.when(l == 0)
+        def _():
+            weight_copies[1].wait()
+            lax.fori_loop(0, steps, second, 0)
+
+        return 0
+
+    lax.fori_loop(0, 2, layer, 0)
+    out_copies = [load(hidden, hidden_hbm), load(mid, middle_hbm)]
 
     select = window_rows(side)
     width = hidden.shape[-1]
@@ -251,10 +285,10 @@
             )
         )
     weight_copy.wait()
-    outs = []
-    for b in range(steps):
-        for copy in copies[b]:
-            copy.wait()
+
+    def finish(b, _):
+        pltpu.make_async_copy(middle_hbm.at[b], mid.at[b], sems.at[1 + 3 * b]).wait()
+        pltpu.make_async_copy(hidden_hbm.at[b], hidden.at[b], sems.at[2 + 3 * b]).wait()
         out = conv(mid, b, weight)
         out = hidden[b].astype(F32).reshape(out.shape) + out
         out = jnp.where(counts_ref[0, b] > 0, out, jnp.zeros_like(out))
@@ -262,13 +296,16 @@
             for j in range(third):
                 for h in range(2):
                     start = side * (half * h + y) + j
-                    for c in range(flat.shape[1]):
-                        flat[b, c, pl.ds(start, LANE, stride=third), :] = out[y, j, h, :, 128 * c : 128 * c + 128]
-        for c in range(flat.shape[1]):
-            done[b, :, 128 * c : 128 * c + 128] = flat[b, c].astype(BF)
-        outs.append(load(3 + 3 * b, done.at[b], out_hbm.at[b]))
-    for copy in outs:
-        copy.wait()
+                    for c in range(flat.shape[0]):
+                        flat[c, pl.ds(start, LANE, stride=third), :] = out[y, j, h, :, 128 * c : 128 * c + 128]
+        for c in range(flat.shape[0]):
+            done[b, :, 128 * c : 128 * c + 128] = flat[c].astype(BF)
+        pltpu.make_async_copy(done.at[b], out_hbm.at[b], sems.at[3 + 3 * b]).start()
+        return 0
+
+    lax.fori_loop(0, steps, finish, 0)
+    for b in range(steps):
+        pltpu.make_async_copy(done.at[b], out_hbm.at[b], sems.at[3 + 3 * b]).wait()
 
 
 SMEM = pl.BlockSpec(memory_space=pltpu.SMEM)
@@ -299,7 +336,7 @@
             pltpu.VMEM((steps, area, pdim), BF),
             pltpu.VMEM(stem.shape, BF),
             pltpu.VMEM((4, TAPS, width, width), BF),
-            pltpu.VMEM((steps, width // 128, area, 128), F32),
+            pltpu.VMEM((width // 128, area, 128), F32),
             pltpu.VMEM(plain, BF),
             pltpu.VMEM(padded, BF),
             pltpu.VMEM(padded, BF),
@@ -330,7 +367,7 @@
             pltpu.VMEM(middle.shape, BF),
             pltpu.VMEM(hidden.shape, BF),
             pltpu.VMEM((TAPS, width, width), BF),
-            pltpu.VMEM((steps, width // 128, area, 128), F32),
+            pltpu.VMEM((width // 128, area, 128), F32),
             pltpu.VMEM((steps, area, width), BF),
             pltpu.SemaphoreType.DMA((32,)),
         ],
@@ -341,22 +378,20 @@
     )(counts, middle, hidden, second)
 
 
-def target_kernel(
-    steps,
-    here_ref,
-    valid_ref,
-    counts_ref,
-    dests_ref,
-    chain_ref,
-    got_ref,
-    targets_ref,
-    load_ref,
-):
-    group, shard = here_ref[0], here_ref[1]
+def target_kernel(steps, valid_hbm, loads_hbm, chain_hbm, got_ref, targets_ref, load_ref, valid_ref, loads_ref, chain_ref, sems):
+    group, shard = lax.axis_index("grp"), lax.axis_index("tm")
     shards = got_ref.shape[0]
+    groups, part = loads_ref.shape[0], loads_hbm.shape[0] // loads_ref.shape[0]
     width = chain_ref.shape[1]
+    copies = [
+        pltpu.make_async_copy(valid_hbm, valid_ref, sems.at[0]),
+        pltpu.make_async_copy(chain_hbm, chain_ref, sems.at[1]),
+    ]
+    for g in range(groups):
+        copies.append(pltpu.make_async_copy(loads_hbm.at[g * part], loads_ref.at[g], sems.at[2 + g]))
+    for copy in copies:
+        copy.start()
     zero = jnp.zeros((1, width), F32)
-
     carry, first = zero, zero
     kept_carry, kept_first = zero, zero
     for s in range(shards - 1, -1, -1):
@@ -365,6 +400,8 @@
         follows = jnp.full((1, width), shard + 1, jnp.int32) == s
         kept_carry = jnp.where(follows, carry, kept_carry)
         kept_first = jnp.where(follows, first, kept_first)
+    for copy in copies:
+        copy.wait()
     for t in range(steps):
         total = (
             chain_ref[t : t + 1]
@@ -372,13 +409,10 @@
             + chain_ref[2 * steps + t : 2 * steps + t + 1] * kept_first
         )
         targets_ref[t : t + 1] = valid_ref[0, t].astype(F32) * total
-    load = jnp.int32(0)
-    for g in range(counts_ref.shape[0]):
-        for t in range(steps):
-            count = counts_ref[g, t]
-            hit = jnp.logical_and(count > 0, dests_ref[g, t] == group)
-            load = load + jnp.where(hit, count, 0)
-    load_ref[0, 0] = load
+    lane = lax.broadcasted_iota(jnp.int32, loads_ref.shape, 2)
+    mine = jnp.where(lane == group, loads_ref[...], 0).astype(F32)
+    mine = jnp.sum(jnp.sum(mine, axis=0), axis=0, keepdims=True)
+    load_ref[...] = jnp.sum(mine, axis=1, keepdims=True).astype(jnp.int32)
 
 
 def per_device(
@@ -400,10 +434,11 @@
     steps, side = frames.shape[1], frames.shape[2]
     width = stem_weight.shape[1]
     heads = value_weight.shape[1]
-    shards = lax.axis_size("tm")
-    here = jnp.stack([lax.axis_index("grp"), lax.axis_index("tm")]).astype(jnp.int32)
-    all_counts = lax.all_gather(sample_counts, "grp", axis=0, tiled=True)
-    all_dests = lax.all_gather(dest_groups, "grp", axis=0, tiled=True)
+    groups, shards = lax.axis_size("grp"), lax.axis_size("tm")
+    lanes = jnp.arange(128, dtype=jnp.int32)[None, :]
+    hits = jnp.where(dest_groups[0][:, None] == lanes, jnp.maximum(sample_counts[0], 0)[:, None], 0)
+    loads = lax.optimization_barrier(jnp.broadcast_to(hits[None], (128, steps, 128)))
+    loads = lax.all_gather(loads, "grp", axis=0, tiled=True)
     middle, hidden, values, send, chain = front(
         sample_counts,
         episode_ends,
@@ -427,9 +462,16 @@
             jax.ShapeDtypeStruct((steps, heads), F32),
             jax.ShapeDtypeStruct((1, 1), jnp.int32),
         ),
-        in_specs=[SMEM] * 4 + [VMEM] * 2,
-        out_specs=(VMEM, SMEM),
-    )(here, valid_steps, all_counts, all_dests, chain, got)
+        in_specs=[HBM, HBM, HBM, VMEM],
+        out_specs=(VMEM, VMEM),
+        scratch_shapes=[
+            pltpu.SMEM(valid_steps.shape, jnp.int32),
+            pltpu.VMEM((groups, steps, 128), jnp.int32),
+            pltpu.VMEM((3 * steps, heads), F32),
+            pltpu.SemaphoreType.DMA((2 + groups,)),
+        ],
+        compiler_params=pltpu.CompilerParams(vmem_limit_bytes=GRANT),
+    )(valid_steps, loads, chain, got)
     latents = latents.reshape(1, steps, side, side, width)
     return latents, values[None], targets[None], load
 

time: 58.7 us -> 54.6 us (0.930)
  the two profiles are of different devices: /device:TPU:34 before, /device:TPU:1 now
where the time goes in v3:
time: 54.6 us; the launch traced here: 54.3 us
  Pallas kernels  28.1 us (51%)
  between operations  14.1 us (26%)
  starting transfers between devices  8.66 us (16%)
  other arithmetic  1.38 us (3%)
  local copies, waits for them, and re-layouts  1.36 us (2%)
  waiting for transfers between devices  0.66 us (1%)
    pallas_call x1, Pallas kernels, front(): pl.pallas_call(functools.partial(front_kernel, side), out_shape=(jax.Shap...  19.3 us
    all_to_all x1, starting transfers between devices, per_device(): got = lax.all_to_all(send, 'tm', split_axis=0, concat_axis=0, tiled=True)  8.62 us
    pallas_call x1, Pallas kernels, back(): pl.pallas_call(functools.partial(back_kernel, side), out_shape=jax.ShapeD...  6.68 us
    pallas_call x1, Pallas kernels, per_device(): pl.pallas_call(functools.partial(target_kernel, steps), out_shape=(jax.Sh...  2.2 us
  transfers between devices with their start and end apart: 2, of which 1 were waited for; matrix products, arithmetic and copies ran while one was open for 0% of the time, Pallas kernels for 48%

profile of v3, /device:TPU:1, one launch (start us, length us, event | category | flops | bytes accessed | tf_op | source)
XLA Modules:
  0.0 54.3 jit_solution(18142218889498972855)
XLA Ops:
  7.2 0.0 all-gather.2.cloned.1.call-start
  7.2 0.7 %maximum_bitcast_fusion = s32[4]{0:T(128)S(1)} fusion(s32[1,4]{1,0:T(1,128)} %counts_ref.1), kind=kLoop, calls=%fused_computation.2 | loop fusion | flops 4 | bytes 32 | tf_op jit(solution)/shard_map/max | solution.py:439
  7.9 0.7 %fusion = s32[4,128]{1,0:T(4,128)S(1)} fusion(s32[4]{0:T(128)S(1)} %maximum_bitcast_fusion, s32[4]{0:T(128)} %bitcast.10), kind=kLoop, calls=%fused_computation.1 | loop fusion | flops 1024 | bytes 2080 | tf_op jit(solution)/shard_map/jit(_where)/select_n | solution.py:439
  8.6 0.7 %broadcast_in_dim.37 = s32[128,4,128]{2,1,0:T(4,128)} broadcast(s32[4,128]{1,0:T(4,128)S(1)} %fusion), dimensions={1,2} | broadcast | bytes 264192 | tf_op jit(solution)/shard_map/broadcast_in_dim | solution.py:440
  9.3 0.0 all-gather.2.cloned.1.call-update
  9.4 19.3 %shard_map.165 = (bf16[4,14,5,16,256]{4,3,2,1,0:T(8,128)(2,1)}, bf16[4,12,3,16,256]{4,3,2,1,0:T(8,128)(2,1)}, f32[4,128]{1,0:T(4,128)}, f32[32,4,128]{2,1,0:T(4,128)}, f32[12,128]{1,0:T(8,128)}) custom-call(s32[1,4]{1,0:T(1,128)} %counts_ref.1, s32[1,4]{1,0:T(1,128)} %ends_hbm.1, f32[1,4]{1,0:T(1,128)} %rewards_hbm.1, f32[1,4]{1,0:T(1,128)} %ratios_hbm.1, ...), custom_call_target="tpu_custom_call" | custom-call | flops 10569646080 | bytes 16000000 | tf_op jit(solution)/shard_map/pallas_call | solution.py:324
  28.6 8.6 %all-to-all-start = ((f32[32,4,128]{2,1,0:T(4,128)}), f32[32,4,128]{2,1,0:T(4,128)S(1)}, u32[]{:S(2)}, u32[]{:S(2)}) async-start(f32[32,4,128]{2,1,0:T(4,128)} %get-tuple-element.15), calls=%async_computation | async-start | bytes 131072 | tf_op jit(solution)/shard_map/all_to_all | solution.py:457
  37.3 6.7 %shard_map.166 = bf16[4,576,256]{2,1,0:T(8,128)(2,1)} custom-call(s32[1,4]{1,0:T(1,128)} %counts_ref.1, bf16[4,14,5,16,256]{4,3,2,1,0:T(8,128)(2,1)} %get-tuple-element.11.middle_hbm, bf16[4,12,3,16,256]{4,3,2,1,0:T(8,128)(2,1)} %get-tuple-element.12.hidden_hbm, bf16[2,9,256,256]{3,2,1,0:T(8,128)(2,1)} %second_hbm.3), custom_call_target="tpu_custom_call" | custom-call | flops 2717908992 | bytes 8000000 | tf_op jit(solution)/shard_map/pallas_call | solution.py:361
  43.9 0.6 %all-to-all-done.got_ref = f32[32,4,128]{2,1,0:T(4,128)S(1)} async-done(((f32[32,4,128]{2,1,0:T(4,128)}), f32[32,4,128]{2,1,0:T(4,128)S(1)}, u32[]{:S(2)}, u32[]{:S(2)}) %all-to-all-start) | async-done | bytes 65568 | tf_op jit(solution)/shard_map/all_to_all | solution.py:457
  44.6 0.0 copy-start
  44.6 0.0 all-gather.2.cloned.1.call-done.loads_hbm
  44.6 0.6 %copy-done = f32[32,4,128]{2,1,0:T(4,128)} copy-done((f32[32,4,128]{2,1,0:T(4,128)}, f32[32,4,128]{2,1,0:T(4,128)S(1)}, u32[]{:S(2)}) %copy-start) | copy-done | bytes 65560
  45.2 2.2 %shard_map.167 = (f32[4,128]{1,0:T(4,128)}, s32[1,1]{1,0:T(1,128)}) custom-call(s32[1,4]{1,0:T(1,128)} %valid_hbm.1, s32[512,4,128]{2,1,0:T(4,128)} %all-gather.2.cloned.1.call-done.loads_hbm, f32[12,128]{1,0:T(8,128)} %get-tuple-element.14.chain_hbm, f32[32,4,128]{2,1,0:T(4,128)} %copy-done), custom_call_target="tpu_custom_call" | custom-call | tf_op jit(solution)/shard_map/pallas_call | solution.py:459
Async XLA Ops:
  7.2 37.4 %all-gather.2.cloned.1.call-start = ((), (), s32[]{:S(2)}) async-start(), calls=%async_computation.1 | async-start | bytes 1310720 | tf_op jit(solution)/shard_map/all_gather | solution.py:441
  28.6 15.9 %all-to-all-start = ((f32[32,4,128]{2,1,0:T(4,128)}), f32[32,4,128]{2,1,0:T(4,128)S(1)}, u32[]{:S(2)}, u32[]{:S(2)}) async-start(f32[32,4,128]{2,1,0:T(4,128)} %get-tuple-element.15), calls=%async_computation | async-start | bytes 131072 | tf_op jit(solution)/shard_map/all_to_all | solution.py:457
  44.6 0.6 %copy-start = (f32[32,4,128]{2,1,0:T(4,128)}, f32[32,4,128]{2,1,0:T(4,128)S(1)}, u32[]{:S(2)}) copy-start(f32[32,4,128]{2,1,0:T(4,128)S(1)} %all-to-all-done.got_ref) | copy-start | bytes 196612
Sparse Core Ops, SparseCore 0:
  9.7 26.5 all-gather.1

commit v4 on v3

--- a/solution.py
+++ b/solution.py
@@ -11,7 +11,8 @@
 F32 = jnp.float32
 LANE = 8
 TAPS = 9
-GRANT = 60 * 2**20
+FRONT_GRANT = 60 * 2**20
+BACK_GRANT = 60 * 2**20
 
 
 def tile_order(flat_ref, side):
@@ -85,6 +86,7 @@
     ends_hbm,
     rewards_hbm,
     ratios_hbm,
+    valid_hbm,
     frames_hbm,
     stored_hbm,
     stem_hbm,
@@ -105,10 +107,13 @@
     hidden,
     act,
     mid,
+    sums,
+    kept,
     counts_ref,
     ends_ref,
     rewards_ref,
     ratios_ref,
+    valid_ref,
     stored_ref,
     head_ref,
     discounts_ref,
@@ -140,12 +145,19 @@
             (ends_hbm, ends_ref),
             (rewards_hbm, rewards_ref),
             (ratios_hbm, ratios_ref),
+            (valid_hbm, valid_ref),
             (stored_hbm, stored_ref),
             (head_hbm, head_ref),
             (discounts_hbm, discounts_ref),
             (lambdas_hbm, lambdas_ref),
         )
     ]
+    hidden_copy = pltpu.make_async_copy(hidden, hidden_hbm, sems.at[next(sem)])
+    middle_sem = next(sem)
+
+    def middle_copy(b):
+        return pltpu.make_async_copy(mid.at[b], middle_hbm.at[b], sems.at[middle_sem + b])
+
     stem_copy.wait()
 
     def begin(b):
@@ -182,6 +194,11 @@
                 weight_copies[2].wait()
 
             put_padded(mid, b, jnp.maximum(conv(act, b, weights.at[2 * l]), 0.0))
+
+            @pl.when(l == 1)
+            def _():
+                middle_copy(b).start()
+
             return 0
 
         def second(b, _):
@@ -197,24 +214,27 @@
         def _():
             weight_copies[1].wait()
             lax.fori_loop(0, steps, second, 0)
+            hidden_copy.start()
 
         return 0
 
     lax.fori_loop(0, 2, layer, 0)
-    out_copies = [load(hidden, hidden_hbm), load(mid, middle_hbm)]
 
     select = window_rows(side)
     width = hidden.shape[-1]
-    sums, kept = [], []
-    for b in range(steps):
+
+    def total(b, _):
         block = mid[b, 1 : half + 1, 1 : mid.shape[2] - 1].reshape(side * side, width)
-        sums.append(jnp.dot(select, block, preferred_element_type=F32))
         rows = hidden[b].reshape(side * side, width)
-        kept.append(jnp.dot(select, rows, preferred_element_type=F32)[TAPS : TAPS + 1])
+        sums[b] = jnp.dot(select, block, preferred_element_type=F32)
+        kept[b] = jnp.dot(select, rows, preferred_element_type=F32)
+        return 0
+
+    lax.fori_loop(0, steps, total, 0)
     weight_copies[3].wait()
     pooled = None
     for tap in range(TAPS):
-        exact = jnp.concatenate([block[tap : tap + 1] for block in sums], axis=0)
+        exact = jnp.concatenate([sums[b, tap : tap + 1] for b in range(steps)], axis=0)
         parts, rest = [], exact
         for _ in range(3):
             part = rest.astype(BF)
@@ -224,7 +244,7 @@
         term = jnp.dot(stacked, weights[3, tap], preferred_element_type=F32)
         pooled = term if pooled is None else pooled + term
     pooled = pooled[0:steps] + pooled[steps : 2 * steps] + pooled[2 * steps : 3 * steps]
-    pooled = (pooled + jnp.concatenate(kept, axis=0)) * (1.0 / (side * side))
+    pooled = (pooled + jnp.concatenate([kept[b, TAPS : TAPS + 1] for b in range(steps)], axis=0)) * (1.0 / (side * side))
     for copy in small:
         copy.wait()
     fresh = jnp.dot(
@@ -256,14 +276,16 @@
             add = reward + weight * rows[t + 1] + step_mul * add
             last = step_mul * last
         mul = step_mul * mul
-        chain_ref[t : t + 1] = add
-        chain_ref[steps + t : steps + t + 1] = mul
-        chain_ref[2 * steps + t : 2 * steps + t + 1] = last
+        valid = valid_ref[0, t].astype(F32)
+        chain_ref[t : t + 1] = valid * add
+        chain_ref[steps + t : steps + t + 1] = valid * mul
+        chain_ref[2 * steps + t : 2 * steps + t + 1] = valid * last
     shards = send_ref.shape[0]
     for place, row in enumerate((add, mul, last, rows[0])):
         send_ref[:, place : place + 1, :] = jnp.broadcast_to(row[None], (shards, 1, row.shape[1]))
-    for copy in out_copies:
-        copy.wait()
+    hidden_copy.wait()
+    for b in range(steps):
+        middle_copy(b).wait()
 
 
 def back_kernel(side, counts_ref, middle_hbm, hidden_hbm, second_hbm, out_hbm, mid, hidden, weight, flat, done, sems):
@@ -313,7 +335,7 @@
 HBM = pl.BlockSpec(memory_space=pl.ANY)
 
 
-def front(counts, ends, rewards, ratios, frames, stored, stem, first, second, head, discounts, lambdas, shards):
+def front(counts, ends, rewards, ratios, valid, frames, stored, stem, first, second, head, discounts, lambdas, shards):
     steps, side, _, pdim = frames.shape
     width, heads = stem.shape[1], head.shape[1]
     half, third = side // 2, side // LANE
@@ -330,7 +352,7 @@
             jax.ShapeDtypeStruct((shards, 4, heads), F32),
             jax.ShapeDtypeStruct((3 * steps, heads), F32),
         ),
-        in_specs=[HBM] * 12,
+        in_specs=[HBM] * 13,
         out_specs=(HBM, HBM, VMEM, VMEM, VMEM),
         scratch_shapes=[
             pltpu.VMEM((steps, area, pdim), BF),
@@ -340,19 +362,22 @@
             pltpu.VMEM(plain, BF),
             pltpu.VMEM(padded, BF),
             pltpu.VMEM(padded, BF),
+            pltpu.VMEM((steps, 2 * LANE, width), F32),
+            pltpu.VMEM((steps, 2 * LANE, width), F32),
             pltpu.SMEM(counts.shape, jnp.int32),
             pltpu.SMEM(ends.shape, jnp.int32),
             pltpu.SMEM(rewards.shape, F32),
             pltpu.SMEM(ratios.shape, F32),
+            pltpu.SMEM(valid.shape, jnp.int32),
             pltpu.VMEM(stored.shape, F32),
             pltpu.VMEM(head.shape, BF),
             pltpu.VMEM(discounts.shape, F32),
             pltpu.VMEM(lambdas.shape, F32),
             pltpu.SemaphoreType.DMA((32,)),
         ],
-        compiler_params=pltpu.CompilerParams(vmem_limit_bytes=GRANT),
+        compiler_params=pltpu.CompilerParams(vmem_limit_bytes=FRONT_GRANT),
         cost_estimate=pl.CostEstimate(flops=work, bytes_accessed=16 * 10**6, transcendentals=0),
-    )(counts, ends, rewards, ratios, frames.reshape(steps, area, pdim), stored, stem, first, second, head, discounts, lambdas)
+    )(counts, ends, rewards, ratios, valid, frames.reshape(steps, area, pdim), stored, stem, first, second, head, discounts, lambdas)
 
 
 def back(counts, middle, hidden, second, side):
@@ -371,24 +396,24 @@
             pltpu.VMEM((steps, area, width), BF),
             pltpu.SemaphoreType.DMA((32,)),
         ],
-        compiler_params=pltpu.CompilerParams(vmem_limit_bytes=GRANT),
+        compiler_params=pltpu.CompilerParams(vmem_limit_bytes=BACK_GRANT),
         cost_estimate=pl.CostEstimate(
             flops=steps * area * 2 * width * TAPS * width, bytes_accessed=8 * 10**6, transcendentals=0
         ),
     )(counts, middle, hidden, second)
 
 
-def target_kernel(steps, valid_hbm, loads_hbm, chain_hbm, got_ref, targets_ref, load_ref, valid_ref, loads_ref, chain_ref, sems):
+def target_kernel(steps, *refs):
+    groups = 4
+    pairs = refs[: 2 * groups]
+    chain_hbm, got_ref, targets_ref, load_ref = refs[2 * groups : 2 * groups + 4]
+    held = refs[2 * groups + 4 : 4 * groups + 4]
+    chain_ref, sems = refs[4 * groups + 4 :]
     group, shard = lax.axis_index("grp"), lax.axis_index("tm")
-    shards = got_ref.shape[0]
-    groups, part = loads_ref.shape[0], loads_hbm.shape[0] // loads_ref.shape[0]
-    width = chain_ref.shape[1]
+    shards, width = got_ref.shape[0], chain_ref.shape[1]
     copies = [
-        pltpu.make_async_copy(valid_hbm, valid_ref, sems.at[0]),
-        pltpu.make_async_copy(chain_hbm, chain_ref, sems.at[1]),
+        pltpu.make_async_copy(src, dst, sems.at[i]) for i, (src, dst) in enumerate(zip(pairs + (chain_hbm,), held + (chain_ref,)))
     ]
-    for g in range(groups):
-        copies.append(pltpu.make_async_copy(loads_hbm.at[g * part], loads_ref.at[g], sems.at[2 + g]))
     for copy in copies:
         copy.start()
     zero = jnp.zeros((1, width), F32)
@@ -403,16 +428,18 @@
     for copy in copies:
         copy.wait()
     for t in range(steps):
-        total = (
+        targets_ref[t : t + 1] = (
             chain_ref[t : t + 1]
             + chain_ref[steps + t : steps + t + 1] * kept_carry
             + chain_ref[2 * steps + t : 2 * steps + t + 1] * kept_first
         )
-        targets_ref[t : t + 1] = valid_ref[0, t].astype(F32) * total
-    lane = lax.broadcasted_iota(jnp.int32, loads_ref.shape, 2)
-    mine = jnp.where(lane == group, loads_ref[...], 0).astype(F32)
-    mine = jnp.sum(jnp.sum(mine, axis=0), axis=0, keepdims=True)
-    load_ref[...] = jnp.sum(mine, axis=1, keepdims=True).astype(jnp.int32)
+    load = jnp.int32(0)
+    for g in range(groups):
+        for t in range(steps):
+            count = held[2 * g][0, t]
+            hit = jnp.logical_and(count > 0, held[2 * g + 1][0, t] == group)
+            load = load + jnp.where(hit, count, 0)
+    load_ref[0, 0] = load
 
 
 def per_device(
@@ -435,15 +462,16 @@
     width = stem_weight.shape[1]
     heads = value_weight.shape[1]
     groups, shards = lax.axis_size("grp"), lax.axis_size("tm")
-    lanes = jnp.arange(128, dtype=jnp.int32)[None, :]
-    hits = jnp.where(dest_groups[0][:, None] == lanes, jnp.maximum(sample_counts[0], 0)[:, None], 0)
-    loads = lax.optimization_barrier(jnp.broadcast_to(hits[None], (128, steps, 128)))
-    loads = lax.all_gather(loads, "grp", axis=0, tiled=True)
+    near = [(g, g ^ 1) for g in range(groups)]
+    far = [(g, g ^ 3) for g in range(groups)]
+    routed = [sample_counts, dest_groups]
+    routed += [lax.ppermute(part, "grp", near) for part in routed]
     middle, hidden, values, send, chain = front(
         sample_counts,
         episode_ends,
         rewards,
         ratios,
+        valid_steps,
         frames[0],
         stored_values[0],
         stem_weight,
@@ -455,6 +483,8 @@
         shards,
     )
     got = lax.all_to_all(send, "tm", split_axis=0, concat_axis=0, tiled=True)
+    routed += [lax.ppermute(part, "grp", far) for part in routed]
+    middle, *routed = lax.optimization_barrier((middle, *routed))
     latents = back(sample_counts, middle, hidden, conv_second, side)
     targets, load = pl.pallas_call(
         functools.partial(target_kernel, steps),
@@ -462,16 +492,12 @@
             jax.ShapeDtypeStruct((steps, heads), F32),
             jax.ShapeDtypeStruct((1, 1), jnp.int32),
         ),
-        in_specs=[HBM, HBM, HBM, VMEM],
-        out_specs=(VMEM, VMEM),
-        scratch_shapes=[
-            pltpu.SMEM(valid_steps.shape, jnp.int32),
-            pltpu.VMEM((groups, steps, 128), jnp.int32),
-            pltpu.VMEM((3 * steps, heads), F32),
-            pltpu.SemaphoreType.DMA((2 + groups,)),
-        ],
-        compiler_params=pltpu.CompilerParams(vmem_limit_bytes=GRANT),
-    )(valid_steps, loads, chain, got)
+        in_specs=[HBM] * (len(routed) + 1) + [VMEM],
+        out_specs=(VMEM, SMEM),
+        scratch_shapes=[pltpu.SMEM(sample_counts.shape, jnp.int32)] * len(routed)
+        + [pltpu.VMEM((3 * steps, heads), F32), pltpu.SemaphoreType.DMA((len(routed) + 1,))],
+        compiler_params=pltpu.CompilerParams(vmem_limit_bytes=BACK_GRANT),
+    )(*routed, chain, got)
     latents = latents.reshape(1, steps, side, side, width)
     return latents, values[None], targets[None], load
 

time: 54.6 us -> 50.8 us (0.930)
  between operations: 14.1 us -> 0.76 us
  starting transfers between devices: 8.66 us -> 17.5 us
  waiting for transfers between devices: 0.66 us -> 3.56 us
  other arithmetic: 1.38 us -> 0 us
  local copies, waits for them, and re-layouts: 1.36 us -> 0.64 us
    ppermute x0 -> x6, starting transfers between devices: none -> 8.89 us  [the longest x4 5.61 us: per_device(): routed += [lax.ppermute(part, 'grp', far) for part in routed]]
    ppermute x0 -> x6, waiting for transfers between devices: none -> 3.55 us  [the longest x4 3.55 us: per_device(): routed += [lax.ppermute(part, 'grp', far) for part in routed]]
    broadcast_in_dim x1 -> x0, local copies, waits for them, and re-layouts: 0.75 us -> none  [per_device(): jnp.broadcast_to(hits[None], (128, steps, 128))]
    select_n x1 -> x0, other arithmetic: 0.72 us -> none  [per_device(): jnp.where(dest_groups[0][:, None] == lanes, jnp.maximum(sample_counts[0],...]
    max x1 -> x0, other arithmetic: 0.66 us -> none  [per_device(): jnp.maximum(sample_counts[0], 0)[:, None]]
    all_to_all x1, waiting for transfers between devices: 0.64 us -> 0.01 us  [per_device(): got = lax.all_to_all(send, 'tm', split_axis=0, concat_axis=0, tiled=True)]
  transfers between devices with their start and end apart: 2 -> 7, of which waited for: 1 -> 2; matrix products, arithmetic and copies ran while one was open for 0% -> 0% of each run, Pallas kernels for 48% -> 51%
where the time goes in v4:
time: 50.8 us; the launch traced here: 50.3 us
  Pallas kernels  27.9 us (55%)
  starting transfers between devices  17.5 us (34%)
  waiting for transfers between devices  3.56 us (7%)
  between operations  0.76 us (1%)
  local copies, waits for them, and re-layouts  0.64 us (1%)
    pallas_call x1, Pallas kernels, front(): pl.pallas_call(functools.partial(front_kernel, side), out_shape=(jax.Shap...  18.9 us
    all_to_all x1, starting transfers between devices, per_device(): got = lax.all_to_all(send, 'tm', split_axis=0, concat_axis=0, tiled=True)  8.64 us
    pallas_call x1, Pallas kernels, back(): pl.pallas_call(functools.partial(back_kernel, side), out_shape=jax.ShapeD...  6.67 us
    ppermute x4, starting transfers between devices, per_device(): routed += [lax.ppermute(part, 'grp', far) for part in routed]  5.61 us
    ppermute x4, waiting for transfers between devices, per_device(): routed += [lax.ppermute(part, 'grp', far) for part in routed]  3.55 us
    ppermute x2, starting transfers between devices, per_device(): routed += [lax.ppermute(part, 'grp', near) for part in routed]  3.28 us
    pallas_call x1, Pallas kernels, per_device(): pl.pallas_call(functools.partial(target_kernel, steps), out_shape=(jax.Sh...  2.24 us
  transfers between devices with their start and end apart: 7, of which 2 were waited for; matrix products, arithmetic and copies ran while one was open for 0% of the time, Pallas kernels for 51%

profile of v4, /device:TPU:1, one launch (start us, length us, event | category | flops | bytes accessed | tf_op | source)
XLA Modules:
  0.0 50.3 jit_solution(5053293107980277748)
XLA Ops:
  0.6 2.5 %collective-permute-start = (s32[1,4]{1,0:T(1,128)}, s32[1,4]{1,0:T(1,128)S(1)}, u32[]{:S(2)}, u32[]{:S(2)}) collective-permute-start(s32[1,4]{1,0:T(1,128)} %refs_0_), channel_id=1, source_target_pairs={{0,32},{32,0},{64,96},{96,64},{1,33},{33,1},{65,97},{97,65},{2,34}... | collective-permute-start | bytes 56 | tf_op jit(solution)/shard_map/ppermute | solution.py:468
  3.2 2.2 %collective-permute-start.2 = (s32[1,4]{1,0:T(1,128)}, s32[1,4]{1,0:T(1,128)S(1)}, u32[]{:S(2)}, u32[]{:S(2)}) collective-permute-start(s32[1,4]{1,0:T(1,128)} %refs_0_), channel_id=1, source_target_pairs={{0,96},{32,64},{64,32},{96,0},{1,97},{33,65},{65,33},{97,1},{2,98}... | collective-permute-start | bytes 56 | tf_op jit(solution)/shard_map/ppermute | solution.py:486
  5.4 0.7 %collective-permute-start.1 = (s32[1,4]{1,0:T(1,128)}, s32[1,4]{1,0:T(1,128)S(1)}, u32[]{:S(2)}, u32[]{:S(2)}) collective-permute-start(s32[1,4]{1,0:T(1,128)} %refs_1_), channel_id=1, source_target_pairs={{0,32},{32,0},{64,96},{96,64},{1,33},{33,1},{65,97},{97,65},{2,34}... | collective-permute-start | bytes 56 | tf_op jit(solution)/shard_map/ppermute | solution.py:468
  6.2 0.6 %collective-permute-start.3 = (s32[1,4]{1,0:T(1,128)}, s32[1,4]{1,0:T(1,128)S(1)}, u32[]{:S(2)}, u32[]{:S(2)}) collective-permute-start(s32[1,4]{1,0:T(1,128)} %refs_1_), channel_id=1, source_target_pairs={{0,96},{32,64},{64,32},{96,0},{1,97},{33,65},{65,33},{97,1},{2,98}... | collective-permute-start | bytes 56 | tf_op jit(solution)/shard_map/ppermute | solution.py:486
  6.8 18.9 %shard_map.165 = (bf16[4,14,5,16,256]{4,3,2,1,0:T(8,128)(2,1)}, bf16[4,12,3,16,256]{4,3,2,1,0:T(8,128)(2,1)}, f32[4,128]{1,0:T(4,128)}, f32[32,4,128]{2,1,0:T(4,128)}, f32[12,128]{1,0:T(8,128)}) custom-call(s32[1,4]{1,0:T(1,128)} %refs_0_, s32[1,4]{1,0:T(1,128)} %ends_hbm.1, f32[1,4]{1,0:T(1,128)} %rewards_hbm.1, f32[1,4]{1,0:T(1,128)} %ratios_hbm.1, ...), custom_call_target="tpu_custom_call" | custom-call | flops 10569646080 | bytes 16000000 | tf_op jit(solution)/shard_map/pallas_call | solution.py:346
  25.7 8.6 %all-to-all-start = ((f32[32,4,128]{2,1,0:T(4,128)}), f32[32,4,128]{2,1,0:T(4,128)S(1)}, u32[]{:S(2)}, u32[]{:S(2)}) async-start(f32[32,4,128]{2,1,0:T(4,128)} %get-tuple-element.33), calls=%async_computation | async-start | bytes 131072 | tf_op jit(solution)/shard_map/all_to_all | solution.py:485
  34.4 0.0 collective-permute-done.refs_2_
  34.4 0.0 copy-start.1
  34.4 2.4 %collective-permute-start.4 = (s32[1,4]{1,0:T(1,128)S(1)}, s32[1,4]{1,0:T(1,128)S(1)}, u32[]{:S(2)}, u32[]{:S(2)}) collective-permute-start(s32[1,4]{1,0:T(1,128)S(1)} %collective-permute-done.refs_2_), channel_id=1, source_target_pairs={{0,96},{32,64},{64,32},{96,0},{1,97},{33,65},{65,33},{97,1},{2,98}... | collective-permute-start | bytes 56 | tf_op jit(solution)/shard_map/ppermute | solution.py:486
  36.8 0.0 collective-permute-done.1.refs_3_
  36.8 0.0 copy-start.3
  36.8 0.3 collective-permute-start.5
  37.2 0.0 collective-permute-done.2.refs_4_
  37.2 0.0 copy-start.2
  37.2 0.0 collective-permute-done.3.refs_5_
  37.2 0.0 copy-start.4
  37.2 1.2 %collective-permute-done.4.refs_6_ = s32[1,4]{1,0:T(1,128)S(1)} collective-permute-done((s32[1,4]{1,0:T(1,128)S(1)}, s32[1,4]{1,0:T(1,128)S(1)}, u32[]{:S(2)}, u32[]{:S(2)}) %collective-permute-start.4) | collective-permute-done | bytes 48 | tf_op jit(solution)/shard_map/ppermute | solution.py:486
  38.4 0.0 copy-start.5
  38.4 2.4 %collective-permute-done.5.refs_7_ = s32[1,4]{1,0:T(1,128)S(1)} collective-permute-done((s32[1,4]{1,0:T(1,128)S(1)}, s32[1,4]{1,0:T(1,128)S(1)}, u32[]{:S(2)}, u32[]{:S(2)}) %collective-permute-start.5) | collective-permute-done | bytes 48 | tf_op jit(solution)/shard_map/ppermute | solution.py:486
  40.7 0.0 copy-start.6
  40.7 6.7 %shard_map.166 = bf16[4,576,256]{2,1,0:T(8,128)(2,1)} custom-call(s32[1,4]{1,0:T(1,128)} %refs_0_, bf16[4,14,5,16,256]{4,3,2,1,0:T(8,128)(2,1)} %get-tuple-element.21.middle_hbm, bf16[4,12,3,16,256]{4,3,2,1,0:T(8,128)(2,1)} %get-tuple-element.22.hidden_hbm, bf16[2,9,256,256]{3,2,1,0:T(8,128)(2,1)} %second_hbm.3), custom_call_target="tpu_custom_call" | custom-call | flops 2717908992 | bytes 8000000 | tf_op jit(solution)/shard_map/pallas_call | solution.py:386
  47.4 0.0 copy-done.1
  47.4 0.0 copy-done.3
  47.4 0.0 copy-done.2
  47.4 0.0 copy-done.4
  47.4 0.0 copy-done.5
  47.5 0.0 copy-done.6
  47.5 0.0 all-to-all-done.refs_9_
  47.5 0.0 copy-start
  47.5 0.6 %copy-done = f32[32,4,128]{2,1,0:T(4,128)} copy-done((f32[32,4,128]{2,1,0:T(4,128)}, f32[32,4,128]{2,1,0:T(4,128)S(1)}, u32[]{:S(2)}) %copy-start) | copy-done | bytes 65560
  48.1 2.2 %shard_map.167 = (f32[4,128]{1,0:T(4,128)}, s32[1,1]{1,0:T(1,128)}) custom-call(s32[1,4]{1,0:T(1,128)} %refs_0_, s32[1,4]{1,0:T(1,128)} %refs_1_, s32[1,4]{1,0:T(1,128)} %copy-done.1, s32[1,4]{1,0:T(1,128)} %copy-done.3, s32[1,4]{1,0:T(1,128)} %copy-done.2, s32[1,4]{1,0:T(1,128)} %copy-done.4, s32[1,4]{1,0:T(1,128)} %copy-done.5, s32[1,4]{1,0:T(1,128)} %copy-done.6, ...), custom_call_target="tpu_custom_call" | custom-call | tf_op jit(solution)/shard_map/pallas_call | solution.py:489
Async XLA Ops:
  0.6 33.7 %collective-permute-start = (s32[1,4]{1,0:T(1,128)}, s32[1,4]{1,0:T(1,128)S(1)}, u32[]{:S(2)}, u32[]{:S(2)}) collective-permute-start(s32[1,4]{1,0:T(1,128)} %refs_0_), channel_id=1, source_target_pairs={{0,32},{32,0},{64,96},{96,64},{1,33},{33,1},{65,97},{97,65},{2,34}... | collective-permute-start | bytes 56 | tf_op jit(solution)/shard_map/ppermute | solution.py:468
  3.2 34.0 %collective-permute-start.2 = (s32[1,4]{1,0:T(1,128)}, s32[1,4]{1,0:T(1,128)S(1)}, u32[]{:S(2)}, u32[]{:S(2)}) collective-permute-start(s32[1,4]{1,0:T(1,128)} %refs_0_), channel_id=1, source_target_pairs={{0,96},{32,64},{64,32},{96,0},{1,97},{33,65},{65,33},{97,1},{2,98}... | collective-permute-start | bytes 56 | tf_op jit(solution)/shard_map/ppermute | solution.py:486
  5.4 31.4 %collective-permute-start.1 = (s32[1,4]{1,0:T(1,128)}, s32[1,4]{1,0:T(1,128)S(1)}, u32[]{:S(2)}, u32[]{:S(2)}) collective-permute-start(s32[1,4]{1,0:T(1,128)} %refs_1_), channel_id=1, source_target_pairs={{0,32},{32,0},{64,96},{96,64},{1,33},{33,1},{65,97},{97,65},{2,34}... | collective-permute-start | bytes 56 | tf_op jit(solution)/shard_map/ppermute | solution.py:468
  6.2 31.0 %collective-permute-start.3 = (s32[1,4]{1,0:T(1,128)}, s32[1,4]{1,0:T(1,128)S(1)}, u32[]{:S(2)}, u32[]{:S(2)}) collective-permute-start(s32[1,4]{1,0:T(1,128)} %refs_1_), channel_id=1, source_target_pairs={{0,96},{32,64},{64,32},{96,0},{1,97},{33,65},{65,33},{97,1},{2,98}... | collective-permute-start | bytes 56 | tf_op jit(solution)/shard_map/ppermute | solution.py:486
  25.7 21.7 %all-to-all-start = ((f32[32,4,128]{2,1,0:T(4,128)}), f32[32,4,128]{2,1,0:T(4,128)S(1)}, u32[]{:S(2)}, u32[]{:S(2)}) async-start(f32[32,4,128]{2,1,0:T(4,128)} %get-tuple-element.33), calls=%async_computation | async-start | bytes 131072 | tf_op jit(solution)/shard_map/all_to_all | solution.py:485
  34.4 13.0 %copy-start.1 = (s32[1,4]{1,0:T(1,128)}, s32[1,4]{1,0:T(1,128)S(1)}, u32[]{:S(2)}) copy-start(s32[1,4]{1,0:T(1,128)S(1)} %collective-permute-done.refs_2_) | copy-start | bytes 52
  34.4 4.0 %collective-permute-start.4 = (s32[1,4]{1,0:T(1,128)S(1)}, s32[1,4]{1,0:T(1,128)S(1)}, u32[]{:S(2)}, u32[]{:S(2)}) collective-permute-start(s32[1,4]{1,0:T(1,128)S(1)} %collective-permute-done.refs_2_), channel_id=1, source_target_pairs={{0,96},{32,64},{64,32},{96,0},{1,97},{33,65},{65,33},{97,1},{2,98}... | collective-permute-start | bytes 56 | tf_op jit(solution)/shard_map/ppermute | solution.py:486
  36.8 10.6 %copy-start.3 = (s32[1,4]{1,0:T(1,128)}, s32[1,4]{1,0:T(1,128)S(1)}, u32[]{:S(2)}) copy-start(s32[1,4]{1,0:T(1,128)S(1)} %collective-permute-done.1.refs_3_) | copy-start | bytes 52
  36.8 3.9 %collective-permute-start.5 = (s32[1,4]{1,0:T(1,128)S(1)}, s32[1,4]{1,0:T(1,128)S(1)}, u32[]{:S(2)}, u32[]{:S(2)}) collective-permute-start(s32[1,4]{1,0:T(1,128)S(1)} %collective-permute-done.1.refs_3_), channel_id=1, source_target_pairs={{0,96},{32,64},{64,32},{96,0},{1,97},{33,65},{65,33},{97,1},{2,98}... | collective-permute-start | bytes 56 | tf_op jit(solution)/shard_map/ppermute | solution.py:486
  37.2 10.3 %copy-start.2 = (s32[1,4]{1,0:T(1,128)}, s32[1,4]{1,0:T(1,128)S(1)}, u32[]{:S(2)}) copy-start(s32[1,4]{1,0:T(1,128)S(1)} %collective-permute-done.2.refs_4_) | copy-start | bytes 52
  37.2 10.3 %copy-start.4 = (s32[1,4]{1,0:T(1,128)}, s32[1,4]{1,0:T(1,128)S(1)}, u32[]{:S(2)}) copy-start(s32[1,4]{1,0:T(1,128)S(1)} %collective-permute-done.3.refs_5_) | copy-start | bytes 52
  38.4 9.1 %copy-start.5 = (s32[1,4]{1,0:T(1,128)}, s32[1,4]{1,0:T(1,128)S(1)}, u32[]{:S(2)}) copy-start(s32[1,4]{1,0:T(1,128)S(1)} %collective-permute-done.4.refs_6_) | copy-start | bytes 52
  40.7 6.7 %copy-start.6 = (s32[1,4]{1,0:T(1,128)}, s32[1,4]{1,0:T(1,128)S(1)}, u32[]{:S(2)}) copy-start(s32[1,4]{1,0:T(1,128)S(1)} %collective-permute-done.5.refs_7_) | copy-start | bytes 52
  47.5 0.6 %copy-start = (f32[32,4,128]{2,1,0:T(4,128)}, f32[32,4,128]{2,1,0:T(4,128)S(1)}, u32[]{:S(2)}) copy-start(f32[32,4,128]{2,1,0:T(4,128)S(1)} %all-to-all-done.refs_9_) | copy-start | bytes 196612

commit v5 on v4

--- a/solution.py
+++ b/solution.py
@@ -11,6 +11,8 @@
 F32 = jnp.float32
 LANE = 8
 TAPS = 9
+WINO = True
+CHUNK = 12
 FRONT_GRANT = 60 * 2**20
 BACK_GRANT = 60 * 2**20
 
@@ -28,21 +30,23 @@
     return jnp.stack(tiles).reshape(half, third, 2, LANE, -1)
 
 
-def put_padded(out_ref, b, tiles):
-    half, third, _, _, width = tiles.shape
-    place = lax.broadcasted_iota(jnp.int32, (half * 2, LANE, width), 1)
-    before = pltpu.roll(tiles[:, third - 1].reshape(half * 2, LANE, width), 1, 1)
-    before = jnp.where(place == 0, 0.0, before).reshape(half, 1, 2, LANE, width)
-    after = pltpu.roll(tiles[:, 0].reshape(half * 2, LANE, width), LANE - 1, 1)
-    after = jnp.where(place == LANE - 1, 0.0, after).reshape(half, 1, 2, LANE, width)
+def put_padded(out_ref, b, tiles, y0, half):
+    count, third, _, _, width = tiles.shape
+    place = lax.broadcasted_iota(jnp.int32, (count * 2, LANE, width), 1)
+    before = pltpu.roll(tiles[:, third - 1].reshape(count * 2, LANE, width), 1, 1)
+    before = jnp.where(place == 0, 0.0, before).reshape(count, 1, 2, LANE, width)
+    after = pltpu.roll(tiles[:, 0].reshape(count * 2, LANE, width), LANE - 1, 1)
+    after = jnp.where(place == LANE - 1, 0.0, after).reshape(count, 1, 2, LANE, width)
     wide = jnp.concatenate([before, tiles, after], axis=1)
-    rows = wide.reshape(half, third + 2, 2 * LANE, width).astype(BF)
-    out_ref[b, 1 : half + 1] = rows
+    rows = wide.reshape(count, third + 2, 2 * LANE, width).astype(BF)
+    out_ref[b, y0 + 1 : y0 + count + 1] = rows
     none = jnp.zeros((third + 2, 1, LANE, width), F32)
-    top = jnp.concatenate([none, wide[half - 1, :, 0:1]], axis=1)
-    out_ref[b, 0] = top.reshape(third + 2, 2 * LANE, width).astype(BF)
-    bottom = jnp.concatenate([wide[0, :, 1:2], none], axis=1)
-    out_ref[b, half + 1] = bottom.reshape(third + 2, 2 * LANE, width).astype(BF)
+    if y0 + count == half:
+        top = jnp.concatenate([none, wide[count - 1, :, 0:1]], axis=1)
+        out_ref[b, 0] = top.reshape(third + 2, 2 * LANE, width).astype(BF)
+    if y0 == 0:
+        bottom = jnp.concatenate([wide[0, :, 1:2], none], axis=1)
+        out_ref[b, half + 1] = bottom.reshape(third + 2, 2 * LANE, width).astype(BF)
 
 
 def normed(hidden):
@@ -51,16 +55,50 @@
     return jnp.maximum(wide * scale, 0.0)
 
 
-def conv(src_ref, b, weight_ref):
+def conv(src_ref, b, weight_ref, mixed_ref, y0, count):
     _, tall, broad, rows, width = src_ref.shape
-    half, third = tall - 2, broad - 2
-    total = None
-    for tap in range(TAPS):
-        dy, dx = tap // 3, tap % 3
-        window = src_ref[b, dy : dy + half, dx : dx + third].reshape(half * third * rows, width)
-        part = jnp.dot(window, weight_ref[tap], preferred_element_type=F32)
-        total = part if total is None else total + part
-    return total.reshape(half, third, 2, LANE, weight_ref.shape[2])
+    third = broad - 2
+    if not WINO:
+        total = None
+        for tap in range(TAPS):
+            dy, dx = tap // 3, tap % 3
+            window = src_ref[b, y0 + dy : y0 + dy + count, dx : dx + third].reshape(count * third * rows, width)
+            part = jnp.dot(window, weight_ref[tap], preferred_element_type=F32)
+            total = part if total is None else total + part
+        return total.reshape(count, third, 2, LANE, weight_ref.shape[2])
+    pairs = count // 2
+    block = src_ref[b, y0 : y0 + count + 2].reshape(pairs + 1, 2, broad, rows, width)
+    e0, e1, e2, e3 = block[:pairs, 0], block[:pairs, 1], block[1:, 0], block[1:, 1]
+    parts = []
+    for k, mix in enumerate((e0 - e2, e1 + e2, e2 - e1, e1 - e3)):
+        total = None
+        for dx in range(3):
+            weight = (weight_ref[dx], mixed_ref[dx], mixed_ref[3 + dx], weight_ref[6 + dx])[k]
+            window = mix[:, dx : dx + third].reshape(pairs * third * rows, width)
+            part = jnp.dot(window, weight, preferred_element_type=F32)
+            total = part if total is None else total + part
+        parts.append(total)
+    low = parts[0] + parts[1] + parts[2]
+    high = parts[1] - parts[2] - parts[3]
+    out = jnp.stack([x.reshape(pairs, third, 2, LANE, -1) for x in (low, high)], axis=1)
+    return out.reshape(count, third, 2, LANE, -1)
+
+
+def mix_weights(weight_ref, mixed_ref):
+    if not WINO:
+        return
+    size = weight_ref.shape[1]
+
+    def some(i, _):
+        rows = pl.ds(pl.multiple_of(i * 64, 64), 64)
+        for dx in range(3):
+            outer = weight_ref[dx, rows].astype(F32) + weight_ref[6 + dx, rows].astype(F32)
+            inner = weight_ref[3 + dx, rows].astype(F32)
+            mixed_ref[dx, rows] = (0.5 * (outer + inner)).astype(BF)
+            mixed_ref[3 + dx, rows] = (0.5 * (outer - inner)).astype(BF)
+        return 0
+
+    lax.fori_loop(0, size // 64, some, 0)
 
 
 def window_rows(side):
@@ -83,6 +121,7 @@
 def front_kernel(
     side,
     counts_hbm,
+    dests_hbm,
     ends_hbm,
     rewards_hbm,
     ratios_hbm,
@@ -100,6 +139,7 @@
     values_ref,
     send_ref,
     chain_ref,
+    loads_ref,
     frames,
     stem,
     weights,
@@ -109,7 +149,9 @@
     mid,
     sums,
     kept,
+    mixed,
     counts_ref,
+    dests_ref,
     ends_ref,
     rewards_ref,
     ratios_ref,
@@ -142,6 +184,7 @@
         load(src, dst)
         for src, dst in (
             (counts_hbm, counts_ref),
+            (dests_hbm, dests_ref),
             (ends_hbm, ends_ref),
             (rewards_hbm, rewards_ref),
             (ratios_hbm, ratios_ref),
@@ -177,7 +220,7 @@
             flat[c] = rows[:, 128 * c : 128 * c + 128]
         start = tile_order(flat, side).astype(BF)
         hidden[b] = start.reshape(hidden.shape[1:])
-        put_padded(act, b, normed(start))
+        put_padded(act, b, normed(start), 0, half)
 
     def layer(l, _):
         def first(b, _):
@@ -188,12 +231,16 @@
             @pl.when((l == 0) & (b == 0))
             def _():
                 weight_copies[0].wait()
+                mix_weights(weights.at[0], mixed)
 
             @pl.when((l == 1) & (b == 0))
             def _():
                 weight_copies[2].wait()
-
-            put_padded(mid, b, jnp.maximum(conv(act, b, weights.at[2 * l]), 0.0))
+                mix_weights(weights.at[2], mixed)
+
+            for y0 in range(0, half, CHUNK):
+                out = conv(act, b, weights.at[2 * l], mixed, y0, CHUNK)
+                put_padded(mid, b, jnp.maximum(out, 0.0), y0, half)
 
             @pl.when(l == 1)
             def _():
@@ -202,10 +249,12 @@
             return 0
 
         def second(b, _):
-            out = conv(mid, b, weights.at[1])
-            now = (hidden[b].astype(F32).reshape(out.shape) + out).astype(BF)
-            hidden[b] = now.reshape(hidden.shape[1:])
-            put_padded(act, b, normed(now))
+            for y0 in range(0, half, CHUNK):
+                out = conv(mid, b, weights.at[1], mixed, y0, CHUNK)
+                now = hidden[b, y0 : y0 + CHUNK].astype(F32).reshape(out.shape) + out
+                now = now.astype(BF)
+                hidden[b, y0 : y0 + CHUNK] = now.reshape((CHUNK,) + hidden.shape[2:])
+                put_padded(act, b, normed(now), y0, half)
             return 0
 
         lax.fori_loop(0, steps, first, 0)
@@ -213,6 +262,7 @@
         @pl.when(l == 0)
         def _():
             weight_copies[1].wait()
+            mix_weights(weights.at[1], mixed)
             lax.fori_loop(0, steps, second, 0)
             hidden_copy.start()
 
@@ -283,12 +333,17 @@
     shards = send_ref.shape[0]
     for place, row in enumerate((add, mul, last, rows[0])):
         send_ref[:, place : place + 1, :] = jnp.broadcast_to(row[None], (shards, 1, row.shape[1]))
+    for g in range(loads_ref.shape[0]):
+        load_here = jnp.int32(0)
+        for t in range(steps):
+            load_here = load_here + jnp.where(dests_ref[0, t] == g, jnp.maximum(counts_ref[0, t], 0), 0)
+        loads_ref[g] = jnp.full((1, 128), load_here, jnp.int32)
     hidden_copy.wait()
     for b in range(steps):
         middle_copy(b).wait()
 
 
-def back_kernel(side, counts_ref, middle_hbm, hidden_hbm, second_hbm, out_hbm, mid, hidden, weight, flat, done, sems):
+def back_kernel(side, counts_ref, middle_hbm, hidden_hbm, second_hbm, out_hbm, mid, hidden, weight, mixed, flat, done, sems):
     steps = mid.shape[0]
     half, third = side // 2, side // LANE
     copies = []
@@ -307,19 +362,22 @@
             )
         )
     weight_copy.wait()
+    mix_weights(weight, mixed)
 
     def finish(b, _):
         pltpu.make_async_copy(middle_hbm.at[b], mid.at[b], sems.at[1 + 3 * b]).wait()
         pltpu.make_async_copy(hidden_hbm.at[b], hidden.at[b], sems.at[2 + 3 * b]).wait()
-        out = conv(mid, b, weight)
-        out = hidden[b].astype(F32).reshape(out.shape) + out
-        out = jnp.where(counts_ref[0, b] > 0, out, jnp.zeros_like(out))
-        for y in range(half):
-            for j in range(third):
-                for h in range(2):
-                    start = side * (half * h + y) + j
-                    for c in range(flat.shape[0]):
-                        flat[c, pl.ds(start, LANE, stride=third), :] = out[y, j, h, :, 128 * c : 128 * c + 128]
+        live = counts_ref[0, b] > 0
+        for y0 in range(0, half, CHUNK):
+            out = conv(mid, b, weight, mixed, y0, CHUNK)
+            out = hidden[b, y0 : y0 + CHUNK].astype(F32).reshape(out.shape) + out
+            out = jnp.where(live, out, jnp.zeros_like(out))
+            for y in range(CHUNK):
+                for j in range(third):
+                    for h in range(2):
+                        start = side * (half * h + y0 + y) + j
+                        for c in range(flat.shape[0]):
+                            flat[c, pl.ds(start, LANE, stride=third), :] = out[y, j, h, :, 128 * c : 128 * c + 128]
         for c in range(flat.shape[0]):
             done[b, :, 128 * c : 128 * c + 128] = flat[c].astype(BF)
         pltpu.make_async_copy(done.at[b], out_hbm.at[b], sems.at[3 + 3 * b]).start()
@@ -332,10 +390,11 @@
 
 SMEM = pl.BlockSpec(memory_space=pltpu.SMEM)
 VMEM = pl.BlockSpec(memory_space=pltpu.VMEM)
-HBM = pl.BlockSpec(memory_space=pl.ANY)
-
-
-def front(counts, ends, rewards, ratios, valid, frames, stored, stem, first, second, head, discounts, lambdas, shards):
+ANY = pl.BlockSpec(memory_space=pl.ANY)
+HBM = pl.BlockSpec(memory_space=pltpu.HBM)
+
+
+def front(counts, dests, ends, rewards, ratios, valid, frames, stored, stem, first, second, head, discounts, lambdas, shards, groups):
     steps, side, _, pdim = frames.shape
     width, heads = stem.shape[1], head.shape[1]
     half, third = side // 2, side // LANE
@@ -351,9 +410,10 @@
             jax.ShapeDtypeStruct((steps, heads), F32),
             jax.ShapeDtypeStruct((shards, 4, heads), F32),
             jax.ShapeDtypeStruct((3 * steps, heads), F32),
+            jax.ShapeDtypeStruct((groups, 1, 128), jnp.int32),
         ),
-        in_specs=[HBM] * 13,
-        out_specs=(HBM, HBM, VMEM, VMEM, VMEM),
+        in_specs=[HBM] * 14,
+        out_specs=(ANY, ANY, VMEM, VMEM, VMEM, VMEM),
         scratch_shapes=[
             pltpu.VMEM((steps, area, pdim), BF),
             pltpu.VMEM(stem.shape, BF),
@@ -364,7 +424,9 @@
             pltpu.VMEM(padded, BF),
             pltpu.VMEM((steps, 2 * LANE, width), F32),
             pltpu.VMEM((steps, 2 * LANE, width), F32),
+            pltpu.VMEM((6, width, width), BF),
             pltpu.SMEM(counts.shape, jnp.int32),
+            pltpu.SMEM(dests.shape, jnp.int32),
             pltpu.SMEM(ends.shape, jnp.int32),
             pltpu.SMEM(rewards.shape, F32),
             pltpu.SMEM(ratios.shape, F32),
@@ -377,7 +439,7 @@
         ],
         compiler_params=pltpu.CompilerParams(vmem_limit_bytes=FRONT_GRANT),
         cost_estimate=pl.CostEstimate(flops=work, bytes_accessed=16 * 10**6, transcendentals=0),
-    )(counts, ends, rewards, ratios, valid, frames.reshape(steps, area, pdim), stored, stem, first, second, head, discounts, lambdas)
+    )(counts, dests, ends, rewards, ratios, valid, frames.reshape(steps, area, pdim), stored, stem, first, second, head, discounts, lambdas)
 
 
 def back(counts, middle, hidden, second, side):
@@ -386,12 +448,13 @@
     return pl.pallas_call(
         functools.partial(back_kernel, side),
         out_shape=jax.ShapeDtypeStruct((steps, area, width), BF),
-        in_specs=[SMEM, HBM, HBM, HBM],
+        in_specs=[SMEM, ANY, ANY, HBM],
         out_specs=HBM,
         scratch_shapes=[
             pltpu.VMEM(middle.shape, BF),
             pltpu.VMEM(hidden.shape, BF),
             pltpu.VMEM((TAPS, width, width), BF),
+            pltpu.VMEM((6, width, width), BF),
             pltpu.VMEM((width // 128, area, 128), F32),
             pltpu.VMEM((steps, area, width), BF),
             pltpu.SemaphoreType.DMA((32,)),
@@ -403,19 +466,15 @@
     )(counts, middle, hidden, second)
 
 
-def target_kernel(steps, *refs):
-    groups = 4
-    pairs = refs[: 2 * groups]
-    chain_hbm, got_ref, targets_ref, load_ref = refs[2 * groups : 2 * groups + 4]
-    held = refs[2 * groups + 4 : 4 * groups + 4]
-    chain_ref, sems = refs[4 * groups + 4 :]
-    group, shard = lax.axis_index("grp"), lax.axis_index("tm")
+def target_kernel(steps, loads_hbm, chain_hbm, got_hbm, targets_ref, load_ref, loads_ref, chain_ref, got_ref, sems):
+    shard = lax.axis_index("tm")
     shards, width = got_ref.shape[0], chain_ref.shape[1]
-    copies = [
-        pltpu.make_async_copy(src, dst, sems.at[i]) for i, (src, dst) in enumerate(zip(pairs + (chain_hbm,), held + (chain_ref,)))
-    ]
+    pairs = ((got_hbm, got_ref), (chain_hbm, chain_ref), (loads_hbm, loads_ref))
+    copies = [pltpu.make_async_copy(src, dst, sems.at[i]) for i, (src, dst) in enumerate(pairs)]
     for copy in copies:
         copy.start()
+    for copy in copies:
+        copy.wait()
     zero = jnp.zeros((1, width), F32)
     carry, first = zero, zero
     kept_carry, kept_first = zero, zero
@@ -425,21 +484,16 @@
         follows = jnp.full((1, width), shard + 1, jnp.int32) == s
         kept_carry = jnp.where(follows, carry, kept_carry)
         kept_first = jnp.where(follows, first, kept_first)
-    for copy in copies:
-        copy.wait()
     for t in range(steps):
         targets_ref[t : t + 1] = (
             chain_ref[t : t + 1]
             + chain_ref[steps + t : steps + t + 1] * kept_carry
             + chain_ref[2 * steps + t : 2 * steps + t + 1] * kept_first
         )
-    load = jnp.int32(0)
-    for g in range(groups):
-        for t in range(steps):
-            count = held[2 * g][0, t]
-            hit = jnp.logical_and(count > 0, held[2 * g + 1][0, t] == group)
-            load = load + jnp.where(hit, count, 0)
-    load_ref[0, 0] = load
+    load = loads_ref[0]
+    for g in range(1, loads_ref.shape[0]):
+        load = load + loads_ref[g]
+    load_ref[...] = load[:, 0:1]
 
 
 def per_device(
@@ -462,12 +516,9 @@
     width = stem_weight.shape[1]
     heads = value_weight.shape[1]
     groups, shards = lax.axis_size("grp"), lax.axis_size("tm")
-    near = [(g, g ^ 1) for g in range(groups)]
-    far = [(g, g ^ 3) for g in range(groups)]
-    routed = [sample_counts, dest_groups]
-    routed += [lax.ppermute(part, "grp", near) for part in routed]
-    middle, hidden, values, send, chain = front(
+    middle, hidden, values, send, chain, loads = front(
         sample_counts,
+        dest_groups,
         episode_ends,
         rewards,
         ratios,
@@ -481,10 +532,10 @@
         discounts[None],
         lambdas[None],
         shards,
+        groups,
     )
     got = lax.all_to_all(send, "tm", split_axis=0, concat_axis=0, tiled=True)
-    routed += [lax.ppermute(part, "grp", far) for part in routed]
-    middle, *routed = lax.optimization_barrier((middle, *routed))
+    loads = lax.all_to_all(loads, "grp", split_axis=0, concat_axis=0, tiled=True)
     latents = back(sample_counts, middle, hidden, conv_second, side)
     targets, load = pl.pallas_call(
         functools.partial(target_kernel, steps),
@@ -492,12 +543,16 @@
             jax.ShapeDtypeStruct((steps, heads), F32),
             jax.ShapeDtypeStruct((1, 1), jnp.int32),
         ),
-        in_specs=[HBM] * (len(routed) + 1) + [VMEM],
-        out_specs=(VMEM, SMEM),
-        scratch_shapes=[pltpu.SMEM(sample_counts.shape, jnp.int32)] * len(routed)
-        + [pltpu.VMEM((3 * steps, heads), F32), pltpu.SemaphoreType.DMA((len(routed) + 1,))],
+        in_specs=[ANY] * 3,
+        out_specs=(VMEM, VMEM),
+        scratch_shapes=[
+            pltpu.VMEM(loads.shape, jnp.int32),
+            pltpu.VMEM(chain.shape, F32),
+            pltpu.VMEM(got.shape, F32),
+            pltpu.SemaphoreType.DMA((3,)),
+        ],
         compiler_params=pltpu.CompilerParams(vmem_limit_bytes=BACK_GRANT),
-    )(*routed, chain, got)
+    )(loads, chain, got)
     latents = latents.reshape(1, steps, side, side, width)
     return latents, values[None], targets[None], load
 

time: 50.8 us -> 46.9 us (0.923)
  blocking collectives: 0 us -> 9.85 us
  starting transfers between devices: 17.5 us -> 9.34 us
  Pallas kernels: 27.9 us -> 24.8 us
  waiting for transfers between devices: 3.56 us -> 1.41 us
    all_to_all x0 -> x1, blocking collectives: none -> 9.85 us  [per_device(): lax.all_to_all(loads, 'grp', split_axis=0, concat_axis=0, tiled=True)]
    ppermute x6 -> x0, starting transfers between devices: 8.89 us -> none  [the longest x4 5.61 us: per_device(): routed += [lax.ppermute(part, 'grp', far) for part in routed]]
    ppermute x6 -> x0, waiting for transfers between devices: 3.55 us -> none  [the longest x4 3.55 us: per_device(): routed += [lax.ppermute(part, 'grp', far) for part in routed]]
    pallas_call x1, Pallas kernels: 18.9 us -> 17.3 us  [front(): pl.pallas_call(functools.partial(front_kernel, side), out_shape=(jax.Shap...]
    all_to_all x1, waiting for transfers between devices: 0.01 us -> 1.41 us  [per_device(): got = lax.all_to_all(send, 'tm', split_axis=0, concat_axis=0, tiled=True)]
    pallas_call x1, Pallas kernels: 6.67 us -> 5.91 us  [back(): pl.pallas_call(functools.partial(back_kernel, side), out_shape=jax.ShapeD...]
    all_to_all x1, starting transfers between devices: 8.64 us -> 9.34 us  [per_device(): got = lax.all_to_all(send, 'tm', split_axis=0, concat_axis=0, tiled=True)]
    pallas_call x1, Pallas kernels: 2.24 us -> 1.55 us  [per_device(): pl.pallas_call(functools.partial(target_kernel, steps), out_shape=(jax.Sh...]
  transfers between devices with their start and end apart: 7 -> 1, of which waited for: 2 -> 1; matrix products, arithmetic and copies ran while one was open for 0% -> 0% of each run, Pallas kernels for 51% -> 13%
where the time goes in v5:
time: 46.9 us; the launch traced here: 46.7 us
  Pallas kernels  24.8 us (53%)
  blocking collectives  9.85 us (21%)
  starting transfers between devices  9.34 us (20%)
  waiting for transfers between devices  1.41 us (3%)
  between operations  0.66 us (1%)
  local copies, waits for them, and re-layouts  0.62 us (1%)
    pallas_call x1, Pallas kernels, front(): pl.pallas_call(functools.partial(front_kernel, side), out_shape=(jax.Shap...  17.3 us
    all_to_all x1, blocking collectives, per_device(): lax.all_to_all(loads, 'grp', split_axis=0, concat_axis=0, tiled=True)  9.85 us
    all_to_all x1, starting transfers between devices, per_device(): got = lax.all_to_all(send, 'tm', split_axis=0, concat_axis=0, tiled=True)  9.34 us
    pallas_call x1, Pallas kernels, back(): pl.pallas_call(functools.partial(back_kernel, side), out_shape=jax.ShapeD...  5.91 us
    pallas_call x1, Pallas kernels, per_device(): pl.pallas_call(functools.partial(target_kernel, steps), out_shape=(jax.Sh...  1.55 us
    all_to_all x1, waiting for transfers between devices, per_device(): got = lax.all_to_all(send, 'tm', split_axis=0, concat_axis=0, tiled=True)  1.41 us
  transfers between devices with their start and end apart: 1, of which 1 were waited for; matrix products, arithmetic and copies ran while one was open for 0% of the time, Pallas kernels for 13%

profile of v5, /device:TPU:1, one launch (start us, length us, event | category | flops | bytes accessed | tf_op | source)
XLA Modules:
  0.0 46.7 jit_solution(15657664670155427724)
XLA Ops:
  0.6 17.3 %shard_map.165 = (bf16[4,14,5,16,256]{4,3,2,1,0:T(8,128)(2,1)}, bf16[4,12,3,16,256]{4,3,2,1,0:T(8,128)(2,1)}, f32[4,128]{1,0:T(4,128)}, f32[32,4,128]{2,1,0:T(4,...) custom-call(s32[1,4]{1,0:T(1,128)} %counts_ref.1, s32[1,4]{1,0:T(1,128)} %dests_hbm.1, s32[1,4]{1,0:T(1,128)} %ends_hbm.1, ...), custom_call_target="tpu_custom_call" | custom-call | flops 10569646080 | bytes 16000000 | tf_op jit(solution)/shard_map/pallas_call | solution.py:405
  18.0 9.8 %all_to_all.10.loads_hbm = s32[4,1,128]{2,1,0:T(1,128)} all-to-all(s32[4,1,128]{2,1,0:T(1,128)} %get-tuple-element.15), channel_id=1, replica_groups=mesh['grp'=4,'tm'=32] {'grp'}, dimensions={0} | all-to-all | bytes 4096 | tf_op jit(solution)/shard_map/all_to_all | solution.py:538
  27.8 9.3 %all-to-all-start.1 = ((f32[32,4,128]{2,1,0:T(4,128)}), f32[32,4,128]{2,1,0:T(4,128)S(1)}, u32[]{:S(2)}, u32[]{:S(2)}) async-start(f32[32,4,128]{2,1,0:T(4,128)} %get-tuple-element.17), calls=%async_computation.1 | async-start | bytes 131072 | tf_op jit(solution)/shard_map/all_to_all | solution.py:537
  37.2 5.9 %shard_map.166 = bf16[4,576,256]{2,1,0:T(8,128)(2,1)} custom-call(s32[1,4]{1,0:T(1,128)} %counts_ref.1, bf16[4,14,5,16,256]{4,3,2,1,0:T(8,128)(2,1)} %get-tuple-element.12.middle_hbm, bf16[4,12,3,16,256]{4,3,2,1,0:T(8,128)(2,1)} %get-tuple-element.13.hidden_hbm, bf16[2,9,256,256]{3,2,1,0:T(8,128)(2,1)} %second_hbm.3), custom_call_target="tpu_custom_call" | custom-call | flops 2717908992 | bytes 8000000 | tf_op jit(solution)/shard_map/pallas_call | solution.py:448
  43.1 1.4 %all-to-all-done.1.got_hbm = f32[32,4,128]{2,1,0:T(4,128)S(1)} async-done(((f32[32,4,128]{2,1,0:T(4,128)}), f32[32,4,128]{2,1,0:T(4,128)S(1)}, u32[]{:S(2)}, u32[]{:S(2)}) %all-to-all-start.1) | async-done | bytes 65568 | tf_op jit(solution)/shard_map/all_to_all | solution.py:537
  44.5 0.0 copy-start
  44.5 0.6 %copy-done = f32[32,4,128]{2,1,0:T(4,128)} copy-done((f32[32,4,128]{2,1,0:T(4,128)}, f32[32,4,128]{2,1,0:T(4,128)S(1)}, u32[]{:S(2)}) %copy-start) | copy-done | bytes 65560
  45.1 1.6 %shard_map.167 = (f32[4,128]{1,0:T(4,128)}, s32[1,1]{1,0:T(1,128)}) custom-call(s32[4,1,128]{2,1,0:T(1,128)} %all_to_all.10.loads_hbm, f32[12,128]{1,0:T(8,128)} %get-tuple-element.16.chain_hbm, f32[32,4,128]{2,1,0:T(4,128)} %copy-done), custom_call_target="tpu_custom_call" | custom-call | tf_op jit(solution)/shard_map/pallas_call | solution.py:540
Async XLA Ops:
  27.8 16.7 %all-to-all-start.1 = ((f32[32,4,128]{2,1,0:T(4,128)}), f32[32,4,128]{2,1,0:T(4,128)S(1)}, u32[]{:S(2)}, u32[]{:S(2)}) async-start(f32[32,4,128]{2,1,0:T(4,128)} %get-tuple-element.17), calls=%async_computation.1 | async-start | bytes 131072 | tf_op jit(solution)/shard_map/all_to_all | solution.py:537
  44.5 0.6 %copy-start = (f32[32,4,128]{2,1,0:T(4,128)}, f32[32,4,128]{2,1,0:T(4,128)S(1)}, u32[]{:S(2)}) copy-start(f32[32,4,128]{2,1,0:T(4,128)S(1)} %all-to-all-done.1.got_hbm) | copy-start | bytes 196612

commit v6 on v5

--- a/solution.py
+++ b/solution.py
@@ -15,6 +15,8 @@
 CHUNK = 12
 FRONT_GRANT = 60 * 2**20
 BACK_GRANT = 60 * 2**20
+LAST_GRANT = 40 * 2**20
+TALL = 2**16
 
 
 def tile_order(flat_ref, side):
@@ -121,7 +123,6 @@
 def front_kernel(
     side,
     counts_hbm,
-    dests_hbm,
     ends_hbm,
     rewards_hbm,
     ratios_hbm,
@@ -138,8 +139,7 @@
     hidden_hbm,
     values_ref,
     send_ref,
-    chain_ref,
-    loads_ref,
+    chain_hbm,
     frames,
     stem,
     weights,
@@ -150,8 +150,8 @@
     sums,
     kept,
     mixed,
+    chain_ref,
     counts_ref,
-    dests_ref,
     ends_ref,
     rewards_ref,
     ratios_ref,
@@ -184,7 +184,6 @@
         load(src, dst)
         for src, dst in (
             (counts_hbm, counts_ref),
-            (dests_hbm, dests_ref),
             (ends_hbm, ends_ref),
             (rewards_hbm, rewards_ref),
             (ratios_hbm, ratios_ref),
@@ -196,7 +195,7 @@
         )
     ]
     hidden_copy = pltpu.make_async_copy(hidden, hidden_hbm, sems.at[next(sem)])
-    middle_sem = next(sem)
+    middle_sem = 24
 
     def middle_copy(b):
         return pltpu.make_async_copy(mid.at[b], middle_hbm.at[b], sems.at[middle_sem + b])
@@ -330,21 +329,25 @@
         chain_ref[t : t + 1] = valid * add
         chain_ref[steps + t : steps + t + 1] = valid * mul
         chain_ref[2 * steps + t : 2 * steps + t + 1] = valid * last
+    chain_copy = load(chain_ref, chain_hbm.at[pl.ds(0, 3 * steps)])
     shards = send_ref.shape[0]
     for place, row in enumerate((add, mul, last, rows[0])):
         send_ref[:, place : place + 1, :] = jnp.broadcast_to(row[None], (shards, 1, row.shape[1]))
-    for g in range(loads_ref.shape[0]):
-        load_here = jnp.int32(0)
-        for t in range(steps):
-            load_here = load_here + jnp.where(dests_ref[0, t] == g, jnp.maximum(counts_ref[0, t], 0), 0)
-        loads_ref[g] = jnp.full((1, 128), load_here, jnp.int32)
+    chain_copy.wait()
     hidden_copy.wait()
     for b in range(steps):
         middle_copy(b).wait()
 
 
-def back_kernel(side, counts_ref, middle_hbm, hidden_hbm, second_hbm, out_hbm, mid, hidden, weight, mixed, flat, done, sems):
+def back_kernel(side, groups, *refs):
+    routed = refs[:groups]
+    middle_hbm, hidden_hbm, second_hbm, out_hbm, load_ref = refs[groups : groups + 5]
+    held = refs[groups + 5 : 2 * groups + 5]
+    mid, hidden, weight, mixed, flat, done, sems = refs[2 * groups + 5 :]
     steps = mid.shape[0]
+    small = [pltpu.make_async_copy(src, dst, sems.at[16 + i]) for i, (src, dst) in enumerate(zip(routed, held))]
+    for copy in small:
+        copy.start()
     half, third = side // 2, side // LANE
     copies = []
 
@@ -361,13 +364,15 @@
                 load(2 + 3 * b, hidden_hbm.at[b], hidden.at[b]),
             )
         )
+    for copy in small:
+        copy.wait()
     weight_copy.wait()
     mix_weights(weight, mixed)
 
     def finish(b, _):
         pltpu.make_async_copy(middle_hbm.at[b], mid.at[b], sems.at[1 + 3 * b]).wait()
         pltpu.make_async_copy(hidden_hbm.at[b], hidden.at[b], sems.at[2 + 3 * b]).wait()
-        live = counts_ref[0, b] > 0
+        live = held[0][0, b] >= groups
         for y0 in range(0, half, CHUNK):
             out = conv(mid, b, weight, mixed, y0, CHUNK)
             out = hidden[b, y0 : y0 + CHUNK].astype(F32).reshape(out.shape) + out
@@ -384,6 +389,13 @@
         return 0
 
     lax.fori_loop(0, steps, finish, 0)
+    group = lax.axis_index("grp")
+    total = jnp.int32(0)
+    for codes in held:
+        for t in range(steps):
+            code = codes[0, t]
+            total = total + jnp.where(code % groups == group, code // groups, 0)
+    load_ref[0, 0] = total
     for b in range(steps):
         pltpu.make_async_copy(done.at[b], out_hbm.at[b], sems.at[3 + 3 * b]).wait()
 
@@ -394,7 +406,7 @@
 HBM = pl.BlockSpec(memory_space=pltpu.HBM)
 
 
-def front(counts, dests, ends, rewards, ratios, valid, frames, stored, stem, first, second, head, discounts, lambdas, shards, groups):
+def front(counts, ends, rewards, ratios, valid, frames, stored, stem, first, second, head, discounts, lambdas, shards):
     steps, side, _, pdim = frames.shape
     width, heads = stem.shape[1], head.shape[1]
     half, third = side // 2, side // LANE
@@ -409,11 +421,10 @@
             jax.ShapeDtypeStruct(plain, BF),
             jax.ShapeDtypeStruct((steps, heads), F32),
             jax.ShapeDtypeStruct((shards, 4, heads), F32),
-            jax.ShapeDtypeStruct((3 * steps, heads), F32),
-            jax.ShapeDtypeStruct((groups, 1, 128), jnp.int32),
+            jax.ShapeDtypeStruct((TALL, heads), F32),
         ),
-        in_specs=[HBM] * 14,
-        out_specs=(ANY, ANY, VMEM, VMEM, VMEM, VMEM),
+        in_specs=[HBM] * 13,
+        out_specs=(ANY, ANY, VMEM, VMEM, ANY),
         scratch_shapes=[
             pltpu.VMEM((steps, area, pdim), BF),
             pltpu.VMEM(stem.shape, BF),
@@ -425,8 +436,8 @@
             pltpu.VMEM((steps, 2 * LANE, width), F32),
             pltpu.VMEM((steps, 2 * LANE, width), F32),
             pltpu.VMEM((6, width, width), BF),
+            pltpu.VMEM((3 * steps, heads), F32),
             pltpu.SMEM(counts.shape, jnp.int32),
-            pltpu.SMEM(dests.shape, jnp.int32),
             pltpu.SMEM(ends.shape, jnp.int32),
             pltpu.SMEM(rewards.shape, F32),
             pltpu.SMEM(ratios.shape, F32),
@@ -439,18 +450,22 @@
         ],
         compiler_params=pltpu.CompilerParams(vmem_limit_bytes=FRONT_GRANT),
         cost_estimate=pl.CostEstimate(flops=work, bytes_accessed=16 * 10**6, transcendentals=0),
-    )(counts, dests, ends, rewards, ratios, valid, frames.reshape(steps, area, pdim), stored, stem, first, second, head, discounts, lambdas)
-
-
-def back(counts, middle, hidden, second, side):
+    )(counts, ends, rewards, ratios, valid, frames.reshape(steps, area, pdim), stored, stem, first, second, head, discounts, lambdas)
+
+
+def back(routed, middle, hidden, second, side):
     steps, width = middle.shape[0], middle.shape[-1]
     area = side * side
     return pl.pallas_call(
-        functools.partial(back_kernel, side),
-        out_shape=jax.ShapeDtypeStruct((steps, area, width), BF),
-        in_specs=[SMEM, ANY, ANY, HBM],
-        out_specs=HBM,
-        scratch_shapes=[
+        functools.partial(back_kernel, side, len(routed)),
+        out_shape=(
+            jax.ShapeDtypeStruct((steps, area, width), BF),
+            jax.ShapeDtypeStruct((1, 1), jnp.int32),
+        ),
+        in_specs=[ANY] * len(routed) + [ANY, ANY, HBM],
+        out_specs=(HBM, SMEM),
+        scratch_shapes=[pltpu.SMEM(routed[0].shape, jnp.int32)] * len(routed)
+        + [
             pltpu.VMEM(middle.shape, BF),
             pltpu.VMEM(hidden.shape, BF),
             pltpu.VMEM((TAPS, width, width), BF),
@@ -463,13 +478,13 @@
         cost_estimate=pl.CostEstimate(
             flops=steps * area * 2 * width * TAPS * width, bytes_accessed=8 * 10**6, transcendentals=0
         ),
-    )(counts, middle, hidden, second)
-
-
-def target_kernel(steps, loads_hbm, chain_hbm, got_hbm, targets_ref, load_ref, loads_ref, chain_ref, got_ref, sems):
+    )(*routed, middle, hidden, second)
+
+
+def target_kernel(steps, chain_hbm, got_hbm, targets_ref, chain_ref, got_ref, sems):
     shard = lax.axis_index("tm")
     shards, width = got_ref.shape[0], chain_ref.shape[1]
-    pairs = ((got_hbm, got_ref), (chain_hbm, chain_ref), (loads_hbm, loads_ref))
+    pairs = ((got_hbm, got_ref), (chain_hbm.at[pl.ds(0, 3 * steps)], chain_ref))
     copies = [pltpu.make_async_copy(src, dst, sems.at[i]) for i, (src, dst) in enumerate(pairs)]
     for copy in copies:
         copy.start()
@@ -490,11 +505,6 @@
             + chain_ref[steps + t : steps + t + 1] * kept_carry
             + chain_ref[2 * steps + t : 2 * steps + t + 1] * kept_first
         )
-    load = loads_ref[0]
-    for g in range(1, loads_ref.shape[0]):
-        load = load + loads_ref[g]
-    load_ref[...] = load[:, 0:1]
-
 
 def per_device(
     frames,
@@ -516,9 +526,12 @@
     width = stem_weight.shape[1]
     heads = value_weight.shape[1]
     groups, shards = lax.axis_size("grp"), lax.axis_size("tm")
-    middle, hidden, values, send, chain, loads = front(
+    codes = sample_counts * groups + dest_groups
+    routed = [codes]
+    for far in range(1, groups):
+        routed.append(lax.ppermute(codes, "grp", [(g, (g + far) % groups) for g in range(groups)]))
+    middle, hidden, values, send, chain = front(
         sample_counts,
-        dest_groups,
         episode_ends,
         rewards,
         ratios,
@@ -532,27 +545,21 @@
         discounts[None],
         lambdas[None],
         shards,
-        groups,
     )
     got = lax.all_to_all(send, "tm", split_axis=0, concat_axis=0, tiled=True)
-    loads = lax.all_to_all(loads, "grp", split_axis=0, concat_axis=0, tiled=True)
-    latents = back(sample_counts, middle, hidden, conv_second, side)
-    targets, load = pl.pallas_call(
+    latents, load = back(routed, middle, hidden, conv_second, side)
+    targets = pl.pallas_call(
         functools.partial(target_kernel, steps),
-        out_shape=(
-            jax.ShapeDtypeStruct((steps, heads), F32),
-            jax.ShapeDtypeStruct((1, 1), jnp.int32),
-        ),
-        in_specs=[ANY] * 3,
-        out_specs=(VMEM, VMEM),
+        out_shape=jax.ShapeDtypeStruct((steps, heads), F32),
+        in_specs=[ANY] * 2,
+        out_specs=VMEM,
         scratch_shapes=[
-            pltpu.VMEM(loads.shape, jnp.int32),
-            pltpu.VMEM(chain.shape, F32),
+            pltpu.VMEM((3 * steps, heads), F32),
             pltpu.VMEM(got.shape, F32),
-            pltpu.SemaphoreType.DMA((3,)),
+            pltpu.SemaphoreType.DMA((2,)),
         ],
-        compiler_params=pltpu.CompilerParams(vmem_limit_bytes=BACK_GRANT),
-    )(loads, chain, got)
+        compiler_params=pltpu.CompilerParams(vmem_limit_bytes=LAST_GRANT),
+    )(chain, got)
     latents = latents.reshape(1, steps, side, side, width)
     return latents, values[None], targets[None], load
 

time: 46.9 us -> 42.1 us (0.90)
  blocking collectives: 9.85 us -> 0 us
  starting transfers between devices: 9.34 us -> 13.9 us
  other arithmetic: 0 us -> 0.68 us
    all_to_all x1 -> x0, blocking collectives: 9.85 us -> none  [per_device(): lax.all_to_all(loads, 'grp', split_axis=0, concat_axis=0, tiled=True)]
    ppermute x0 -> x3, starting transfers between devices: none -> 5.29 us  [per_device(): lax.ppermute(codes, 'grp', [(g, (g + far) % groups) for g in range(groups)])]
    all_to_all x1, starting transfers between devices: 9.34 us -> 8.62 us  [per_device(): got = lax.all_to_all(send, 'tm', split_axis=0, concat_axis=0, tiled=True)]
    add x0 -> x1, other arithmetic: none -> 0.68 us  [per_device(): codes = sample_counts * groups + dest_groups]
    pallas_call x1, Pallas kernels: 17.3 us -> 17.9 us  [front(): pl.pallas_call(functools.partial(front_kernel, side), out_shape=(jax.Shap...]
  transfers between devices with their start and end apart: 1 -> 4, of which waited for: 1 -> 1; matrix products, arithmetic and copies ran while one was open for 0% -> 0% of each run, Pallas kernels for 13% -> 56%
where the time goes in v6:
time: 42.1 us; the launch traced here: 41.9 us
  Pallas kernels  25.1 us (60%)
  starting transfers between devices  13.9 us (33%)
  waiting for transfers between devices  0.98 us (2%)
  between operations  0.71 us (2%)
  other arithmetic  0.68 us (2%)
  local copies, waits for them, and re-layouts  0.53 us (1%)
    pallas_call x1, Pallas kernels, front(): pl.pallas_call(functools.partial(front_kernel, side), out_shape=(jax.Shap...  17.9 us
    all_to_all x1, starting transfers between devices, per_device(): got = lax.all_to_all(send, 'tm', split_axis=0, concat_axis=0, tiled=True)  8.62 us
    pallas_call x1, Pallas kernels, back(): pl.pallas_call(functools.partial(back_kernel, side, len(routed)), out_sha...  5.76 us
    ppermute x3, starting transfers between devices, per_device(): lax.ppermute(codes, 'grp', [(g, (g + far) % groups) for g in range(groups)])  5.29 us
    pallas_call x1, Pallas kernels, per_device(): pl.pallas_call(functools.partial(target_kernel, steps), out_shape=jax.Sha...  1.45 us
    all_to_all x1, waiting for transfers between devices, per_device(): got = lax.all_to_all(send, 'tm', split_axis=0, concat_axis=0, tiled=True)  0.97 us
  transfers between devices with their start and end apart: 4, of which 1 were waited for; matrix products, arithmetic and copies ran while one was open for 0% of the time, Pallas kernels for 56%

profile of v6, /device:TPU:1, one launch (start us, length us, event | category | flops | bytes accessed | tf_op | source)
XLA Modules:
  0.0 41.9 jit_solution(17547839480003387059)
XLA Ops:
  0.6 0.7 %multiply_add_fusion.refs_0_ = s32[1,4]{1,0:T(1,128)S(1)} fusion(s32[1,4]{1,0:T(1,128)} %param.16, s32[1,4]{1,0:T(1,128)} %counts_hbm.1), kind=kLoop, calls=%fused_computation | loop fusion | flops 8 | bytes 48 | tf_op jit(solution)/shard_map/add | solution.py:529
  1.3 0.0 copy-start
  1.3 4.6 %collective-permute-start.2 = (s32[1,4]{1,0:T(1,128)S(1)}, s32[1,4]{1,0:T(1,128)S(1)}, u32[]{:S(2)}, u32[]{:S(2)}) collective-permute-start(s32[1,4]{1,0:T(1,128)S(1)} %multiply_add_fusion.refs_0_), channel_id=1, source_target_pairs={{0,96},{32,0},{64,32},{96,64},{1,97},{33,1},{65,33},{97,65},{2,98}... | collective-permute-start | bytes 56 | tf_op jit(solution)/shard_map/ppermute | solution.py:532
  5.9 0.0 collective-permute-start.1
  5.9 0.7 %collective-permute-start = (s32[1,4]{1,0:T(1,128)S(1)}, s32[1,4]{1,0:T(1,128)S(1)}, u32[]{:S(2)}, u32[]{:S(2)}) collective-permute-start(s32[1,4]{1,0:T(1,128)S(1)} %multiply_add_fusion.refs_0_), channel_id=1, source_target_pairs={{0,32},{32,64},{64,96},{96,0},{1,33},{33,65},{65,97},{97,1},{2,34}... | collective-permute-start | bytes 56 | tf_op jit(solution)/shard_map/ppermute | solution.py:532
  6.6 17.9 %shard_map.165 = (bf16[4,14,5,16,256]{4,3,2,1,0:T(8,128)(2,1)}, bf16[4,12,3,16,256]{4,3,2,1,0:T(8,128)(2,1)}, f32[4,128]{1,0:T(4,128)}, f32[32,4,128]{2,1,0:T(4,128)}, f32[65536,128]{1,0:T(8,128)}) custom-call(s32[1,4]{1,0:T(1,128)} %counts_hbm.1, s32[1,4]{1,0:T(1,128)} %ends_hbm.1, f32[1,4]{1,0:T(1,128)} %rewards_hbm.1, f32[1,4]{1,0:T(1,128)} %ratios_hbm.1, ...), custom_call_target="tpu_custom_call" | custom-call | flops 10569646080 | bytes 16000000 | tf_op jit(solution)/shard_map/pallas_call | solution.py:417
  24.5 0.0 copy-done
  24.5 8.6 %all-to-all-start = ((f32[32,4,128]{2,1,0:T(4,128)}), f32[32,4,128]{2,1,0:T(4,128)S(1)}, u32[]{:S(2)}, u32[]{:S(2)}) async-start(f32[32,4,128]{2,1,0:T(4,128)} %get-tuple-element.16), calls=%async_computation | async-start | bytes 131072 | tf_op jit(solution)/shard_map/all_to_all | solution.py:549
  33.1 0.0 collective-permute-done.2.refs_3_
  33.1 0.0 copy-start.1
  33.2 0.0 collective-permute-done.1.refs_2_
  33.2 0.0 copy-start.2
  33.2 0.0 collective-permute-done.refs_1_
  33.2 0.0 copy-start.3
  33.2 0.5 %copy-done.1 = s32[1,4]{1,0:T(1,128)} copy-done((s32[1,4]{1,0:T(1,128)}, s32[1,4]{1,0:T(1,128)S(1)}, u32[]{:S(2)}) %copy-start.1) | copy-done | bytes 40
  33.7 0.0 copy-done.2
  33.7 0.0 copy-done.3
  33.7 5.8 %shard_map.166 = (bf16[4,576,256]{2,1,0:T(8,128)(2,1)}, s32[1,1]{1,0:T(1,128)}) custom-call(s32[1,4]{1,0:T(1,128)} %copy-done, s32[1,4]{1,0:T(1,128)} %copy-done.3, s32[1,4]{1,0:T(1,128)} %copy-done.2, s32[1,4]{1,0:T(1,128)} %copy-done.1, bf16[4,14,5,16,256]{4,3,2,1,0:T(8,128)(2,1)} %get-tuple-element.11.refs_4_, ...), custom_call_target="tpu_custom_call" | custom-call | flops 2717908992 | bytes 8000000 | tf_op jit(solution)/shard_map/pallas_call | solution.py:459
  39.5 1.0 %all-to-all-done.got_hbm = f32[32,4,128]{2,1,0:T(4,128)S(1)} async-done(((f32[32,4,128]{2,1,0:T(4,128)}), f32[32,4,128]{2,1,0:T(4,128)S(1)}, u32[]{:S(2)}, u32[]{:S(2)}) %all-to-all-start) | async-done | bytes 65568 | tf_op jit(solution)/shard_map/all_to_all | solution.py:549
  40.5 1.4 %shard_map.167 = f32[4,128]{1,0:T(4,128)} custom-call(f32[65536,128]{1,0:T(8,128)} %get-tuple-element.15.chain_hbm, f32[32,4,128]{2,1,0:T(4,128)S(1)} %all-to-all-done.got_hbm), custom_call_target="tpu_custom_call" | custom-call | tf_op jit(solution)/shard_map/pallas_call | solution.py:551
Async XLA Ops:
  1.3 23.2 %copy-start = (s32[1,4]{1,0:T(1,128)}, s32[1,4]{1,0:T(1,128)S(1)}, u32[]{:S(2)}) copy-start(s32[1,4]{1,0:T(1,128)S(1)} %multiply_add_fusion.refs_0_) | copy-start | bytes 52
  1.3 31.8 %collective-permute-start.2 = (s32[1,4]{1,0:T(1,128)S(1)}, s32[1,4]{1,0:T(1,128)S(1)}, u32[]{:S(2)}, u32[]{:S(2)}) collective-permute-start(s32[1,4]{1,0:T(1,128)S(1)} %multiply_add_fusion.refs_0_), channel_id=1, source_target_pairs={{0,96},{32,0},{64,32},{96,64},{1,97},{33,1},{65,33},{97,65},{2,98}... | collective-permute-start | bytes 56 | tf_op jit(solution)/shard_map/ppermute | solution.py:532
  5.9 27.3 %collective-permute-start.1 = (s32[1,4]{1,0:T(1,128)S(1)}, s32[1,4]{1,0:T(1,128)S(1)}, u32[]{:S(2)}, u32[]{:S(2)}) collective-permute-start(s32[1,4]{1,0:T(1,128)S(1)} %multiply_add_fusion.refs_0_), channel_id=1, source_target_pairs={{0,64},{32,96},{64,0},{96,32},{1,65},{33,97},{65,1},{97,33},{2,66}... | collective-permute-start | bytes 56 | tf_op jit(solution)/shard_map/ppermute | solution.py:532
  5.9 27.3 %collective-permute-start = (s32[1,4]{1,0:T(1,128)S(1)}, s32[1,4]{1,0:T(1,128)S(1)}, u32[]{:S(2)}, u32[]{:S(2)}) collective-permute-start(s32[1,4]{1,0:T(1,128)S(1)} %multiply_add_fusion.refs_0_), channel_id=1, source_target_pairs={{0,32},{32,64},{64,96},{96,0},{1,33},{33,65},{65,97},{97,1},{2,34}... | collective-permute-start | bytes 56 | tf_op jit(solution)/shard_map/ppermute | solution.py:532
  24.5 15.9 %all-to-all-start = ((f32[32,4,128]{2,1,0:T(4,128)}), f32[32,4,128]{2,1,0:T(4,128)S(1)}, u32[]{:S(2)}, u32[]{:S(2)}) async-start(f32[32,4,128]{2,1,0:T(4,128)} %get-tuple-element.16), calls=%async_computation | async-start | bytes 131072 | tf_op jit(solution)/shard_map/all_to_all | solution.py:549
  33.1 0.6 %copy-start.1 = (s32[1,4]{1,0:T(1,128)}, s32[1,4]{1,0:T(1,128)S(1)}, u32[]{:S(2)}) copy-start(s32[1,4]{1,0:T(1,128)S(1)} %collective-permute-done.2.refs_3_) | copy-start | bytes 52
  33.2 0.5 %copy-start.2 = (s32[1,4]{1,0:T(1,128)}, s32[1,4]{1,0:T(1,128)S(1)}, u32[]{:S(2)}) copy-start(s32[1,4]{1,0:T(1,128)S(1)} %collective-permute-done.1.refs_2_) | copy-start | bytes 52
  33.2 0.5 %copy-start.3 = (s32[1,4]{1,0:T(1,128)}, s32[1,4]{1,0:T(1,128)S(1)}, u32[]{:S(2)}) copy-start(s32[1,4]{1,0:T(1,128)S(1)} %collective-permute-done.refs_1_) | copy-start | bytes 52

commit v7 on v6

--- a/solution.py
+++ b/solution.py
@@ -262,7 +262,7 @@
         def _():
             weight_copies[1].wait()
             mix_weights(weights.at[1], mixed)
-            lax.fori_loop(0, steps, second, 0)
+            lax.fori_loop(0, steps, second, 0, unroll=2)
             hidden_copy.start()
 
         return 0
@@ -339,15 +339,12 @@
         middle_copy(b).wait()
 
 
-def back_kernel(side, groups, *refs):
-    routed = refs[:groups]
-    middle_hbm, hidden_hbm, second_hbm, out_hbm, load_ref = refs[groups : groups + 5]
-    held = refs[groups + 5 : 2 * groups + 5]
-    mid, hidden, weight, mixed, flat, done, sems = refs[2 * groups + 5 :]
+def back_kernel(
+    side, counts_hbm, middle_hbm, hidden_hbm, second_hbm, out_hbm, counts_ref, mid, hidden, weight, mixed, flat, done, sems
+):
     steps = mid.shape[0]
-    small = [pltpu.make_async_copy(src, dst, sems.at[16 + i]) for i, (src, dst) in enumerate(zip(routed, held))]
-    for copy in small:
-        copy.start()
+    counts_copy = pltpu.make_async_copy(counts_hbm, counts_ref, sems.at[16])
+    counts_copy.start()
     half, third = side // 2, side // LANE
     copies = []
 
@@ -364,15 +361,14 @@
                 load(2 + 3 * b, hidden_hbm.at[b], hidden.at[b]),
             )
         )
-    for copy in small:
-        copy.wait()
+    counts_copy.wait()
     weight_copy.wait()
     mix_weights(weight, mixed)
 
     def finish(b, _):
         pltpu.make_async_copy(middle_hbm.at[b], mid.at[b], sems.at[1 + 3 * b]).wait()
         pltpu.make_async_copy(hidden_hbm.at[b], hidden.at[b], sems.at[2 + 3 * b]).wait()
-        live = held[0][0, b] >= groups
+        live = counts_ref[0, b] > 0
         for y0 in range(0, half, CHUNK):
             out = conv(mid, b, weight, mixed, y0, CHUNK)
             out = hidden[b, y0 : y0 + CHUNK].astype(F32).reshape(out.shape) + out
@@ -389,13 +385,6 @@
         return 0
 
     lax.fori_loop(0, steps, finish, 0)
-    group = lax.axis_index("grp")
-    total = jnp.int32(0)
-    for codes in held:
-        for t in range(steps):
-            code = codes[0, t]
-            total = total + jnp.where(code % groups == group, code // groups, 0)
-    load_ref[0, 0] = total
     for b in range(steps):
         pltpu.make_async_copy(done.at[b], out_hbm.at[b], sems.at[3 + 3 * b]).wait()
 
@@ -453,19 +442,16 @@
     )(counts, ends, rewards, ratios, valid, frames.reshape(steps, area, pdim), stored, stem, first, second, head, discounts, lambdas)
 
 
-def back(routed, middle, hidden, second, side):
+def back(counts, middle, hidden, second, side):
     steps, width = middle.shape[0], middle.shape[-1]
     area = side * side
     return pl.pallas_call(
-        functools.partial(back_kernel, side, len(routed)),
-        out_shape=(
-            jax.ShapeDtypeStruct((steps, area, width), BF),
-            jax.ShapeDtypeStruct((1, 1), jnp.int32),
-        ),
-        in_specs=[ANY] * len(routed) + [ANY, ANY, HBM],
-        out_specs=(HBM, SMEM),
-        scratch_shapes=[pltpu.SMEM(routed[0].shape, jnp.int32)] * len(routed)
-        + [
+        functools.partial(back_kernel, side),
+        out_shape=jax.ShapeDtypeStruct((steps, area, width), BF),
+        in_specs=[HBM, ANY, ANY, HBM],
+        out_specs=HBM,
+        scratch_shapes=[
+            pltpu.SMEM(counts.shape, jnp.int32),
             pltpu.VMEM(middle.shape, BF),
             pltpu.VMEM(hidden.shape, BF),
             pltpu.VMEM((TAPS, width, width), BF),
@@ -478,13 +464,16 @@
         cost_estimate=pl.CostEstimate(
             flops=steps * area * 2 * width * TAPS * width, bytes_accessed=8 * 10**6, transcendentals=0
         ),
-    )(*routed, middle, hidden, second)
-
-
-def target_kernel(steps, chain_hbm, got_hbm, targets_ref, chain_ref, got_ref, sems):
-    shard = lax.axis_index("tm")
+    )(counts, middle, hidden, second)
+
+
+def target_kernel(steps, groups, chain_hbm, got_hbm, *refs):
+    routed, targets_ref, load_ref = refs[:groups], refs[groups], refs[groups + 1]
+    chain_ref, got_ref, sems = refs[groups + 2 : groups + 5]
+    held = refs[groups + 5 :]
+    group, shard = lax.axis_index("grp"), lax.axis_index("tm")
     shards, width = got_ref.shape[0], chain_ref.shape[1]
-    pairs = ((got_hbm, got_ref), (chain_hbm.at[pl.ds(0, 3 * steps)], chain_ref))
+    pairs = ((got_hbm, got_ref), (chain_hbm.at[pl.ds(0, 3 * steps)], chain_ref)) + tuple(zip(routed, held))
     copies = [pltpu.make_async_copy(src, dst, sems.at[i]) for i, (src, dst) in enumerate(pairs)]
     for copy in copies:
         copy.start()
@@ -505,6 +494,13 @@
             + chain_ref[steps + t : steps + t + 1] * kept_carry
             + chain_ref[2 * steps + t : 2 * steps + t + 1] * kept_first
         )
+    load = jnp.int32(0)
+    for codes in held:
+        for t in range(steps):
+            code = codes[0, t]
+            load = load + jnp.where(code % groups == group, code // groups, 0)
+    load_ref[0, 0] = load
+
 
 def per_device(
     frames,
@@ -547,19 +543,23 @@
         shards,
     )
     got = lax.all_to_all(send, "tm", split_axis=0, concat_axis=0, tiled=True)
-    latents, load = back(routed, middle, hidden, conv_second, side)
-    targets = pl.pallas_call(
-        functools.partial(target_kernel, steps),
-        out_shape=jax.ShapeDtypeStruct((steps, heads), F32),
-        in_specs=[ANY] * 2,
-        out_specs=VMEM,
+    latents = back(sample_counts, middle, hidden, conv_second, side)
+    targets, load = pl.pallas_call(
+        functools.partial(target_kernel, steps, groups),
+        out_shape=(
+            jax.ShapeDtypeStruct((steps, heads), F32),
+            jax.ShapeDtypeStruct((1, 1), jnp.int32),
+        ),
+        in_specs=[ANY] * (2 + groups),
+        out_specs=(VMEM, SMEM),
         scratch_shapes=[
             pltpu.VMEM((3 * steps, heads), F32),
             pltpu.VMEM(got.shape, F32),
-            pltpu.SemaphoreType.DMA((2,)),
-        ],
+            pltpu.SemaphoreType.DMA((2 + groups,)),
+        ]
+        + [pltpu.SMEM(codes.shape, jnp.int32)] * groups,
         compiler_params=pltpu.CompilerParams(vmem_limit_bytes=LAST_GRANT),
-    )(chain, got)
+    )(chain, got, *routed)
     latents = latents.reshape(1, steps, side, side, width)
     return latents, values[None], targets[None], load
 

time: 42.1 us -> 43 us (1.021)
  starting transfers between devices: 13.9 us -> 15.1 us
  waiting for transfers between devices: 0.98 us -> 2.05 us
  Pallas kernels: 25.1 us -> 24.3 us
  local copies, waits for them, and re-layouts: 0.53 us -> 0 us
    ppermute x3, starting transfers between devices: 5.29 us -> 6.5 us  [per_device(): lax.ppermute(codes, 'grp', [(g, (g + far) % groups) for g in range(groups)])]
    all_to_all x1, waiting for transfers between devices: 0.97 us -> 2.04 us  [per_device(): got = lax.all_to_all(send, 'tm', split_axis=0, concat_axis=0, tiled=True)]
    unnamed x8 -> x0, local copies, waits for them, and re-layouts: 0.53 us -> none
    pallas_call x2, Pallas kernels: 7.2 us -> 6.77 us  [the longest x1 5.24 us: back(): pl.pallas_call(functools.partial(back_kernel, side), out_shape=jax.ShapeD...]
  transfers between devices with their start and end apart: 4 -> 4, of which waited for: 1 -> 1; matrix products, arithmetic and copies ran while one was open for 0% -> 0% of each run, Pallas kernels for 56% -> 53%
where the time goes in v7:
time: 43 us; the launch traced here: 42.8 us
  Pallas kernels  24.3 us (57%)
  starting transfers between devices  15.1 us (35%)
  waiting for transfers between devices  2.05 us (5%)
  other arithmetic  0.68 us (2%)
  between operations  0.68 us (2%)
    pallas_call x1, Pallas kernels, front(): pl.pallas_call(functools.partial(front_kernel, side), out_shape=(jax.Shap...  17.5 us
    all_to_all x1, starting transfers between devices, per_device(): got = lax.all_to_all(send, 'tm', split_axis=0, concat_axis=0, tiled=True)  8.59 us
    ppermute x3, starting transfers between devices, per_device(): lax.ppermute(codes, 'grp', [(g, (g + far) % groups) for g in range(groups)])  6.5 us
    pallas_call x1, Pallas kernels, back(): pl.pallas_call(functools.partial(back_kernel, side), out_shape=jax.ShapeD...  5.24 us
    all_to_all x1, waiting for transfers between devices, per_device(): got = lax.all_to_all(send, 'tm', split_axis=0, concat_axis=0, tiled=True)  2.04 us
    pallas_call x1, Pallas kernels, per_device(): pl.pallas_call(functools.partial(target_kernel, steps, groups), out_shape...  1.53 us
  transfers between devices with their start and end apart: 4, of which 1 were waited for; matrix products, arithmetic and copies ran while one was open for 0% of the time, Pallas kernels for 53%

profile of v7, /device:TPU:1, one launch (start us, length us, event | category | flops | bytes accessed | tf_op | source)
XLA Modules:
  0.0 42.8 jit_solution(17898635182390292214)
XLA Ops:
  0.6 0.7 %multiply_add_fusion.refs_0_ = s32[1,4]{1,0:T(1,128)S(1)} fusion(s32[1,4]{1,0:T(1,128)} %param.16, s32[1,4]{1,0:T(1,128)} %counts_hbm.3), kind=kLoop, calls=%fused_computation | loop fusion | flops 8 | bytes 48 | tf_op jit(solution)/shard_map/add | solution.py:525
  1.3 2.5 %collective-permute-start = (s32[1,4]{1,0:T(1,128)S(1)}, s32[1,4]{1,0:T(1,128)S(1)}, u32[]{:S(2)}, u32[]{:S(2)}) collective-permute-start(s32[1,4]{1,0:T(1,128)S(1)} %multiply_add_fusion.refs_0_), channel_id=1, source_target_pairs={{0,32},{32,64},{64,96},{96,0},{1,33},{33,65},{65,97},{97,1},{2,34}... | collective-permute-start | bytes 56 | tf_op jit(solution)/shard_map/ppermute | solution.py:528
  3.8 3.3 %collective-permute-start.1 = (s32[1,4]{1,0:T(1,128)S(1)}, s32[1,4]{1,0:T(1,128)S(1)}, u32[]{:S(2)}, u32[]{:S(2)}) collective-permute-start(s32[1,4]{1,0:T(1,128)S(1)} %multiply_add_fusion.refs_0_), channel_id=1, source_target_pairs={{0,64},{32,96},{64,0},{96,32},{1,65},{33,97},{65,1},{97,33},{2,66}... | collective-permute-start | bytes 56 | tf_op jit(solution)/shard_map/ppermute | solution.py:528
  7.1 0.7 %collective-permute-start.2 = (s32[1,4]{1,0:T(1,128)S(1)}, s32[1,4]{1,0:T(1,128)S(1)}, u32[]{:S(2)}, u32[]{:S(2)}) collective-permute-start(s32[1,4]{1,0:T(1,128)S(1)} %multiply_add_fusion.refs_0_), channel_id=1, source_target_pairs={{0,96},{32,0},{64,32},{96,64},{1,97},{33,1},{65,33},{97,65},{2,98}... | collective-permute-start | bytes 56 | tf_op jit(solution)/shard_map/ppermute | solution.py:528
  7.8 17.5 %shard_map.165 = (bf16[4,14,5,16,256]{4,3,2,1,0:T(8,128)(2,1)}, bf16[4,12,3,16,256]{4,3,2,1,0:T(8,128)(2,1)}, f32[4,128]{1,0:T(4,128)}, f32[32,4,128]{2,1,0:T(4,128)}, f32[65536,128]{1,0:T(8,128)}) custom-call(s32[1,4]{1,0:T(1,128)} %counts_hbm.3, s32[1,4]{1,0:T(1,128)} %ends_hbm.1, f32[1,4]{1,0:T(1,128)} %rewards_hbm.1, f32[1,4]{1,0:T(1,128)} %ratios_hbm.1, ...), custom_call_target="tpu_custom_call" | custom-call | flops 10569646080 | bytes 16000000 | tf_op jit(solution)/shard_map/pallas_call | solution.py:406
  25.3 8.6 %all-to-all-start = ((f32[32,4,128]{2,1,0:T(4,128)}), f32[32,4,128]{2,1,0:T(4,128)S(1)}, u32[]{:S(2)}, u32[]{:S(2)}) async-start(f32[32,4,128]{2,1,0:T(4,128)} %get-tuple-element.15), calls=%async_computation | async-start | bytes 131072 | tf_op jit(solution)/shard_map/all_to_all | solution.py:545
  33.9 5.2 %shard_map.166 = bf16[4,576,256]{2,1,0:T(8,128)(2,1)} custom-call(s32[1,4]{1,0:T(1,128)} %counts_hbm.3, bf16[4,14,5,16,256]{4,3,2,1,0:T(8,128)(2,1)} %get-tuple-element.11.middle_hbm, bf16[4,12,3,16,256]{4,3,2,1,0:T(8,128)(2,1)} %get-tuple-element.12.hidden_hbm, bf16[2,9,256,256]{3,2,1,0:T(8,128)(2,1)} %second_hbm.3), custom_call_target="tpu_custom_call" | custom-call | flops 2717908992 | bytes 8000000 | tf_op jit(solution)/shard_map/pallas_call | solution.py:448
  39.2 0.0 collective-permute-done.refs_1_
  39.2 0.0 collective-permute-done.1.refs_2_
  39.2 0.0 collective-permute-done.2.refs_3_
  39.2 2.0 %all-to-all-done.got_hbm = f32[32,4,128]{2,1,0:T(4,128)S(1)} async-done(((f32[32,4,128]{2,1,0:T(4,128)}), f32[32,4,128]{2,1,0:T(4,128)S(1)}, u32[]{:S(2)}, u32[]{:S(2)}) %all-to-all-start) | async-done | bytes 65568 | tf_op jit(solution)/shard_map/all_to_all | solution.py:545
  41.2 1.5 %shard_map.167 = (f32[4,128]{1,0:T(4,128)}, s32[1,1]{1,0:T(1,128)}) custom-call(f32[65536,128]{1,0:T(8,128)} %get-tuple-element.14.chain_hbm, f32[32,4,128]{2,1,0:T(4,128)S(1)} %all-to-all-done.got_hbm, s32[1,4]{1,0:T(1,128)S(1)} %multiply_add_fusion.refs_0_, s32[1,4]{1,0:T(1,128)S(1)} %collective-permute-done.refs_1_, ...), custom_call_target="tpu_custom_call" | custom-call | tf_op jit(solution)/shard_map/pallas_call | solution.py:547
Async XLA Ops:
  1.3 37.9 %collective-permute-start = (s32[1,4]{1,0:T(1,128)S(1)}, s32[1,4]{1,0:T(1,128)S(1)}, u32[]{:S(2)}, u32[]{:S(2)}) collective-permute-start(s32[1,4]{1,0:T(1,128)S(1)} %multiply_add_fusion.refs_0_), channel_id=1, source_target_pairs={{0,32},{32,64},{64,96},{96,0},{1,33},{33,65},{65,97},{97,1},{2,34}... | collective-permute-start | bytes 56 | tf_op jit(solution)/shard_map/ppermute | solution.py:528
  3.8 35.4 %collective-permute-start.1 = (s32[1,4]{1,0:T(1,128)S(1)}, s32[1,4]{1,0:T(1,128)S(1)}, u32[]{:S(2)}, u32[]{:S(2)}) collective-permute-start(s32[1,4]{1,0:T(1,128)S(1)} %multiply_add_fusion.refs_0_), channel_id=1, source_target_pairs={{0,64},{32,96},{64,0},{96,32},{1,65},{33,97},{65,1},{97,33},{2,66}... | collective-permute-start | bytes 56 | tf_op jit(solution)/shard_map/ppermute | solution.py:528
  7.1 32.1 %collective-permute-start.2 = (s32[1,4]{1,0:T(1,128)S(1)}, s32[1,4]{1,0:T(1,128)S(1)}, u32[]{:S(2)}, u32[]{:S(2)}) collective-permute-start(s32[1,4]{1,0:T(1,128)S(1)} %multiply_add_fusion.refs_0_), channel_id=1, source_target_pairs={{0,96},{32,0},{64,32},{96,64},{1,97},{33,1},{65,33},{97,65},{2,98}... | collective-permute-start | bytes 56 | tf_op jit(solution)/shard_map/ppermute | solution.py:528
  25.3 15.9 %all-to-all-start = ((f32[32,4,128]{2,1,0:T(4,128)}), f32[32,4,128]{2,1,0:T(4,128)S(1)}, u32[]{:S(2)}, u32[]{:S(2)}) async-start(f32[32,4,128]{2,1,0:T(4,128)} %get-tuple-element.15), calls=%async_computation | async-start | bytes 131072 | tf_op jit(solution)/shard_map/all_to_all | solution.py:545

commit v8 on v7

--- a/solution.py
+++ b/solution.py
@@ -524,7 +524,7 @@
     groups, shards = lax.axis_size("grp"), lax.axis_size("tm")
     codes = sample_counts * groups + dest_groups
     routed = [codes]
-    for far in range(1, groups):
+    for far in range(groups - 1, 0, -1):
         routed.append(lax.ppermute(codes, "grp", [(g, (g + far) % groups) for g in range(groups)]))
     middle, hidden, values, send, chain = front(
         sample_counts,

time: 43 us -> 41.8 us (0.972)
  starting transfers between devices: 15.1 us -> 13.9 us
    ppermute x3, starting transfers between devices: 6.5 us -> 5.29 us  [per_device(): lax.ppermute(codes, 'grp', [(g, (g + far) % groups) for g in range(groups)])]
  transfers between devices with their start and end apart: 4 -> 4, of which waited for: 1 -> 1; matrix products, arithmetic and copies ran while one was open for 0% -> 0% of each run, Pallas kernels for 53% -> 55%
where the time goes in v8:
time: 41.8 us; the launch traced here: 41.6 us
  Pallas kernels  24.3 us (58%)
  starting transfers between devices  13.9 us (33%)
  waiting for transfers between devices  2.05 us (5%)
  other arithmetic  0.68 us (2%)
  between operations  0.68 us (2%)
    pallas_call x1, Pallas kernels, front(): pl.pallas_call(functools.partial(front_kernel, side), out_shape=(jax.Shap...  17.5 us
    all_to_all x1, starting transfers between devices, per_device(): got = lax.all_to_all(send, 'tm', split_axis=0, concat_axis=0, tiled=True)  8.61 us
    ppermute x3, starting transfers between devices, per_device(): lax.ppermute(codes, 'grp', [(g, (g + far) % groups) for g in range(groups)])  5.29 us
    pallas_call x1, Pallas kernels, back(): pl.pallas_call(functools.partial(back_kernel, side), out_shape=jax.ShapeD...  5.24 us
    all_to_all x1, waiting for transfers between devices, per_device(): got = lax.all_to_all(send, 'tm', split_axis=0, concat_axis=0, tiled=True)  2.04 us
    pallas_call x1, Pallas kernels, per_device(): pl.pallas_call(functools.partial(target_kernel, steps, groups), out_shape...  1.53 us
  transfers between devices with their start and end apart: 4, of which 1 were waited for; matrix products, arithmetic and copies ran while one was open for 0% of the time, Pallas kernels for 55%

profile of v8, /device:TPU:1, one launch (start us, length us, event | category | flops | bytes accessed | tf_op | source)
XLA Modules:
  0.0 41.6 jit_solution(13123578533001287788)
XLA Ops:
  0.6 0.7 %multiply_add_fusion.refs_0_ = s32[1,4]{1,0:T(1,128)S(1)} fusion(s32[1,4]{1,0:T(1,128)} %param.16, s32[1,4]{1,0:T(1,128)} %counts_hbm.3), kind=kLoop, calls=%fused_computation | loop fusion | flops 8 | bytes 48 | tf_op jit(solution)/shard_map/add | solution.py:525
  1.3 4.6 %collective-permute-start = (s32[1,4]{1,0:T(1,128)S(1)}, s32[1,4]{1,0:T(1,128)S(1)}, u32[]{:S(2)}, u32[]{:S(2)}) collective-permute-start(s32[1,4]{1,0:T(1,128)S(1)} %multiply_add_fusion.refs_0_), channel_id=1, source_target_pairs={{0,96},{32,0},{64,32},{96,64},{1,97},{33,1},{65,33},{97,65},{2,98}... | collective-permute-start | bytes 56 | tf_op jit(solution)/shard_map/ppermute | solution.py:528
  5.9 0.0 collective-permute-start.1
  5.9 0.7 %collective-permute-start.2 = (s32[1,4]{1,0:T(1,128)S(1)}, s32[1,4]{1,0:T(1,128)S(1)}, u32[]{:S(2)}, u32[]{:S(2)}) collective-permute-start(s32[1,4]{1,0:T(1,128)S(1)} %multiply_add_fusion.refs_0_), channel_id=1, source_target_pairs={{0,32},{32,64},{64,96},{96,0},{1,33},{33,65},{65,97},{97,1},{2,34}... | collective-permute-start | bytes 56 | tf_op jit(solution)/shard_map/ppermute | solution.py:528
  6.6 17.5 %shard_map.165 = (bf16[4,14,5,16,256]{4,3,2,1,0:T(8,128)(2,1)}, bf16[4,12,3,16,256]{4,3,2,1,0:T(8,128)(2,1)}, f32[4,128]{1,0:T(4,128)}, f32[32,4,128]{2,1,0:T(4,128)}, f32[65536,128]{1,0:T(8,128)}) custom-call(s32[1,4]{1,0:T(1,128)} %counts_hbm.3, s32[1,4]{1,0:T(1,128)} %ends_hbm.1, f32[1,4]{1,0:T(1,128)} %rewards_hbm.1, f32[1,4]{1,0:T(1,128)} %ratios_hbm.1, ...), custom_call_target="tpu_custom_call" | custom-call | flops 10569646080 | bytes 16000000 | tf_op jit(solution)/shard_map/pallas_call | solution.py:406
  24.1 8.6 %all-to-all-start = ((f32[32,4,128]{2,1,0:T(4,128)}), f32[32,4,128]{2,1,0:T(4,128)S(1)}, u32[]{:S(2)}, u32[]{:S(2)}) async-start(f32[32,4,128]{2,1,0:T(4,128)} %get-tuple-element.15), calls=%async_computation | async-start | bytes 131072 | tf_op jit(solution)/shard_map/all_to_all | solution.py:545
  32.7 5.2 %shard_map.166 = bf16[4,576,256]{2,1,0:T(8,128)(2,1)} custom-call(s32[1,4]{1,0:T(1,128)} %counts_hbm.3, bf16[4,14,5,16,256]{4,3,2,1,0:T(8,128)(2,1)} %get-tuple-element.11.middle_hbm, bf16[4,12,3,16,256]{4,3,2,1,0:T(8,128)(2,1)} %get-tuple-element.12.hidden_hbm, bf16[2,9,256,256]{3,2,1,0:T(8,128)(2,1)} %second_hbm.3), custom_call_target="tpu_custom_call" | custom-call | flops 2717908992 | bytes 8000000 | tf_op jit(solution)/shard_map/pallas_call | solution.py:448
  38.0 0.0 collective-permute-done.refs_1_
  38.0 0.0 collective-permute-done.1.refs_2_
  38.0 0.0 collective-permute-done.2.refs_3_
  38.0 2.0 %all-to-all-done.got_hbm = f32[32,4,128]{2,1,0:T(4,128)S(1)} async-done(((f32[32,4,128]{2,1,0:T(4,128)}), f32[32,4,128]{2,1,0:T(4,128)S(1)}, u32[]{:S(2)}, u32[]{:S(2)}) %all-to-all-start) | async-done | bytes 65568 | tf_op jit(solution)/shard_map/all_to_all | solution.py:545
  40.0 1.5 %shard_map.167 = (f32[4,128]{1,0:T(4,128)}, s32[1,1]{1,0:T(1,128)}) custom-call(f32[65536,128]{1,0:T(8,128)} %get-tuple-element.14.chain_hbm, f32[32,4,128]{2,1,0:T(4,128)S(1)} %all-to-all-done.got_hbm, s32[1,4]{1,0:T(1,128)S(1)} %multiply_add_fusion.refs_0_, s32[1,4]{1,0:T(1,128)S(1)} %collective-permute-done.refs_1_, ...), custom_call_target="tpu_custom_call" | custom-call | tf_op jit(solution)/shard_map/pallas_call | solution.py:547
Async XLA Ops:
  1.3 36.7 %collective-permute-start = (s32[1,4]{1,0:T(1,128)S(1)}, s32[1,4]{1,0:T(1,128)S(1)}, u32[]{:S(2)}, u32[]{:S(2)}) collective-permute-start(s32[1,4]{1,0:T(1,128)S(1)} %multiply_add_fusion.refs_0_), channel_id=1, source_target_pairs={{0,96},{32,0},{64,32},{96,64},{1,97},{33,1},{65,33},{97,65},{2,98}... | collective-permute-start | bytes 56 | tf_op jit(solution)/shard_map/ppermute | solution.py:528
  5.9 32.1 %collective-permute-start.1 = (s32[1,4]{1,0:T(1,128)S(1)}, s32[1,4]{1,0:T(1,128)S(1)}, u32[]{:S(2)}, u32[]{:S(2)}) collective-permute-start(s32[1,4]{1,0:T(1,128)S(1)} %multiply_add_fusion.refs_0_), channel_id=1, source_target_pairs={{0,64},{32,96},{64,0},{96,32},{1,65},{33,97},{65,1},{97,33},{2,66}... | collective-permute-start | bytes 56 | tf_op jit(solution)/shard_map/ppermute | solution.py:528
  5.9 32.1 %collective-permute-start.2 = (s32[1,4]{1,0:T(1,128)S(1)}, s32[1,4]{1,0:T(1,128)S(1)}, u32[]{:S(2)}, u32[]{:S(2)}) collective-permute-start(s32[1,4]{1,0:T(1,128)S(1)} %multiply_add_fusion.refs_0_), channel_id=1, source_target_pairs={{0,32},{32,64},{64,96},{96,0},{1,33},{33,65},{65,97},{97,1},{2,34}... | collective-permute-start | bytes 56 | tf_op jit(solution)/shard_map/ppermute | solution.py:528
  24.1 15.9 %all-to-all-start = ((f32[32,4,128]{2,1,0:T(4,128)}), f32[32,4,128]{2,1,0:T(4,128)S(1)}, u32[]{:S(2)}, u32[]{:S(2)}) async-start(f32[32,4,128]{2,1,0:T(4,128)} %get-tuple-element.15), calls=%async_computation | async-start | bytes 131072 | tf_op jit(solution)/shard_map/all_to_all | solution.py:545

commit v9 on v8

--- a/solution.py
+++ b/solution.py
@@ -248,15 +248,19 @@
             return 0
 
         def second(b, _):
+            row = jnp.zeros((1, hidden.shape[-1]), F32)
             for y0 in range(0, half, CHUNK):
                 out = conv(mid, b, weights.at[1], mixed, y0, CHUNK)
                 now = hidden[b, y0 : y0 + CHUNK].astype(F32).reshape(out.shape) + out
                 now = now.astype(BF)
                 hidden[b, y0 : y0 + CHUNK] = now.reshape((CHUNK,) + hidden.shape[2:])
+                sum_here = jnp.sum(now.astype(F32).reshape(-1, LANE, now.shape[-1]), axis=0)
+                row = row + jnp.sum(sum_here, axis=0, keepdims=True)
                 put_padded(act, b, normed(now), y0, half)
+            kept[b, TAPS : TAPS + 1] = row
             return 0
 
-        lax.fori_loop(0, steps, first, 0)
+        lax.fori_loop(0, steps, first, 0, unroll=2)
 
         @pl.when(l == 0)
         def _():
@@ -274,9 +278,7 @@
 
     def total(b, _):
         block = mid[b, 1 : half + 1, 1 : mid.shape[2] - 1].reshape(side * side, width)
-        rows = hidden[b].reshape(side * side, width)
         sums[b] = jnp.dot(select, block, preferred_element_type=F32)
-        kept[b] = jnp.dot(select, rows, preferred_element_type=F32)
         return 0
 
     lax.fori_loop(0, steps, total, 0)

time: 41.8 us -> 41.8 us (level)
  no operation moved by 1% of the time
where the time goes in v9:
time: 41.8 us; the launch traced here: 41.6 us
  Pallas kernels  24.2 us (58%)
  starting transfers between devices  13.9 us (33%)
  waiting for transfers between devices  2.05 us (5%)
  other arithmetic  0.68 us (2%)
  between operations  0.68 us (2%)
    pallas_call x1, Pallas kernels, front(): pl.pallas_call(functools.partial(front_kernel, side), out_shape=(jax.Shap...  17.5 us
    all_to_all x1, starting transfers between devices, per_device(): got = lax.all_to_all(send, 'tm', split_axis=0, concat_axis=0, tiled=True)  8.63 us
    ppermute x3, starting transfers between devices, per_device(): lax.ppermute(codes, 'grp', [(g, (g + far) % groups) for g in range(groups)])  5.29 us
    pallas_call x1, Pallas kernels, back(): pl.pallas_call(functools.partial(back_kernel, side), out_shape=jax.ShapeD...  5.24 us
    all_to_all x1, waiting for transfers between devices, per_device(): got = lax.all_to_all(send, 'tm', split_axis=0, concat_axis=0, tiled=True)  2.04 us
    pallas_call x1, Pallas kernels, per_device(): pl.pallas_call(functools.partial(target_kernel, steps, groups), out_shape...  1.53 us
  transfers between devices with their start and end apart: 4, of which 1 were waited for; matrix products, arithmetic and copies ran while one was open for 0% of the time, Pallas kernels for 55%

profile of v9, /device:TPU:1, one launch (start us, length us, event | category | flops | bytes accessed | tf_op | source)
XLA Modules:
  0.0 41.6 jit_solution(11531694896742523287)
XLA Ops:
  0.6 0.7 %multiply_add_fusion.refs_0_ = s32[1,4]{1,0:T(1,128)S(1)} fusion(s32[1,4]{1,0:T(1,128)} %param.16, s32[1,4]{1,0:T(1,128)} %counts_hbm.3), kind=kLoop, calls=%fused_computation | loop fusion | flops 8 | bytes 48 | tf_op jit(solution)/shard_map/add | solution.py:527
  1.3 4.6 %collective-permute-start = (s32[1,4]{1,0:T(1,128)S(1)}, s32[1,4]{1,0:T(1,128)S(1)}, u32[]{:S(2)}, u32[]{:S(2)}) collective-permute-start(s32[1,4]{1,0:T(1,128)S(1)} %multiply_add_fusion.refs_0_), channel_id=1, source_target_pairs={{0,96},{32,0},{64,32},{96,64},{1,97},{33,1},{65,33},{97,65},{2,98}... | collective-permute-start | bytes 56 | tf_op jit(solution)/shard_map/ppermute | solution.py:530
  5.9 0.0 collective-permute-start.1
  5.9 0.7 %collective-permute-start.2 = (s32[1,4]{1,0:T(1,128)S(1)}, s32[1,4]{1,0:T(1,128)S(1)}, u32[]{:S(2)}, u32[]{:S(2)}) collective-permute-start(s32[1,4]{1,0:T(1,128)S(1)} %multiply_add_fusion.refs_0_), channel_id=1, source_target_pairs={{0,32},{32,64},{64,96},{96,0},{1,33},{33,65},{65,97},{97,1},{2,34}... | collective-permute-start | bytes 56 | tf_op jit(solution)/shard_map/ppermute | solution.py:530
  6.6 17.5 %shard_map.165 = (bf16[4,14,5,16,256]{4,3,2,1,0:T(8,128)(2,1)}, bf16[4,12,3,16,256]{4,3,2,1,0:T(8,128)(2,1)}, f32[4,128]{1,0:T(4,128)}, f32[32,4,128]{2,1,0:T(4,128)}, f32[65536,128]{1,0:T(8,128)}) custom-call(s32[1,4]{1,0:T(1,128)} %counts_hbm.3, s32[1,4]{1,0:T(1,128)} %ends_hbm.1, f32[1,4]{1,0:T(1,128)} %rewards_hbm.1, f32[1,4]{1,0:T(1,128)} %ratios_hbm.1, ...), custom_call_target="tpu_custom_call" | custom-call | flops 10569646080 | bytes 16000000 | tf_op jit(solution)/shard_map/pallas_call | solution.py:408
  24.1 8.6 %all-to-all-start = ((f32[32,4,128]{2,1,0:T(4,128)}), f32[32,4,128]{2,1,0:T(4,128)S(1)}, u32[]{:S(2)}, u32[]{:S(2)}) async-start(f32[32,4,128]{2,1,0:T(4,128)} %get-tuple-element.15), calls=%async_computation | async-start | bytes 131072 | tf_op jit(solution)/shard_map/all_to_all | solution.py:547
  32.7 5.2 %shard_map.166 = bf16[4,576,256]{2,1,0:T(8,128)(2,1)} custom-call(s32[1,4]{1,0:T(1,128)} %counts_hbm.3, bf16[4,14,5,16,256]{4,3,2,1,0:T(8,128)(2,1)} %get-tuple-element.11.middle_hbm, bf16[4,12,3,16,256]{4,3,2,1,0:T(8,128)(2,1)} %get-tuple-element.12.hidden_hbm, bf16[2,9,256,256]{3,2,1,0:T(8,128)(2,1)} %second_hbm.3), custom_call_target="tpu_custom_call" | custom-call | flops 2717908992 | bytes 8000000 | tf_op jit(solution)/shard_map/pallas_call | solution.py:450
  38.0 0.0 collective-permute-done.refs_1_
  38.0 0.0 collective-permute-done.1.refs_2_
  38.0 0.0 collective-permute-done.2.refs_3_
  38.0 2.0 %all-to-all-done.got_hbm = f32[32,4,128]{2,1,0:T(4,128)S(1)} async-done(((f32[32,4,128]{2,1,0:T(4,128)}), f32[32,4,128]{2,1,0:T(4,128)S(1)}, u32[]{:S(2)}, u32[]{:S(2)}) %all-to-all-start) | async-done | bytes 65568 | tf_op jit(solution)/shard_map/all_to_all | solution.py:547
  40.0 1.5 %shard_map.167 = (f32[4,128]{1,0:T(4,128)}, s32[1,1]{1,0:T(1,128)}) custom-call(f32[65536,128]{1,0:T(8,128)} %get-tuple-element.14.chain_hbm, f32[32,4,128]{2,1,0:T(4,128)S(1)} %all-to-all-done.got_hbm, s32[1,4]{1,0:T(1,128)S(1)} %multiply_add_fusion.refs_0_, s32[1,4]{1,0:T(1,128)S(1)} %collective-permute-done.refs_1_, ...), custom_call_target="tpu_custom_call" | custom-call | tf_op jit(solution)/shard_map/pallas_call | solution.py:549
Async XLA Ops:
  1.3 36.7 %collective-permute-start = (s32[1,4]{1,0:T(1,128)S(1)}, s32[1,4]{1,0:T(1,128)S(1)}, u32[]{:S(2)}, u32[]{:S(2)}) collective-permute-start(s32[1,4]{1,0:T(1,128)S(1)} %multiply_add_fusion.refs_0_), channel_id=1, source_target_pairs={{0,96},{32,0},{64,32},{96,64},{1,97},{33,1},{65,33},{97,65},{2,98}... | collective-permute-start | bytes 56 | tf_op jit(solution)/shard_map/ppermute | solution.py:530
  5.9 32.1 %collective-permute-start.1 = (s32[1,4]{1,0:T(1,128)S(1)}, s32[1,4]{1,0:T(1,128)S(1)}, u32[]{:S(2)}, u32[]{:S(2)}) collective-permute-start(s32[1,4]{1,0:T(1,128)S(1)} %multiply_add_fusion.refs_0_), channel_id=1, source_target_pairs={{0,64},{32,96},{64,0},{96,32},{1,65},{33,97},{65,1},{97,33},{2,66}... | collective-permute-start | bytes 56 | tf_op jit(solution)/shard_map/ppermute | solution.py:530
  5.9 32.1 %collective-permute-start.2 = (s32[1,4]{1,0:T(1,128)S(1)}, s32[1,4]{1,0:T(1,128)S(1)}, u32[]{:S(2)}, u32[]{:S(2)}) collective-permute-start(s32[1,4]{1,0:T(1,128)S(1)} %multiply_add_fusion.refs_0_), channel_id=1, source_target_pairs={{0,32},{32,64},{64,96},{96,0},{1,33},{33,65},{65,97},{97,1},{2,34}... | collective-permute-start | bytes 56 | tf_op jit(solution)/shard_map/ppermute | solution.py:530
  24.1 16.0 %all-to-all-start = ((f32[32,4,128]{2,1,0:T(4,128)}), f32[32,4,128]{2,1,0:T(4,128)S(1)}, u32[]{:S(2)}, u32[]{:S(2)}) async-start(f32[32,4,128]{2,1,0:T(4,128)} %get-tuple-element.15), calls=%async_computation | async-start | bytes 131072 | tf_op jit(solution)/shard_map/all_to_all | solution.py:547
